TPU v7x, 256 devices: a whole 4x4x8 slice. The times are simulated.
256 devices in a mesh: row: 8 (over x, core), col: 16 (over y_lo, z), layer: 2 (over y_hi).
Axes of the slice: x: 4, y: 4 (y_hi: 2, y_lo: 2; y = y_hi * 2 + y_lo), z: 8, core: 2. Of those that a mesh axis runs over, the one named last changes fastest.
Arguments:
- a_vals: bfloat16 [8, 16, 2, 24, 128, 128], P('row', 'col', 'layer'), may hold values from -1.1953125 to 1.1953125
- a_pos: int32 [8, 16, 2, 24], P('row', 'col', 'layer'), may hold values from 0 to 31, as said below
- a_count: int32 [8, 16, 2], P('row', 'col', 'layer'), may hold values from 6 to 24
- b_vals: bfloat16 [8, 16, 2, 2, 6, 128, 128], P('row', 'col', 'layer'), may hold values from -1.1953125 to 1.1953125
- b_pos: int32 [8, 16, 2, 2, 6], P('row', 'col', 'layer'), may hold values from 0 to 31, as said below
- b_count: int32 [8, 16, 2, 2], P('row', 'col', 'layer'), may hold values from 1 to 6
Outputs:
- product: float32 [8192, 16384], P('row', ('col', 'layer'))
Inputs may be any that keep to these rules, and one draw needn't show every extreme that they name: `a_pos`: within one panel (fixed first three indices) the 24 entries are distinct. `b_pos`: within one panel (fixed first four indices) the 6 entries are distinct.
All inputs are finite; a program needn't handle non-finite values.
Results may differ from a plain program's by a relative error of at most 0.0003.
Values may be sent and summed in bfloat16 or wider, within the bound.
No kernel may reach another device: no remote copies, remote signals or barrier semaphores. Data moves between devices by JAX's collectives and lax.ppermute only.
A program may use at most 64 MiB of HBM per device.

v0:
```python
import jax
import jax.numpy as jnp
from jax import lax
from jax.sharding import PartitionSpec as P

KB = 4
CB = 8
RB = 8


def passed_along(block, axis, distance):
    devices = range(lax.axis_size(axis))
    route = [((i - distance) % len(devices), i) for i in devices]
    return lax.ppermute(block, axis, route)


def contribute(total, a_vals, a_pos, a_count, b_vals, b_pos, b_count):
    block = a_vals.shape[-1]
    slots_a = a_vals.shape[0]
    target = a_pos % KB * RB + a_pos // KB
    live_a = jnp.arange(slots_a, dtype=jnp.int32) < a_count
    places = jnp.arange(KB * RB, dtype=jnp.int32)
    select = ((target[:, None] == places[None, :]) & live_a[:, None]).astype(jnp.bfloat16)
    placed = jnp.einsum("sp,sab->pab", select, a_vals, preferred_element_type=jnp.float32).astype(
        jnp.bfloat16
    )
    columns = placed.reshape(KB, RB * block, block)
    for slot in range(b_vals.shape[0]):
        entry = b_pos[slot]
        left = lax.dynamic_index_in_dim(columns, entry // CB, 0, keepdims=False)
        term = jnp.dot(left, b_vals[slot], preferred_element_type=jnp.float32)
        live = (slot < b_count).astype(jnp.float32)
        start = entry % CB * block
        old = lax.dynamic_slice_in_dim(total, start, block, 1)
        total = lax.dynamic_update_slice_in_dim(total, old + live * term, start, 1)
    return total


def pick(state, index):
    return tuple((lax.dynamic_index_in_dim(member, index, 0, keepdims=False) for member in state))


def per_device(a_vals, a_pos, a_count, b_vals, b_pos, b_count):
    n_row = lax.axis_size("row")
    n_col = lax.axis_size("col")
    row_i = lax.axis_index("row")
    col_j = lax.axis_index("col")
    block = a_vals.shape[-1]
    a_state = (a_vals[0, 0], a_pos[0, 0], a_count[0, 0])
    b_state = (b_vals[0, 0, 0], b_pos[0, 0, 0], b_count[0, 0, 0])

    def apply(total, a_now, b_now, turn):
        wanted = (row_i + col_j + turn) % n_col
        a_index = 0
        b_index = wanted // n_row
        a_part = pick(a_now, a_index)
        b_part = pick(b_now, b_index)
        return contribute(total, a_part[0], a_part[1], a_part[2], b_part[0], b_part[1], b_part[2])

    def advance(turn, carry):
        total, a_now, b_now = carry
        total = apply(total, a_now, b_now, turn)
        a_now = passed_along((a_now[0], a_now[1], a_now[2]), "col", -1)
        b_now = passed_along((b_now[0], b_now[1], b_now[2]), "row", -1)
        return (total, tuple(a_now), tuple(b_now))

    start = jnp.zeros((RB * block, CB * block), jnp.float32)
    total, a_now, b_now = lax.fori_loop(
        0, n_col - 1, advance, (start, tuple(a_state), tuple(b_state))
    )
    total = apply(total, a_now, b_now, n_col - 1)
    return lax.psum_scatter(total, "layer", scatter_dimension=1, tiled=True)


def solution(mesh):
    placed = (
        P("row", "col", "layer", None, None, None),
        P("row", "col", "layer", None),
        P("row", "col", "layer"),
        P("row", "col", "layer", None, None, None, None),
        P("row", "col", "layer", None, None),
        P("row", "col", "layer", None),
    )
    return jax.shard_map(
        per_device,
        mesh=mesh,
        in_specs=placed,
        out_specs=P("row", ("col", "layer")),
        check_vma=False,
    )
```

profile of v0, /device:TPU:8, one launch (start us, length us, event | category | flops | bytes accessed | tf_op | source)
XLA Modules:
  0.0 1008.9 jit_solution(678499090832563157)
XLA Ops:
  8.4 2.5 copy.12
  11.6 2.5 broadcast_in_dim.15
  14.1 886.8 %while.28 = (s32[]{:T(128)}, f32[1024,1024]{1,0:T(8,128)}, bf16[1,24,128,128]{3,1,2,0:T(8,128)(2,1)}, s32[1,24]{1,0:T(1,128)S(1)}, s32[1]{0:T(128)}, /*index=5*/...) while((s32[]{:T(128)}, f32[1024,1024]{1,0:T(8,128)}, ...), condition=%wide.region_1.2_spmd, body=%wide.region_0.1_spmd.sunk | while | flops 228591680 | bytes 19078096 | solution.py:68
  15.2 5.7 collective-permute-start
  22.0 15.8 %collective-permute-start.2 = (s32[1]{0:T(128)}, s32[1]{0:T(128)}, u32[]{:S(2)}, u32[]{:S(2)}) collective-permute-start(s32[1]{0:T(128)} %copy.33), channel_id=1, source_target_pairs={{2,0},{4,2},{6,4},{8,6},{10,8},{12,10},{14,12},{16,14},{18,16},{20... | collective-permute-start | bytes 20 | tf_op jit(solution)/shard_map/while/body/eval_jaxpr/ppermute | solution.py:14
  81.4 16.7 %collective-permute-start.2 = (s32[1]{0:T(128)}, s32[1]{0:T(128)}, u32[]{:S(2)}, u32[]{:S(2)}) collective-permute-start(s32[1]{0:T(128)} %copy.33), channel_id=1, source_target_pairs={{2,0},{4,2},{6,4},{8,6},{10,8},{12,10},{14,12},{16,14},{18,16},{20... | collective-permute-start | bytes 20 | tf_op jit(solution)/shard_map/while/body/eval_jaxpr/ppermute | solution.py:14
  140.2 16.7 %collective-permute-start.2 = (s32[1]{0:T(128)}, s32[1]{0:T(128)}, u32[]{:S(2)}, u32[]{:S(2)}) collective-permute-start(s32[1]{0:T(128)} %copy.33), channel_id=1, source_target_pairs={{2,0},{4,2},{6,4},{8,6},{10,8},{12,10},{14,12},{16,14},{18,16},{20... | collective-permute-start | bytes 20 | tf_op jit(solution)/shard_map/while/body/eval_jaxpr/ppermute | solution.py:14
  197.4 16.2 %collective-permute-start.2 = (s32[1]{0:T(128)}, s32[1]{0:T(128)}, u32[]{:S(2)}, u32[]{:S(2)}) collective-permute-start(s32[1]{0:T(128)} %copy.33), channel_id=1, source_target_pairs={{2,0},{4,2},{6,4},{8,6},{10,8},{12,10},{14,12},{16,14},{18,16},{20... | collective-permute-start | bytes 20 | tf_op jit(solution)/shard_map/while/body/eval_jaxpr/ppermute | solution.py:14
  214.6 2.4 collective-permute-start.3
  258.3 15.8 %collective-permute-start.2 = (s32[1]{0:T(128)}, s32[1]{0:T(128)}, u32[]{:S(2)}, u32[]{:S(2)}) collective-permute-start(s32[1]{0:T(128)} %copy.33), channel_id=1, source_target_pairs={{2,0},{4,2},{6,4},{8,6},{10,8},{12,10},{14,12},{16,14},{18,16},{20... | collective-permute-start | bytes 20 | tf_op jit(solution)/shard_map/while/body/eval_jaxpr/ppermute | solution.py:14
  275.1 2.2 collective-permute-start.3
  315.5 16.6 %collective-permute-start.2 = (s32[1]{0:T(128)}, s32[1]{0:T(128)}, u32[]{:S(2)}, u32[]{:S(2)}) collective-permute-start(s32[1]{0:T(128)} %copy.33), channel_id=1, source_target_pairs={{2,0},{4,2},{6,4},{8,6},{10,8},{12,10},{14,12},{16,14},{18,16},{20... | collective-permute-start | bytes 20 | tf_op jit(solution)/shard_map/while/body/eval_jaxpr/ppermute | solution.py:14
  373.8 17.2 %collective-permute-start.2 = (s32[1]{0:T(128)}, s32[1]{0:T(128)}, u32[]{:S(2)}, u32[]{:S(2)}) collective-permute-start(s32[1]{0:T(128)} %copy.33), channel_id=1, source_target_pairs={{2,0},{4,2},{6,4},{8,6},{10,8},{12,10},{14,12},{16,14},{18,16},{20... | collective-permute-start | bytes 20 | tf_op jit(solution)/shard_map/while/body/eval_jaxpr/ppermute | solution.py:14
  430.1 6.5 collective-permute-start.1
  436.6 10.0 collective-permute-start.2
  466.1 2.1 fusion.105
  491.2 6.3 collective-permute-start
  498.3 15.2 %collective-permute-start.2 = (s32[1]{0:T(128)}, s32[1]{0:T(128)}, u32[]{:S(2)}, u32[]{:S(2)}) collective-permute-start(s32[1]{0:T(128)} %copy.33), channel_id=1, source_target_pairs={{2,0},{4,2},{6,4},{8,6},{10,8},{12,10},{14,12},{16,14},{18,16},{20... | collective-permute-start | bytes 20 | tf_op jit(solution)/shard_map/while/body/eval_jaxpr/ppermute | solution.py:14
  556.7 15.0 %collective-permute-start.2 = (s32[1]{0:T(128)}, s32[1]{0:T(128)}, u32[]{:S(2)}, u32[]{:S(2)}) collective-permute-start(s32[1]{0:T(128)} %copy.33), channel_id=1, source_target_pairs={{2,0},{4,2},{6,4},{8,6},{10,8},{12,10},{14,12},{16,14},{18,16},{20... | collective-permute-start | bytes 20 | tf_op jit(solution)/shard_map/while/body/eval_jaxpr/ppermute | solution.py:14
  612.1 2.5 collective-permute-start
  614.7 17.4 %collective-permute-start.2 = (s32[1]{0:T(128)}, s32[1]{0:T(128)}, u32[]{:S(2)}, u32[]{:S(2)}) collective-permute-start(s32[1]{0:T(128)} %copy.33), channel_id=1, source_target_pairs={{2,0},{4,2},{6,4},{8,6},{10,8},{12,10},{14,12},{16,14},{18,16},{20... | collective-permute-start | bytes 20 | tf_op jit(solution)/shard_map/while/body/eval_jaxpr/ppermute | solution.py:14
  671.1 16.5 %collective-permute-start.2 = (s32[1]{0:T(128)}, s32[1]{0:T(128)}, u32[]{:S(2)}, u32[]{:S(2)}) collective-permute-start(s32[1]{0:T(128)} %copy.33), channel_id=1, source_target_pairs={{2,0},{4,2},{6,4},{8,6},{10,8},{12,10},{14,12},{16,14},{18,16},{20... | collective-permute-start | bytes 20 | tf_op jit(solution)/shard_map/while/body/eval_jaxpr/ppermute | solution.py:14
  690.3 2.5 collective-permute-start.4
  732.4 15.4 %collective-permute-start.2 = (s32[1]{0:T(128)}, s32[1]{0:T(128)}, u32[]{:S(2)}, u32[]{:S(2)}) collective-permute-start(s32[1]{0:T(128)} %copy.33), channel_id=1, source_target_pairs={{2,0},{4,2},{6,4},{8,6},{10,8},{12,10},{14,12},{16,14},{18,16},{20... | collective-permute-start | bytes 20 | tf_op jit(solution)/shard_map/while/body/eval_jaxpr/ppermute | solution.py:14
  748.8 2.3 collective-permute-start.3
  765.5 2.1 fusion.105
  788.8 16.5 %collective-permute-start.2 = (s32[1]{0:T(128)}, s32[1]{0:T(128)}, u32[]{:S(2)}, u32[]{:S(2)}) collective-permute-start(s32[1]{0:T(128)} %copy.33), channel_id=1, source_target_pairs={{2,0},{4,2},{6,4},{8,6},{10,8},{12,10},{14,12},{16,14},{18,16},{20... | collective-permute-start | bytes 20 | tf_op jit(solution)/shard_map/while/body/eval_jaxpr/ppermute | solution.py:14
  820.4 2.2 fusion.104
  845.7 16.5 %collective-permute-start.2 = (s32[1]{0:T(128)}, s32[1]{0:T(128)}, u32[]{:S(2)}, u32[]{:S(2)}) collective-permute-start(s32[1]{0:T(128)} %copy.33), channel_id=1, source_target_pairs={{2,0},{4,2},{6,4},{8,6},{10,8},{12,10},{14,12},{16,14},{18,16},{20... | collective-permute-start | bytes 20 | tf_op jit(solution)/shard_map/while/body/eval_jaxpr/ppermute | solution.py:14
  923.6 2.2 fusion.39
  932.1 2.2 fusion.47
  936.3 65.8 %reduce-scatter.2.cloned.1.call-done = f32[1024,512]{1,0:T(8,128)} async-done(((f32[1024,1024]{1,0:T(8,128)}), f32[1024,512]{1,0:T(8,128)}) %reduce-scatter.2.cloned.1.call-update) | async-done | bytes 2097168 | tf_op jit(solution)/shard_map/reduce_scatter | solution.py:72
  (444 shorter events, 321.2 us)
Async XLA Ops:
  6.5 995.6 %reduce-scatter.2.cloned.1.call-start = ((), (), s32[]{:S(2)}) async-start(), calls=%async_computation.1 | async-start | bytes 6291456 | tf_op jit(solution)/shard_map/reduce_scatter | solution.py:72
  15.2 62.4 %collective-permute-start = (bf16[1,24,128,128]{3,1,2,0:T(8,128)(2,1)S(1)}, bf16[1,24,128,128]{3,1,2,0:T(8,128)(2,1)}, u32[]{:S(2)}, u32[]{:S(2)}) collective-permute-start(bf16[1,24,128,128]{3,1,2,0:T(8,128)(2,1)S(1)} %copy.31), channel_id=1, source_target_pairs={{2,0},{4,2},{6,4},{8,6},{10,8},{12,10},{14,12},{16,14},{18,16},{20... | collective-permute-start | bytes 2359304 | tf_op jit(solution)/shard_map/while/body/eval_jaxpr/ppermute | solution.py:14
  20.9 56.6 %collective-permute-start.1 = (s32[1,24]{1,0:T(1,128)S(1)}, s32[1,24]{1,0:T(1,128)S(1)}, u32[]{:S(2)}, u32[]{:S(2)}) collective-permute-start(s32[1,24]{1,0:T(1,128)S(1)} %copy.32), channel_id=1, source_target_pairs={{2,0},{4,2},{6,4},{8,6},{10,8},{12,10},{14,12},{16,14},{18,16},{20... | collective-permute-start | bytes 296 | tf_op jit(solution)/shard_map/while/body/eval_jaxpr/ppermute | solution.py:14
  79.4 57.1 %collective-permute-start = (bf16[1,24,128,128]{3,1,2,0:T(8,128)(2,1)S(1)}, bf16[1,24,128,128]{3,1,2,0:T(8,128)(2,1)}, u32[]{:S(2)}, u32[]{:S(2)}) collective-permute-start(bf16[1,24,128,128]{3,1,2,0:T(8,128)(2,1)S(1)} %copy.31), channel_id=1, source_target_pairs={{2,0},{4,2},{6,4},{8,6},{10,8},{12,10},{14,12},{16,14},{18,16},{20... | collective-permute-start | bytes 2359304 | tf_op jit(solution)/shard_map/while/body/eval_jaxpr/ppermute | solution.py:14
  80.4 56.0 %collective-permute-start.1 = (s32[1,24]{1,0:T(1,128)S(1)}, s32[1,24]{1,0:T(1,128)S(1)}, u32[]{:S(2)}, u32[]{:S(2)}) collective-permute-start(s32[1,24]{1,0:T(1,128)S(1)} %copy.32), channel_id=1, source_target_pairs={{2,0},{4,2},{6,4},{8,6},{10,8},{12,10},{14,12},{16,14},{18,16},{20... | collective-permute-start | bytes 296 | tf_op jit(solution)/shard_map/while/body/eval_jaxpr/ppermute | solution.py:14
  138.2 56.1 %collective-permute-start = (bf16[1,24,128,128]{3,1,2,0:T(8,128)(2,1)S(1)}, bf16[1,24,128,128]{3,1,2,0:T(8,128)(2,1)}, u32[]{:S(2)}, u32[]{:S(2)}) collective-permute-start(bf16[1,24,128,128]{3,1,2,0:T(8,128)(2,1)S(1)} %copy.31), channel_id=1, source_target_pairs={{2,0},{4,2},{6,4},{8,6},{10,8},{12,10},{14,12},{16,14},{18,16},{20... | collective-permute-start | bytes 2359304 | tf_op jit(solution)/shard_map/while/body/eval_jaxpr/ppermute | solution.py:14
  139.3 55.0 %collective-permute-start.1 = (s32[1,24]{1,0:T(1,128)S(1)}, s32[1,24]{1,0:T(1,128)S(1)}, u32[]{:S(2)}, u32[]{:S(2)}) collective-permute-start(s32[1,24]{1,0:T(1,128)S(1)} %copy.32), channel_id=1, source_target_pairs={{2,0},{4,2},{6,4},{8,6},{10,8},{12,10},{14,12},{16,14},{18,16},{20... | collective-permute-start | bytes 296 | tf_op jit(solution)/shard_map/while/body/eval_jaxpr/ppermute | solution.py:14
  196.1 59.3 %collective-permute-start = (bf16[1,24,128,128]{3,1,2,0:T(8,128)(2,1)S(1)}, bf16[1,24,128,128]{3,1,2,0:T(8,128)(2,1)}, u32[]{:S(2)}, u32[]{:S(2)}) collective-permute-start(bf16[1,24,128,128]{3,1,2,0:T(8,128)(2,1)S(1)} %copy.31), channel_id=1, source_target_pairs={{2,0},{4,2},{6,4},{8,6},{10,8},{12,10},{14,12},{16,14},{18,16},{20... | collective-permute-start | bytes 2359304 | tf_op jit(solution)/shard_map/while/body/eval_jaxpr/ppermute | solution.py:14
  196.8 58.6 %collective-permute-start.1 = (s32[1,24]{1,0:T(1,128)S(1)}, s32[1,24]{1,0:T(1,128)S(1)}, u32[]{:S(2)}, u32[]{:S(2)}) collective-permute-start(s32[1,24]{1,0:T(1,128)S(1)} %copy.32), channel_id=1, source_target_pairs={{2,0},{4,2},{6,4},{8,6},{10,8},{12,10},{14,12},{16,14},{18,16},{20... | collective-permute-start | bytes 296 | tf_op jit(solution)/shard_map/while/body/eval_jaxpr/ppermute | solution.py:14
  197.4 55.4 %collective-permute-start.2 = (s32[1]{0:T(128)}, s32[1]{0:T(128)}, u32[]{:S(2)}, u32[]{:S(2)}) collective-permute-start(s32[1]{0:T(128)} %copy.33), channel_id=1, source_target_pairs={{2,0},{4,2},{6,4},{8,6},{10,8},{12,10},{14,12},{16,14},{18,16},{20... | collective-permute-start | bytes 20 | tf_op jit(solution)/shard_map/while/body/eval_jaxpr/ppermute | solution.py:14
  257.2 56.0 %collective-permute-start = (bf16[1,24,128,128]{3,1,2,0:T(8,128)(2,1)S(1)}, bf16[1,24,128,128]{3,1,2,0:T(8,128)(2,1)}, u32[]{:S(2)}, u32[]{:S(2)}) collective-permute-start(bf16[1,24,128,128]{3,1,2,0:T(8,128)(2,1)S(1)} %copy.31), channel_id=1, source_target_pairs={{2,0},{4,2},{6,4},{8,6},{10,8},{12,10},{14,12},{16,14},{18,16},{20... | collective-permute-start | bytes 2359304 | tf_op jit(solution)/shard_map/while/body/eval_jaxpr/ppermute | solution.py:14
  258.2 55.0 %collective-permute-start.1 = (s32[1,24]{1,0:T(1,128)S(1)}, s32[1,24]{1,0:T(1,128)S(1)}, u32[]{:S(2)}, u32[]{:S(2)}) collective-permute-start(s32[1,24]{1,0:T(1,128)S(1)} %copy.32), channel_id=1, source_target_pairs={{2,0},{4,2},{6,4},{8,6},{10,8},{12,10},{14,12},{16,14},{18,16},{20... | collective-permute-start | bytes 296 | tf_op jit(solution)/shard_map/while/body/eval_jaxpr/ppermute | solution.py:14
  315.0 56.5 %collective-permute-start = (bf16[1,24,128,128]{3,1,2,0:T(8,128)(2,1)S(1)}, bf16[1,24,128,128]{3,1,2,0:T(8,128)(2,1)}, u32[]{:S(2)}, u32[]{:S(2)}) collective-permute-start(bf16[1,24,128,128]{3,1,2,0:T(8,128)(2,1)S(1)} %copy.31), channel_id=1, source_target_pairs={{2,0},{4,2},{6,4},{8,6},{10,8},{12,10},{14,12},{16,14},{18,16},{20... | collective-permute-start | bytes 2359304 | tf_op jit(solution)/shard_map/while/body/eval_jaxpr/ppermute | solution.py:14
  315.4 56.1 %collective-permute-start.1 = (s32[1,24]{1,0:T(1,128)S(1)}, s32[1,24]{1,0:T(1,128)S(1)}, u32[]{:S(2)}, u32[]{:S(2)}) collective-permute-start(s32[1,24]{1,0:T(1,128)S(1)} %copy.32), channel_id=1, source_target_pairs={{2,0},{4,2},{6,4},{8,6},{10,8},{12,10},{14,12},{16,14},{18,16},{20... | collective-permute-start | bytes 296 | tf_op jit(solution)/shard_map/while/body/eval_jaxpr/ppermute | solution.py:14
  373.3 54.8 %collective-permute-start = (bf16[1,24,128,128]{3,1,2,0:T(8,128)(2,1)S(1)}, bf16[1,24,128,128]{3,1,2,0:T(8,128)(2,1)}, u32[]{:S(2)}, u32[]{:S(2)}) collective-permute-start(bf16[1,24,128,128]{3,1,2,0:T(8,128)(2,1)S(1)} %copy.31), channel_id=1, source_target_pairs={{2,0},{4,2},{6,4},{8,6},{10,8},{12,10},{14,12},{16,14},{18,16},{20... | collective-permute-start | bytes 2359304 | tf_op jit(solution)/shard_map/while/body/eval_jaxpr/ppermute | solution.py:14
  373.6 54.6 %collective-permute-start.1 = (s32[1,24]{1,0:T(1,128)S(1)}, s32[1,24]{1,0:T(1,128)S(1)}, u32[]{:S(2)}, u32[]{:S(2)}) collective-permute-start(s32[1,24]{1,0:T(1,128)S(1)} %copy.32), channel_id=1, source_target_pairs={{2,0},{4,2},{6,4},{8,6},{10,8},{12,10},{14,12},{16,14},{18,16},{20... | collective-permute-start | bytes 296 | tf_op jit(solution)/shard_map/while/body/eval_jaxpr/ppermute | solution.py:14
  430.0 59.5 %collective-permute-start = (bf16[1,24,128,128]{3,1,2,0:T(8,128)(2,1)S(1)}, bf16[1,24,128,128]{3,1,2,0:T(8,128)(2,1)}, u32[]{:S(2)}, u32[]{:S(2)}) collective-permute-start(bf16[1,24,128,128]{3,1,2,0:T(8,128)(2,1)S(1)} %copy.31), channel_id=1, source_target_pairs={{2,0},{4,2},{6,4},{8,6},{10,8},{12,10},{14,12},{16,14},{18,16},{20... | collective-permute-start | bytes 2359304 | tf_op jit(solution)/shard_map/while/body/eval_jaxpr/ppermute | solution.py:14
  430.1 59.4 %collective-permute-start.1 = (s32[1,24]{1,0:T(1,128)S(1)}, s32[1,24]{1,0:T(1,128)S(1)}, u32[]{:S(2)}, u32[]{:S(2)}) collective-permute-start(s32[1,24]{1,0:T(1,128)S(1)} %copy.32), channel_id=1, source_target_pairs={{2,0},{4,2},{6,4},{8,6},{10,8},{12,10},{14,12},{16,14},{18,16},{20... | collective-permute-start | bytes 296 | tf_op jit(solution)/shard_map/while/body/eval_jaxpr/ppermute | solution.py:14
  491.2 61.4 %collective-permute-start = (bf16[1,24,128,128]{3,1,2,0:T(8,128)(2,1)S(1)}, bf16[1,24,128,128]{3,1,2,0:T(8,128)(2,1)}, u32[]{:S(2)}, u32[]{:S(2)}) collective-permute-start(bf16[1,24,128,128]{3,1,2,0:T(8,128)(2,1)S(1)} %copy.31), channel_id=1, source_target_pairs={{2,0},{4,2},{6,4},{8,6},{10,8},{12,10},{14,12},{16,14},{18,16},{20... | collective-permute-start | bytes 2359304 | tf_op jit(solution)/shard_map/while/body/eval_jaxpr/ppermute | solution.py:14
  497.6 55.0 %collective-permute-start.1 = (s32[1,24]{1,0:T(1,128)S(1)}, s32[1,24]{1,0:T(1,128)S(1)}, u32[]{:S(2)}, u32[]{:S(2)}) collective-permute-start(s32[1,24]{1,0:T(1,128)S(1)} %copy.32), channel_id=1, source_target_pairs={{2,0},{4,2},{6,4},{8,6},{10,8},{12,10},{14,12},{16,14},{18,16},{20... | collective-permute-start | bytes 296 | tf_op jit(solution)/shard_map/while/body/eval_jaxpr/ppermute | solution.py:14
  554.4 56.0 %collective-permute-start = (bf16[1,24,128,128]{3,1,2,0:T(8,128)(2,1)S(1)}, bf16[1,24,128,128]{3,1,2,0:T(8,128)(2,1)}, u32[]{:S(2)}, u32[]{:S(2)}) collective-permute-start(bf16[1,24,128,128]{3,1,2,0:T(8,128)(2,1)S(1)} %copy.31), channel_id=1, source_target_pairs={{2,0},{4,2},{6,4},{8,6},{10,8},{12,10},{14,12},{16,14},{18,16},{20... | collective-permute-start | bytes 2359304 | tf_op jit(solution)/shard_map/while/body/eval_jaxpr/ppermute | solution.py:14
  554.8 55.6 %collective-permute-start.1 = (s32[1,24]{1,0:T(1,128)S(1)}, s32[1,24]{1,0:T(1,128)S(1)}, u32[]{:S(2)}, u32[]{:S(2)}) collective-permute-start(s32[1,24]{1,0:T(1,128)S(1)} %copy.32), channel_id=1, source_target_pairs={{2,0},{4,2},{6,4},{8,6},{10,8},{12,10},{14,12},{16,14},{18,16},{20... | collective-permute-start | bytes 296 | tf_op jit(solution)/shard_map/while/body/eval_jaxpr/ppermute | solution.py:14
  612.1 57.1 %collective-permute-start = (bf16[1,24,128,128]{3,1,2,0:T(8,128)(2,1)S(1)}, bf16[1,24,128,128]{3,1,2,0:T(8,128)(2,1)}, u32[]{:S(2)}, u32[]{:S(2)}) collective-permute-start(bf16[1,24,128,128]{3,1,2,0:T(8,128)(2,1)S(1)} %copy.31), channel_id=1, source_target_pairs={{2,0},{4,2},{6,4},{8,6},{10,8},{12,10},{14,12},{16,14},{18,16},{20... | collective-permute-start | bytes 2359304 | tf_op jit(solution)/shard_map/while/body/eval_jaxpr/ppermute | solution.py:14
  614.7 54.6 %collective-permute-start.1 = (s32[1,24]{1,0:T(1,128)S(1)}, s32[1,24]{1,0:T(1,128)S(1)}, u32[]{:S(2)}, u32[]{:S(2)}) collective-permute-start(s32[1,24]{1,0:T(1,128)S(1)} %copy.32), channel_id=1, source_target_pairs={{2,0},{4,2},{6,4},{8,6},{10,8},{12,10},{14,12},{16,14},{18,16},{20... | collective-permute-start | bytes 296 | tf_op jit(solution)/shard_map/while/body/eval_jaxpr/ppermute | solution.py:14
  671.1 59.5 %collective-permute-start = (bf16[1,24,128,128]{3,1,2,0:T(8,128)(2,1)S(1)}, bf16[1,24,128,128]{3,1,2,0:T(8,128)(2,1)}, u32[]{:S(2)}, u32[]{:S(2)}) collective-permute-start(bf16[1,24,128,128]{3,1,2,0:T(8,128)(2,1)S(1)} %copy.31), channel_id=1, source_target_pairs={{2,0},{4,2},{6,4},{8,6},{10,8},{12,10},{14,12},{16,14},{18,16},{20... | collective-permute-start | bytes 2359304 | tf_op jit(solution)/shard_map/while/body/eval_jaxpr/ppermute | solution.py:14
  671.1 59.5 %collective-permute-start.1 = (s32[1,24]{1,0:T(1,128)S(1)}, s32[1,24]{1,0:T(1,128)S(1)}, u32[]{:S(2)}, u32[]{:S(2)}) collective-permute-start(s32[1,24]{1,0:T(1,128)S(1)} %copy.32), channel_id=1, source_target_pairs={{2,0},{4,2},{6,4},{8,6},{10,8},{12,10},{14,12},{16,14},{18,16},{20... | collective-permute-start | bytes 296 | tf_op jit(solution)/shard_map/while/body/eval_jaxpr/ppermute | solution.py:14
  671.1 56.2 %collective-permute-start.2 = (s32[1]{0:T(128)}, s32[1]{0:T(128)}, u32[]{:S(2)}, u32[]{:S(2)}) collective-permute-start(s32[1]{0:T(128)} %copy.33), channel_id=1, source_target_pairs={{2,0},{4,2},{6,4},{8,6},{10,8},{12,10},{14,12},{16,14},{18,16},{20... | collective-permute-start | bytes 20 | tf_op jit(solution)/shard_map/while/body/eval_jaxpr/ppermute | solution.py:14
  732.4 54.6 %collective-permute-start = (bf16[1,24,128,128]{3,1,2,0:T(8,128)(2,1)S(1)}, bf16[1,24,128,128]{3,1,2,0:T(8,128)(2,1)}, u32[]{:S(2)}, u32[]{:S(2)}) collective-permute-start(bf16[1,24,128,128]{3,1,2,0:T(8,128)(2,1)S(1)} %copy.31), channel_id=1, source_target_pairs={{2,0},{4,2},{6,4},{8,6},{10,8},{12,10},{14,12},{16,14},{18,16},{20... | collective-permute-start | bytes 2359304 | tf_op jit(solution)/shard_map/while/body/eval_jaxpr/ppermute | solution.py:14
  732.4 54.6 %collective-permute-start.1 = (s32[1,24]{1,0:T(1,128)S(1)}, s32[1,24]{1,0:T(1,128)S(1)}, u32[]{:S(2)}, u32[]{:S(2)}) collective-permute-start(s32[1,24]{1,0:T(1,128)S(1)} %copy.32), channel_id=1, source_target_pairs={{2,0},{4,2},{6,4},{8,6},{10,8},{12,10},{14,12},{16,14},{18,16},{20... | collective-permute-start | bytes 296 | tf_op jit(solution)/shard_map/while/body/eval_jaxpr/ppermute | solution.py:14
  788.7 55.2 %collective-permute-start = (bf16[1,24,128,128]{3,1,2,0:T(8,128)(2,1)S(1)}, bf16[1,24,128,128]{3,1,2,0:T(8,128)(2,1)}, u32[]{:S(2)}, u32[]{:S(2)}) collective-permute-start(bf16[1,24,128,128]{3,1,2,0:T(8,128)(2,1)S(1)} %copy.31), channel_id=1, source_target_pairs={{2,0},{4,2},{6,4},{8,6},{10,8},{12,10},{14,12},{16,14},{18,16},{20... | collective-permute-start | bytes 2359304 | tf_op jit(solution)/shard_map/while/body/eval_jaxpr/ppermute | solution.py:14
  788.8 55.1 %collective-permute-start.1 = (s32[1,24]{1,0:T(1,128)S(1)}, s32[1,24]{1,0:T(1,128)S(1)}, u32[]{:S(2)}, u32[]{:S(2)}) collective-permute-start(s32[1,24]{1,0:T(1,128)S(1)} %copy.32), channel_id=1, source_target_pairs={{2,0},{4,2},{6,4},{8,6},{10,8},{12,10},{14,12},{16,14},{18,16},{20... | collective-permute-start | bytes 296 | tf_op jit(solution)/shard_map/while/body/eval_jaxpr/ppermute | solution.py:14
  845.7 54.5 %collective-permute-start = (bf16[1,24,128,128]{3,1,2,0:T(8,128)(2,1)S(1)}, bf16[1,24,128,128]{3,1,2,0:T(8,128)(2,1)}, u32[]{:S(2)}, u32[]{:S(2)}) collective-permute-start(bf16[1,24,128,128]{3,1,2,0:T(8,128)(2,1)S(1)} %copy.31), channel_id=1, source_target_pairs={{2,0},{4,2},{6,4},{8,6},{10,8},{12,10},{14,12},{16,14},{18,16},{20... | collective-permute-start | bytes 2359304 | tf_op jit(solution)/shard_map/while/body/eval_jaxpr/ppermute | solution.py:14
  (62 other events, 1920.0 us)
Sparse Core Ops, SparseCore 0:
  936.5 65.5 reduce-scatter.1
where the time goes:
time: 1020 us; the launch traced here: 1010 us
  starting transfers between devices  307 us (30%)
  loops' own time  305 us (30%)
  matrix products  211 us (21%)
  waiting for transfers between devices  85.4 us (8%)
  local copies, waits for them, and re-layouts  66.9 us (7%)
  between operations  33.3 us (3%)
    ppermute x90, starting transfers between devices, passed_along(): return lax.ppermute(block, axis, route)  307 us
    another operation x1, loops' own time, per_device(): lax.fori_loop(0, n_col - 1, advance, (start, tuple(a_state), tuple(b_stat...  305 us
    dot_general x96, matrix products, contribute(): term = jnp.dot(left, b_vals[slot], preferred_element_type=jnp.float32)  201 us
    reduce_scatter x1, waiting for transfers between devices, per_device(): return lax.psum_scatter(total, 'layer', scatter_dimension=1, tiled=True)  65.8 us
    another operation x75, local copies, waits for them, and re-layouts  32 us
  transfers between devices with their start and end apart: 91, of which 16 were waited for; matrix products, arithmetic and copies ran while one was open for 24% of the time, Pallas kernels for 0%

commit v1 on v0

v1 whole, which is shorter than its diff:
```python
import functools

import jax
import jax.numpy as jnp
from jax import lax
from jax.experimental import pallas as pl
from jax.experimental.pallas import tpu as pltpu
from jax.sharding import Mesh
from jax.sharding import PartitionSpec as P

BLOCK = 128
KB = 4
CB = 8
RB = 8
SA = 24
SB = 6
FIRST = 16
LATER = SA - FIRST
HALF = RB // 2
META = 16
ROWS_1 = FIRST * BLOCK + META
ROWS_2 = LATER * BLOCK
ROWS_B = 2 * SB * BLOCK + META
OFFSETS = (0, -1, 1, -2, 2, -3, 3, 4)
HEIGHT = HALF * BLOCK
NEAR = (0, 1, 2, 3, 4)
FAR = (5, 6, 7)
STEPS = 64.0
TOP = 32760.0
LOWEST = -120.0
GRANT = 56 * 1024 * 1024

ANY = pl.BlockSpec(memory_space=pl.ANY)
SMEM = pl.BlockSpec(memory_space=pltpu.SMEM)
VMEM = pl.BlockSpec(memory_space=pltpu.VMEM)


def pack_kernel(a_pos, a_count, b_pos, b_count, a_vals, b_vals, p1, p2, pb, place):
    pb[: 2 * SB * BLOCK, :] = b_vals[...]
    p1[...] = jnp.zeros_like(p1)
    p2[...] = jnp.zeros_like(p2)
    for p in range(KB * RB):
        place[p] = -1
    for s in range(SA):
        place[a_pos[s]] = jnp.where(s < a_count[0], s, -1)
    lane = lax.broadcasted_iota(jnp.int32, (META, BLOCK), 1)

    def send(p, carry):
        rank, low, words = carry
        slot = place[p]
        live = slot >= 0
        start = pl.ds(pl.multiple_of(jnp.maximum(slot, 0) * BLOCK, BLOCK), BLOCK)

        @pl.when(live & (rank < FIRST))
        def _():
            p1[pl.ds(pl.multiple_of(rank * BLOCK, BLOCK), BLOCK), :] = a_vals[start, :]

        @pl.when(live & (rank >= FIRST))
        def _():
            p2[pl.ds(pl.multiple_of((rank - FIRST) * BLOCK, BLOCK), BLOCK), :] = a_vals[start, :]

        one = live.astype(jnp.int32)
        words = jnp.where((lane == rank) & live, p, words)
        return rank + one, low + jnp.where(p < HALF * KB, one, 0), words

    words = jnp.zeros((META, BLOCK), jnp.int32)
    total, low, words = lax.fori_loop(0, KB * RB, send, (jnp.int32(0), jnp.int32(0), words))
    words = jnp.where(lane == SA, low, words)
    words = jnp.where(lane == SA + 1, total, words)
    p1[FIRST * BLOCK :, :] = words.astype(jnp.float32).astype(jnp.bfloat16)
    words = jnp.zeros((META, BLOCK), jnp.int32)
    for h in range(2):
        for s in range(SB):
            words = jnp.where(lane == h * SB + s, b_pos[h, s], words)
        words = jnp.where(lane == 2 * SB + h, b_count[h], words)
    pb[2 * SB * BLOCK :, :] = words.astype(jnp.float32).astype(jnp.bfloat16)


def pack(a_pos, a_count, b_pos, b_count, a_vals, b_vals):
    return pl.pallas_call(
        pack_kernel,
        out_shape=[
            jax.ShapeDtypeStruct((ROWS_1, BLOCK), jnp.bfloat16),
            jax.ShapeDtypeStruct((ROWS_2, BLOCK), jnp.bfloat16),
            jax.ShapeDtypeStruct((ROWS_B, BLOCK), jnp.bfloat16),
        ],
        in_specs=[SMEM, SMEM, SMEM, SMEM, VMEM, VMEM],
        out_specs=[VMEM, VMEM, VMEM],
        scratch_shapes=[pltpu.SMEM((KB * RB,), jnp.int32)],
        name="pack",
    )(a_pos, a_count, b_pos, b_count, a_vals, b_vals)


def x_distances(p):
    offset = OFFSETS[p]
    if offset % 2 == 0:
        return (offset // 2 % 4,)
    return ((offset - 1) // 2 % 4, (offset + 1) // 2 % 4)


def wanted(panels):
    lists = [x_distances(p) for p in panels]
    same = sorted({d for one in lists if len(one) == 1 for d in one})
    other = sorted({d for one in lists if len(one) == 2 for d in one})
    return same, other


def product_kernel(upper, panels, first, last, place, *refs):
    count = len(panels)
    refs = list(refs)
    ones = {p: [refs.pop(0) for _ in range(1 if p < 7 else 2)] for p in panels}
    twos = {p: [refs.pop(0) for _ in range(1 if p < 7 else 2)] for p in panels} if upper else {}
    same_wanted, other_wanted = wanted(panels)
    same = {d: refs.pop(0) for d in same_wanted}
    other = {d: refs.pop(0) for d in other_wanted}
    acc_in = None if first else refs.pop(0)
    outs = [refs.pop(0) for _ in range(4 if last else 1)]
    a_buf, a_buf2, b_buf, dense, acc, meta, words, said = refs[:8]
    sem_a, sem_a2, sem_b, sem_am, sem_bm, sem_w = refs[8:]
    i, core, yl, z, yh = (place[k] for k in range(5))

    def whole(of, buf, sem, n, split):
        if len(of) == 1:
            return [pltpu.make_async_copy(of[0], buf.at[n], sem.at[n])]
        rest = buf.shape[1] - split
        return [
            pltpu.make_async_copy(of[0], buf.at[n, pl.ds(0, split)], sem.at[n]),
            pltpu.make_async_copy(of[1], buf.at[n, pl.ds(split, rest)], sem.at[count]),
        ]

    def a_copies(n, p):
        copies = whole(ones[p], a_buf, sem_a, n, FIRST // 2 * BLOCK)
        if upper:
            copies += whole(twos[p], a_buf2, sem_a2, n, LATER // 2 * BLOCK)
        return copies

    def a_meta(n, p):
        of = ones[p][-1]
        return pltpu.make_async_copy(of.at[pl.ds(of.shape[0] - META, META)], meta.at[n], sem_am.at[n])

    def b_source(p):
        distances = x_distances(p)
        if len(distances) == 1:
            return [(None, same[distances[0]])]
        return [(c, other[d]) for c, d in enumerate(distances)]

    def b_meta(n, p, group, of):
        k = n * 2 + group
        start = group * ROWS_B + 2 * SB * BLOCK
        return pltpu.make_async_copy(of.at[pl.ds(start, META)], meta.at[count + k], sem_bm.at[k])

    def stack(p):
        residue = lax.rem(i + z + OFFSETS[p] + 8, 8)
        return jnp.where(residue < i, 1 - yl, yl)

    def b_copy(n, p, group, of):
        start = pl.multiple_of(group * ROWS_B + stack(p) * (SB * BLOCK), META)
        return pltpu.make_async_copy(of.at[pl.ds(start, SB * BLOCK)], b_buf.at[n, group], sem_b.at[n * 2 + group])

    def each_b(make):
        for n, p in enumerate(panels):
            for group in range(2):
                for when, of in b_source(p):
                    if when is None:
                        make(n, p, group, of).start()
                    else:

                        @pl.when(core == when)
                        def _(n=n, p=p, group=group, of=of):
                            make(n, p, group, of).start()

    for n, p in enumerate(panels):
        a_meta(n, p).start()
    each_b(b_meta)
    if not first:
        acc_copy = pltpu.make_async_copy(acc_in, acc, sem_w.at[1])
        acc_copy.start()
    for n, p in enumerate(panels):
        for copy in a_copies(n, p):
            copy.start()
    each_b(b_copy)

    for n, p in enumerate(panels):
        a_meta(n, p).wait()
        for group in range(2):
            b_meta(n, p, group, b_source(p)[0][1]).wait()
    for k in range(3 * count):
        words[pl.ds(k, 1), :] = meta[k].astype(jnp.float32)[:1].astype(jnp.int32)
    to_scalars = pltpu.make_async_copy(words, said, sem_w.at[0])
    to_scalars.start()
    dense[...] = jnp.zeros_like(dense)
    if first:
        acc[...] = jnp.zeros_like(acc)
    to_scalars.wait()
    if not first:
        acc_copy.wait()

    blank = jnp.zeros((BLOCK, BLOCK), jnp.bfloat16)
    for n, p in enumerate(panels):
        for copy in a_copies(n, p):
            copy.wait()
        for group in range(2):
            b_copy(n, p, group, b_source(p)[0][1]).wait()

        def put(s, carry, source, skip, n=n):
            at = said[n, s]
            row = lax.shift_right_logical(at, 2) - (HALF if upper else 0)
            to = pl.multiple_of(row * BLOCK, BLOCK)
            start = pl.multiple_of((s - skip) * BLOCK, BLOCK)
            dense[n, lax.rem(at, KB), pl.ds(to, BLOCK), :] = source[n, pl.ds(start, BLOCK), :]
            return carry

        low, total = said[n, SA], said[n, SA + 1]
        if upper:
            lax.fori_loop(low, jnp.minimum(total, FIRST), functools.partial(put, source=a_buf, skip=0), 0)
            lax.fori_loop(FIRST, total, functools.partial(put, source=a_buf2, skip=FIRST), 0)
        else:
            lax.fori_loop(0, low, functools.partial(put, source=a_buf, skip=0), 0)

        h = stack(p)
        for s in range(SB):
            for group in range(2):
                k = count + 2 * n + group
                at = said[k, h * SB + s]
                live = s < said[k, 2 * SB + h]
                right = jnp.where(live, b_buf[n, group, s * BLOCK : (s + 1) * BLOCK, :], blank)
                left = dense[n, lax.shift_right_logical(at, 3)]
                acc[group * CB + lax.rem(at, CB)] += jnp.dot(left, right, preferred_element_type=jnp.float32)

    if not last:
        out_copy = pltpu.make_async_copy(acc, outs[0], sem_w.at[2])
        out_copy.start()
        out_copy.wait()
        return
    own_out, q2_out, qp_out, qm_out = outs
    for c in range(CB // 2):
        own_out[:, c * BLOCK : (c + 1) * BLOCK] = acc[yh * (CB // 2) + c]
    row = lax.broadcasted_iota(jnp.int32, (META, BLOCK), 0)
    for q_out, group, side in (
        (q2_out, 0, 1 - yh),
        (qp_out, 1, jnp.where(yl == 1, 1 - yh, yh)),
        (qm_out, 1, jnp.where(yl == 1, yh, 1 - yh)),
    ):
        for c in range(CB // 2):
            columns = slice(c * BLOCK, (c + 1) * BLOCK)
            codes = jnp.zeros((META, BLOCK), jnp.float32)
            for r in range(HALF):
                rows = slice(r * BLOCK, (r + 1) * BLOCK)
                value = acc[group * CB + side * (CB // 2) + c, rows, :]
                peak = jnp.max(jnp.max(jnp.abs(value), axis=0, keepdims=True), axis=1, keepdims=True)
                code = jnp.ceil(jnp.maximum(jnp.log2(peak), LOWEST) * STEPS)
                scaled = value * (TOP * jnp.exp2(code * (-1.0 / STEPS)))
                q_out[rows, columns] = jnp.round(scaled).astype(jnp.int32).astype(jnp.int16)
                codes = jnp.where(row == r, code, codes)
            q_out[HEIGHT:, columns] = codes.astype(jnp.int32).astype(jnp.int16)


def product(upper, panels, place, ones, twos, same, other, so_far, last):
    sent = jax.ShapeDtypeStruct((HEIGHT + META, CB // 2 * BLOCK), jnp.int16)
    count = len(panels)

    def picked(of):
        return [one for p in panels for one in (of[p : p + 1] if p < 7 else of[7:9])]

    arrays = picked(ones) + (picked(twos) if upper else [])
    same_wanted, other_wanted = wanted(panels)
    arrays += [same[d] for d in same_wanted] + [other[d] for d in other_wanted]
    first = so_far is None
    if not first:
        arrays.append(so_far)
    if last:
        outs = [jax.ShapeDtypeStruct((HEIGHT, CB // 2 * BLOCK), jnp.float32), sent, sent, sent]
    else:
        outs = jax.ShapeDtypeStruct((2 * CB, HEIGHT, BLOCK), jnp.float32)
    return pl.pallas_call(
        functools.partial(product_kernel, upper, panels, first, last),
        out_shape=outs,
        in_specs=[SMEM] + [ANY] * len(arrays),
        out_specs=[VMEM] * 4 if last else ANY,
        scratch_shapes=[
            pltpu.VMEM((count, ROWS_1, BLOCK), jnp.bfloat16),
            pltpu.VMEM((count, ROWS_2, BLOCK) if upper else (1, META, BLOCK), jnp.bfloat16),
            pltpu.VMEM((count, 2, SB * BLOCK, BLOCK), jnp.bfloat16),
            pltpu.VMEM((count, KB, HEIGHT, BLOCK), jnp.bfloat16),
            pltpu.VMEM((2 * CB, HEIGHT, BLOCK), jnp.float32),
            pltpu.VMEM((3 * count, META, BLOCK), jnp.bfloat16),
            pltpu.VMEM((24, BLOCK), jnp.int32),
            pltpu.SMEM((24, BLOCK), jnp.int32),
            pltpu.SemaphoreType.DMA((count + 1,)),
            pltpu.SemaphoreType.DMA((count + 1,)),
            pltpu.SemaphoreType.DMA((2 * count,)),
            pltpu.SemaphoreType.DMA((count,)),
            pltpu.SemaphoreType.DMA((2 * count,)),
            pltpu.SemaphoreType.DMA((3,)),
        ],
        compiler_params=pltpu.CompilerParams(vmem_limit_bytes=GRANT),
        cost_estimate=pl.CostEstimate(flops=1_000_000_000 * count, bytes_accessed=2_000_000 * count, transcendentals=0),
        name=("upper" if upper else "lower") + ("_last" if last else "_first"),
    )(place, *arrays)


def sum_kernel(*refs):
    own, parts, out = refs[0], refs[1:7], refs[-1]
    r = pl.program_id(0)
    row = lax.broadcasted_iota(jnp.int32, (META, CB // 2 * BLOCK), 0)
    total = own[...]
    for value, codes in zip(parts[:3], parts[3:]):
        code = jnp.where(row == r, codes[...].astype(jnp.int32).astype(jnp.float32), 0.0)
        scale = jnp.exp2(jnp.sum(code, axis=0, keepdims=True) * (1.0 / STEPS)) * (1.0 / TOP)
        total = total + value[...].astype(jnp.int32).astype(jnp.float32) * scale
    out[...] = total


def add_up(own, parts, so_far):
    width = CB // 2 * BLOCK
    skip = 0 if so_far is None else HALF
    values = pl.BlockSpec((BLOCK, width), lambda r: (r, 0))
    codes = pl.BlockSpec((META, width), lambda r: (HEIGHT // META, 0))
    extra = () if so_far is None else (so_far,)
    return pl.pallas_call(
        sum_kernel,
        grid=(HALF,),
        out_shape=jax.ShapeDtypeStruct((RB * BLOCK, width), jnp.float32),
        in_specs=[values] + [values] * 3 + [codes] * 3 + [ANY] * len(extra),
        out_specs=pl.BlockSpec((BLOCK, width), lambda r: (r + skip, 0)),
        input_output_aliases={7: 0} if extra else {},
        name="add_up",
    )(own, *parts, *parts, *extra)


def shift(value, axis, distance):
    size = lax.axis_size(axis)
    return lax.ppermute(value, axis, [(k, (k + distance) % size) for k in range(size)])


def shift_y(value, distance):
    pairs = []
    for y in range(4):
        to = (y + distance) % 4
        pairs.append((y % 2 * 2 + y // 2, to % 2 * 2 + to // 2))
    return lax.ppermute(value, ("yl", "yh"), pairs)


def round_z(own, split, after=None):
    up, down, ups, downs = own, own, [], []
    for step in range(3):
        if step == 1 and after is not None:
            up, down, _ = lax.optimization_barrier((up, down, after))
        up, down = shift(up, "z", 1), shift(down, "z", -1)
        ups.append(up)
        downs.append(down)
    opposite = [shift(up[:split], "z", 1), shift(down[split:], "z", -1)]
    return [own, ups[0], downs[0], ups[1], downs[1], ups[2], downs[2], *opposite]


def per_device(a_vals, a_pos, a_count, b_vals, b_pos, b_count):
    place = jnp.stack(
        [
            lax.axis_index("x") * 2 + lax.axis_index("core"),
            lax.axis_index("core"),
            lax.axis_index("yl"),
            lax.axis_index("z"),
            lax.axis_index("yh"),
        ]
    ).astype(jnp.int32)
    p1, p2, pb = pack(
        a_pos.reshape(SA),
        a_count.reshape(1),
        b_pos.reshape(2, SB),
        b_count.reshape(2),
        a_vals.reshape(SA * BLOCK, BLOCK),
        b_vals.reshape(2 * SB * BLOCK, BLOCK),
    )
    both = jnp.concatenate([pb, shift(pb, "yl", 1)], axis=0)
    after, before = shift(both, "x", -1), shift(both, "x", 1)
    late, _, _ = lax.optimization_barrier((both, after, before))
    same = [both, after, shift(late, "x", 2), before]
    other = [shift(one, "core", 1) for one in same]
    ones = round_z(p1, FIRST // 2 * BLOCK)
    p2, _ = lax.optimization_barrier((p2, ones[6]))

    def half(upper, twos):
        so_far = product(upper, NEAR, place, ones, twos, same, other, None, False)
        own, q2, qp, qm = product(upper, FAR, place, ones, twos, same, other, so_far, True)
        return own, (shift_y(q2, 2), shift_y(qp, 1), shift_y(qm, -1)), q2

    own1, parts1, done = half(False, None)
    twos = round_z(p2, LATER // 2 * BLOCK, done)
    own2, parts2, _ = half(True, twos)
    return add_up(own2, parts2, add_up(own1, parts1, None))


def solution(mesh):
    cores = 2
    x = mesh.shape["row"] // cores
    z = mesh.shape["col"] // 2
    split = Mesh(mesh.devices.reshape(x, cores, 2, z, mesh.shape["layer"]), ("x", "core", "yl", "z", "yh"))
    lead = (("x", "core"), ("yl", "z"), "yh")
    return jax.shard_map(
        per_device,
        mesh=split,
        in_specs=(P(*lead), P(*lead), P(*lead), P(*lead), P(*lead), P(*lead)),
        out_specs=P(("x", "core"), ("yl", "z", "yh")),
        check_vma=False,
    )
```

time: 1020 us -> 156 us (0.15); the launches traced: 1010 us -> 155 us
  loops' own time: 305 us -> 0 us
  starting transfers between devices: 307 us -> 46 us
  matrix products: 211 us -> 0 us
  local copies, waits for them, and re-layouts: 66.9 us -> 5.93 us
  Pallas kernels: 0 us -> 47.1 us
  between operations: 33.3 us -> 1 us
  waiting for transfers between devices: 85.4 us -> 55.4 us
    another operation x1 -> x0, loops' own time: 305 us -> none  [per_device(): lax.fori_loop(0, n_col - 1, advance, (start, tuple(a_state), tuple(b_stat...]
    ppermute x90 -> x30, starting transfers between devices: 307 us -> 46 us  [the longest x24 36.9 us: shift(): lax.ppermute(value, axis, [(k, (k + distance) % size) for k in range(size)])]
    dot_general x112 -> x0, matrix products: 211 us -> none  [the longest x96 201 us: contribute(): term = jnp.dot(left, b_vals[slot], preferred_element_type=jnp.float32)]
    reduce_scatter x1 -> x0, waiting for transfers between devices: 65.8 us -> none  [per_device(): return lax.psum_scatter(total, 'layer', scatter_dimension=1, tiled=True)]
    pallas_call x0 -> x7, Pallas kernels: none -> 47.1 us  [the longest x4 36.2 us: product(): pl.pallas_call(functools.partial(product_kernel, upper, panels, first, la...]
    ppermute x90 -> x30, waiting for transfers between devices: 19.6 us -> 55.4 us  [the longest x24 46.1 us: shift(): lax.ppermute(value, axis, [(k, (k + distance) % size) for k in range(size)])]
    another operation x75 -> x1, local copies, waits for them, and re-layouts: 32 us -> 0.66 us  [per_device(): jnp.stack([lax.axis_index('x') * 2 + lax.axis_index('core'), lax.axis_ind...]
    dynamic_slice x32 -> x0, local copies, waits for them, and re-layouts: 10.8 us -> none  [pick(): lax.dynamic_index_in_dim(member, index, 0, keepdims=False)]
  transfers between devices with their start and end apart: 91 -> 30, of which waited for: 16 -> 12; matrix products, arithmetic and copies ran while one was open for 24% -> 1% of each run, Pallas kernels for 0% -> 26%
where the time goes in v1:
time: 156 us; the launch traced here: 155 us
  waiting for transfers between devices  55.4 us (36%)
  Pallas kernels  47.1 us (30%)
  starting transfers between devices  46 us (29%)
  local copies, waits for them, and re-layouts  5.93 us (4%)
    ppermute x24, waiting for transfers between devices, shift(): lax.ppermute(value, axis, [(k, (k + distance) % size) for k in range(size)])  46.1 us
    ppermute x24, starting transfers between devices, shift(): lax.ppermute(value, axis, [(k, (k + distance) % size) for k in range(size)])  36.9 us
    pallas_call x4, Pallas kernels, product(): pl.pallas_call(functools.partial(product_kernel, upper, panels, first, la...  36.2 us
    ppermute x6, waiting for transfers between devices, shift_y(): return lax.ppermute(value, ('yl', 'yh'), pairs)  9.35 us
    ppermute x6, starting transfers between devices, shift_y(): return lax.ppermute(value, ('yl', 'yh'), pairs)  9.15 us
    pallas_call x2, Pallas kernels, add_up(): pl.pallas_call(sum_kernel, grid=(HALF,), out_shape=jax.ShapeDtypeStruct((...  7.78 us
    unnamed x49, local copies, waits for them, and re-layouts  5.16 us
  transfers between devices with their start and end apart: 30, of which 12 were waited for; matrix products, arithmetic and copies ran while one was open for 1% of the time, Pallas kernels for 26%

profile of v1, /device:TPU:8, one launch (start us, length us, event | category | flops | bytes accessed | tf_op | source)
XLA Modules:
  0.0 155.5 jit_solution(4404967245150642062)
XLA Ops:
  0.7 3.1 %pack.1 = (bf16[2064,128]{1,0:T(8,128)(2,1)}, bf16[1024,128]{1,0:T(8,128)(2,1)}, bf16[1552,128]{1,0:T(8,128)(2,1)}) custom-call(s32[24]{0:T(128)} %bitcast.15, s32[1]{0:T(128)} %bitcast.11.a_count, s32[2,6]{1,0:T(2,128)} %bitcast.14, s32[2]{0:T(128)} %bitcast.16, bf16[3072,128]{1,0:T(8,128)(2,1)} %bitcast.12, bf16[1536,128]{1,0:T(8,128)(2,1)} %bitcast.13), custom_call_target="tpu_custom_call" | custom-call | tf_op jit(solution)/shard_map/pack/pallas_call | solution.py:80
  3.7 2.2 %collective-permute-start.10 = (bf16[1552,128]{1,0:T(8,128)(2,1)}, bf16[1552,128]{1,0:T(8,128)(2,1)S(1)}, u32[]{:S(2)}, u32[]{:S(2)}) collective-permute-start(bf16[1552,128]{1,0:T(8,128)(2,1)} %get-tuple-element.23), channel_id=1, source_target_pairs={{0,16},{16,0},{1,17},{17,1},{2,18},{18,2},{3,19},{19,3},{4,20},{20... | collective-permute-start | bytes 1191944 | tf_op jit(solution)/shard_map/ppermute | solution.py:333
  5.9 4.1 %collective-permute-start.3 = (bf16[2064,128]{1,0:T(8,128)(2,1)}, bf16[2064,128]{1,0:T(8,128)(2,1)S(1)}, u32[]{:S(2)}, u32[]{:S(2)}) collective-permute-start(bf16[2064,128]{1,0:T(8,128)(2,1)} %get-tuple-element.20.refs_0_), channel_id=1, source_target_pairs={{0,14},{2,0},{4,2},{6,4},{8,6},{10,8},{12,10},{14,12},{1,15},{3,1}... | collective-permute-start | bytes 1585160 | tf_op jit(solution)/shard_map/ppermute | solution.py:333
  11.1 3.8 %collective-permute-done.10 = bf16[1552,128]{1,0:T(8,128)(2,1)S(1)} collective-permute-done((bf16[1552,128]{1,0:T(8,128)(2,1)}, bf16[1552,128]{1,0:T(8,128)(2,1)S(1)}, u32[]{:S(2)}, u32[]{:S(2)}) %collective-permute-start.10) | collective-permute-done | bytes 397344 | tf_op jit(solution)/shard_map/ppermute | solution.py:333
  15.0 2.8 %collective-permute-start.11 = (bf16[3104,128]{1,0:T(8,128)(2,1)S(1)}, bf16[3104,128]{1,0:T(8,128)(2,1)S(1)}, u32[]{:S(2)}, u32[]{:S(2)}) collective-permute-start(bf16[3104,128]{1,0:T(8,128)(2,1)S(1)} %constant_dynamic-update-slice_fusion.refs_5_.refs_10_), channel_id=1, source_target_pairs={{0,192},{64,0},{128,64},{192,128},{1,193},{65,1},{129,65},{193,129... | collective-permute-start | bytes 2383880 | tf_op jit(solution)/shard_map/ppermute | solution.py:333
  17.8 1.9 %collective-permute-start = (bf16[2064,128]{1,0:T(8,128)(2,1)}, bf16[2064,128]{1,0:T(8,128)(2,1)S(1)}, u32[]{:S(2)}, u32[]{:S(2)}) collective-permute-start(bf16[2064,128]{1,0:T(8,128)(2,1)} %get-tuple-element.20.refs_0_), channel_id=1, source_target_pairs={{0,2},{2,4},{4,6},{6,8},{8,10},{10,12},{12,14},{14,0},{1,3},{3,5},... | collective-permute-start | bytes 1585160 | tf_op jit(solution)/shard_map/ppermute | solution.py:333
  19.7 1.6 %collective-permute-done.3.refs_2_ = bf16[2064,128]{1,0:T(8,128)(2,1)S(1)} collective-permute-done((bf16[2064,128]{1,0:T(8,128)(2,1)}, bf16[2064,128]{1,0:T(8,128)(2,1)S(1)}, u32[]{:S(2)}, u32[]{:S(2)}) %collective-permute-start.3) | collective-permute-done | bytes 528416 | tf_op jit(solution)/shard_map/ppermute | solution.py:333
  21.3 3.6 %collective-permute-start.4 = (bf16[2064,128]{1,0:T(8,128)(2,1)S(1)}, bf16[2064,128]{1,0:T(8,128)(2,1)S(1)}, u32[]{:S(2)}, u32[]{:S(2)}) collective-permute-start(bf16[2064,128]{1,0:T(8,128)(2,1)S(1)} %collective-permute-done.3.refs_2_), channel_id=1, source_target_pairs={{0,14},{2,0},{4,2},{6,4},{8,6},{10,8},{12,10},{14,12},{1,15},{3,1}... | collective-permute-start | bytes 1585160 | tf_op jit(solution)/shard_map/ppermute | solution.py:333
  24.9 9.8 %collective-permute-done.refs_1_ = bf16[2064,128]{1,0:T(8,128)(2,1)S(1)} collective-permute-done((bf16[2064,128]{1,0:T(8,128)(2,1)}, bf16[2064,128]{1,0:T(8,128)(2,1)S(1)}, u32[]{:S(2)}, u32[]{:S(2)}) %collective-permute-start) | collective-permute-done | bytes 528416 | tf_op jit(solution)/shard_map/ppermute | solution.py:333
  34.7 2.6 %collective-permute-done.12.refs_7_.refs_12_ = bf16[3104,128]{1,0:T(8,128)(2,1)S(1)} collective-permute-done((bf16[3104,128]{1,0:T(8,128)(2,1)S(1)}, bf16[3104,128]{1,0:T(8,128)(2,1)S(1)}, u32[]{:S(2)}, u32[]{:S(2)}) %collective-permute-start.12) | collective-permute-done | bytes 794656 | tf_op jit(solution)/shard_map/ppermute | solution.py:333
  37.3 5.9 %collective-permute-start.5 = (bf16[2064,128]{1,0:T(8,128)(2,1)S(1)}, bf16[2064,128]{1,0:T(8,128)(2,1)S(1)}, u32[]{:S(2)}, u32[]{:S(2)}) collective-permute-start(bf16[2064,128]{1,0:T(8,128)(2,1)S(1)} %collective-permute-done.4.refs_4_), channel_id=1, source_target_pairs={{0,14},{2,0},{4,2},{6,4},{8,6},{10,8},{12,10},{14,12},{1,15},{3,1}... | collective-permute-start | bytes 1585160 | tf_op jit(solution)/shard_map/ppermute | solution.py:333
  43.8 4.2 %collective-permute-done.1.refs_3_ = bf16[2064,128]{1,0:T(8,128)(2,1)} collective-permute-done((bf16[2064,128]{1,0:T(8,128)(2,1)S(1)}, bf16[2064,128]{1,0:T(8,128)(2,1)}, u32[]{:S(2)}, u32[]{:S(2)}) %collective-permute-start.1) | collective-permute-done | bytes 528416 | tf_op jit(solution)/shard_map/ppermute | solution.py:333
  48.0 4.5 %collective-permute-done.5.refs_1_ = bf16[2064,128]{1,0:T(8,128)(2,1)S(1)} collective-permute-done((bf16[2064,128]{1,0:T(8,128)(2,1)S(1)}, bf16[2064,128]{1,0:T(8,128)(2,1)S(1)}, u32[]{:S(2)}, u32[]{:S(2)}) %collective-permute-start.5) | collective-permute-done | bytes 528416 | tf_op jit(solution)/shard_map/ppermute | solution.py:333
  52.5 3.8 %collective-permute-done.13.refs_4_.refs_8_ = bf16[3104,128]{1,0:T(8,128)(2,1)} collective-permute-done((bf16[3104,128]{1,0:T(8,128)(2,1)S(1)}, bf16[3104,128]{1,0:T(8,128)(2,1)}, u32[]{:S(2)}, u32[]{:S(2)}) %collective-permute-start.13) | collective-permute-done | bytes 794656 | tf_op jit(solution)/shard_map/ppermute | solution.py:333
  57.0 8.5 %collective-permute-done.2.refs_0_ = bf16[2064,128]{1,0:T(8,128)(2,1)S(1)} collective-permute-done((bf16[2064,128]{1,0:T(8,128)(2,1)}, bf16[2064,128]{1,0:T(8,128)(2,1)S(1)}, u32[]{:S(2)}, u32[]{:S(2)}) %collective-permute-start.2) | collective-permute-done | bytes 528416 | tf_op jit(solution)/shard_map/ppermute | solution.py:333
  65.5 3.3 %collective-permute-start.9 = (bf16[1024,128]{1,0:T(8,128)(2,1)}, bf16[1024,128]{1,0:T(8,128)(2,1)S(1)}, u32[]{:S(2)}, u32[]{:S(2)}) collective-permute-start(bf16[1024,128]{1,0:T(8,128)(2,1)} %get-tuple-element.22.refs_5_), channel_id=1, source_target_pairs={{0,14},{2,0},{4,2},{6,4},{8,6},{10,8},{12,10},{14,12},{1,15},{3,1}... | collective-permute-start | bytes 786440 | tf_op jit(solution)/shard_map/ppermute | solution.py:333
  70.9 9.9 %lower_first.1.refs_8_ = f32[16,512,128]{2,1,0:T(8,128)} custom-call(s32[5]{0:T(128)} %stack.23.place, bf16[2064,128]{1,0:T(8,128)(2,1)} %get-tuple-element.20.refs_0_, bf16[2064,128]{1,0:T(8,128)(2,1)} %copy-done.14, bf16[2064,128]{1,0:T(8,128)(2,1)} %copy-done.13, bf16[2064,128]{1,0:T(8,128)(2,1)} %collective-permute-done.1.refs_3_, ...), custom_call_target="tpu_custom_call" | custom-call | flops 5000000000 | bytes 10000000 | tf_op jit(solution)/shard_map/lower_first/pallas_call | solution.py:275
  81.7 7.9 %lower_last.1 = (f32[512,512]{1,0:T(8,128)}, s16[528,512]{1,0:T(8,128)(2,1)}, s16[528,512]{1,0:T(8,128)(2,1)}, s16[528,512]{1,0:T(8,128)(2,1)}) custom-call(s32[5]{0:T(128)} %stack.23.place, bf16[2064,128]{1,0:T(8,128)(2,1)} %copy-done.8, bf16[2064,128]{1,0:T(8,128)(2,1)} %copy-done.7, bf16[1024,128]{1,0:T(8,128)(2,1)} %copy-done.17, ...), custom_call_target="tpu_custom_call" | custom-call | flops 3000000000 | bytes 6000000 | tf_op jit(solution)/shard_map/lower_last/pallas_call | solution.py:275
  89.7 3.2 %collective-permute-start.20 = (bf16[1024,128]{1,0:T(8,128)(2,1)S(1)}, bf16[1024,128]{1,0:T(8,128)(2,1)S(1)}, u32[]{:S(2)}, u32[]{:S(2)}) collective-permute-start(bf16[1024,128]{1,0:T(8,128)(2,1)S(1)} %collective-permute-done.9.refs_7_), channel_id=1, source_target_pairs={{0,14},{2,0},{4,2},{6,4},{8,6},{10,8},{12,10},{14,12},{1,15},{3,1}... | collective-permute-start | bytes 786440 | tf_op jit(solution)/shard_map/ppermute | solution.py:333
  92.9 6.5 %collective-permute-done.18.refs_8_ = bf16[1024,128]{1,0:T(8,128)(2,1)S(1)} collective-permute-done((bf16[1024,128]{1,0:T(8,128)(2,1)S(1)}, bf16[1024,128]{1,0:T(8,128)(2,1)S(1)}, u32[]{:S(2)}, u32[]{:S(2)}) %collective-permute-start.18) | collective-permute-done | bytes 262176 | tf_op jit(solution)/shard_map/ppermute | solution.py:333
  99.5 3.5 %collective-permute-start.21 = (bf16[1024,128]{1,0:T(8,128)(2,1)S(1)}, bf16[1024,128]{1,0:T(8,128)(2,1)S(1)}, u32[]{:S(2)}, u32[]{:S(2)}) collective-permute-start(bf16[1024,128]{1,0:T(8,128)(2,1)S(1)} %collective-permute-done.20.refs_9_), channel_id=1, source_target_pairs={{0,14},{2,0},{4,2},{6,4},{8,6},{10,8},{12,10},{14,12},{1,15},{3,1}... | collective-permute-start | bytes 786440 | tf_op jit(solution)/shard_map/ppermute | solution.py:333
  103.0 2.5 %collective-permute-start.27 = (s16[528,512]{1,0:T(8,128)(2,1)}, s16[528,512]{1,0:T(8,128)(2,1)S(1)}, u32[]{:S(2)}, u32[]{:S(2)}) collective-permute-start(s16[528,512]{1,0:T(8,128)(2,1)} %get-tuple-element.25), channel_id=1, source_target_pairs={{0,1},{16,17},{1,0},{17,16},{2,3},{18,19},{3,2},{19,18},{4,5},{20,... | collective-permute-start | bytes 1622024 | tf_op jit(solution)/shard_map/ppermute | solution.py:341
  105.5 2.0 %collective-permute-start.29 = (s16[528,512]{1,0:T(8,128)(2,1)}, s16[528,512]{1,0:T(8,128)(2,1)S(1)}, u32[]{:S(2)}, u32[]{:S(2)}) collective-permute-start(s16[528,512]{1,0:T(8,128)(2,1)} %get-tuple-element.34), channel_id=1, source_target_pairs={{0,17},{16,0},{1,16},{17,1},{2,19},{18,2},{3,18},{19,3},{4,21},{20... | collective-permute-start | bytes 1622024 | tf_op jit(solution)/shard_map/ppermute | solution.py:341
  108.6 3.3 %collective-permute-start.23 = (bf16[512,128]{1,0:T(8,128)(2,1)S(1)}, bf16[512,128]{1,0:T(8,128)(2,1)S(1)}, u32[]{:S(2)}, u32[]{:S(2)}) collective-permute-start(bf16[512,128]{1,0:T(8,128)(2,1)S(1)} %slice.19), channel_id=1, source_target_pairs={{0,14},{2,0},{4,2},{6,4},{8,6},{10,8},{12,10},{14,12},{1,15},{3,1}... | collective-permute-start | bytes 393224 | tf_op jit(solution)/shard_map/ppermute | solution.py:333
  111.9 10.3 %upper_first.1.refs_12_ = f32[16,512,128]{2,1,0:T(8,128)} custom-call(s32[5]{0:T(128)} %stack.23.place, bf16[2064,128]{1,0:T(8,128)(2,1)} %get-tuple-element.20.refs_0_, bf16[2064,128]{1,0:T(8,128)(2,1)} %copy-done.14, bf16[2064,128]{1,0:T(8,128)(2,1)} %copy-done.13, bf16[2064,128]{1,0:T(8,128)(2,1)} %collective-permute-done.1.refs_3_, ...), custom_call_target="tpu_custom_call" | custom-call | flops 5000000000 | bytes 10000000 | tf_op jit(solution)/shard_map/upper_first/pallas_call | solution.py:275
  123.6 8.1 %upper_last.1 = (f32[512,512]{1,0:T(8,128)}, s16[528,512]{1,0:T(8,128)(2,1)}, s16[528,512]{1,0:T(8,128)(2,1)}, s16[528,512]{1,0:T(8,128)(2,1)}) custom-call(s32[5]{0:T(128)} %stack.23.place, bf16[2064,128]{1,0:T(8,128)(2,1)} %copy-done.8, bf16[2064,128]{1,0:T(8,128)(2,1)} %copy-done.7, bf16[1024,128]{1,0:T(8,128)(2,1)} %copy-done.17, ...), custom_call_target="tpu_custom_call" | custom-call | flops 3000000000 | bytes 6000000 | tf_op jit(solution)/shard_map/upper_last/pallas_call | solution.py:275
  131.6 2.6 %collective-permute-start.24 = (s16[528,512]{1,0:T(8,128)(2,1)}, s16[528,512]{1,0:T(8,128)(2,1)S(1)}, u32[]{:S(2)}, u32[]{:S(2)}) collective-permute-start(s16[528,512]{1,0:T(8,128)(2,1)} %get-tuple-element.29), channel_id=1, source_target_pairs={{0,1},{16,17},{1,0},{17,16},{2,3},{18,19},{3,2},{19,18},{4,5},{20,... | collective-permute-start | bytes 1622024 | tf_op jit(solution)/shard_map/ppermute | solution.py:341
  134.3 2.0 %collective-permute-start.26 = (s16[528,512]{1,0:T(8,128)(2,1)}, s16[528,512]{1,0:T(8,128)(2,1)S(1)}, u32[]{:S(2)}, u32[]{:S(2)}) collective-permute-start(s16[528,512]{1,0:T(8,128)(2,1)} %get-tuple-element.31), channel_id=1, source_target_pairs={{0,17},{16,0},{1,16},{17,1},{2,19},{18,2},{3,18},{19,3},{4,21},{20... | collective-permute-start | bytes 1622024 | tf_op jit(solution)/shard_map/ppermute | solution.py:341
  137.3 3.9 %add_up.2.refs_7_ = f32[1024,512]{1,0:T(8,128)} custom-call(f32[512,512]{1,0:T(8,128)} %get-tuple-element.32.refs_0_, s16[528,512]{1,0:T(8,128)(2,1)} %copy-done, s16[528,512]{1,0:T(8,128)(2,1)} %copy-done.1, s16[528,512]{1,0:T(8,128)(2,1)} %copy-done.2, s16[528,512]{1,0:T(8,128)(2,1)} %copy-done, s16[528,512]{1,0:T(8,128)(2,1)} %copy-done.1, ...), custom_call_target="tpu_custom_call" | custom-call | tf_op jit(solution)/shard_map/add_up/pallas_call | solution.py:320
  141.2 3.6 %collective-permute-done.24.refs_1_.refs_4_ = s16[528,512]{1,0:T(8,128)(2,1)S(1)} collective-permute-done((s16[528,512]{1,0:T(8,128)(2,1)}, s16[528,512]{1,0:T(8,128)(2,1)S(1)}, u32[]{:S(2)}, u32[]{:S(2)}) %collective-permute-start.24) | collective-permute-done | bytes 540704 | tf_op jit(solution)/shard_map/ppermute | solution.py:341
  144.8 5.7 %collective-permute-done.25.refs_2_.refs_5_ = s16[528,512]{1,0:T(8,128)(2,1)S(1)} collective-permute-done((s16[528,512]{1,0:T(8,128)(2,1)}, s16[528,512]{1,0:T(8,128)(2,1)S(1)}, u32[]{:S(2)}, u32[]{:S(2)}) %collective-permute-start.25) | collective-permute-done | bytes 540704 | tf_op jit(solution)/shard_map/ppermute | solution.py:341
  151.6 3.9 %add_up.3 = f32[1024,512]{1,0:T(8,128)} custom-call(f32[512,512]{1,0:T(8,128)} %get-tuple-element.28.refs_0_, s16[528,512]{1,0:T(8,128)(2,1)} %copy-done.3, s16[528,512]{1,0:T(8,128)(2,1)} %copy-done.4, s16[528,512]{1,0:T(8,128)(2,1)} %copy-done.5, s16[528,512]{1,0:T(8,128)(2,1)} %copy-done.3, ...), custom_call_target="tpu_custom_call", output_to_operand_aliasing={{}: (7, {})} | custom-call | tf_op jit(solution)/shard_map/add_up/pallas_call | solution.py:320
  (90 shorter events, 9.7 us)
Async XLA Ops:
  3.7 11.2 %collective-permute-start.10 = (bf16[1552,128]{1,0:T(8,128)(2,1)}, bf16[1552,128]{1,0:T(8,128)(2,1)S(1)}, u32[]{:S(2)}, u32[]{:S(2)}) collective-permute-start(bf16[1552,128]{1,0:T(8,128)(2,1)} %get-tuple-element.23), channel_id=1, source_target_pairs={{0,16},{16,0},{1,17},{17,1},{2,18},{18,2},{3,19},{19,3},{4,20},{20... | collective-permute-start | bytes 1191944 | tf_op jit(solution)/shard_map/ppermute | solution.py:333
  5.9 15.4 %collective-permute-start.3 = (bf16[2064,128]{1,0:T(8,128)(2,1)}, bf16[2064,128]{1,0:T(8,128)(2,1)S(1)}, u32[]{:S(2)}, u32[]{:S(2)}) collective-permute-start(bf16[2064,128]{1,0:T(8,128)(2,1)} %get-tuple-element.20.refs_0_), channel_id=1, source_target_pairs={{0,14},{2,0},{4,2},{6,4},{8,6},{10,8},{12,10},{14,12},{1,15},{3,1}... | collective-permute-start | bytes 1585160 | tf_op jit(solution)/shard_map/ppermute | solution.py:333
  15.0 55.9 %copy-start.6 = (bf16[3104,128]{1,0:T(8,128)(2,1)}, bf16[3104,128]{1,0:T(8,128)(2,1)S(1)}, u32[]{:S(2)}) copy-start(bf16[3104,128]{1,0:T(8,128)(2,1)S(1)} %constant_dynamic-update-slice_fusion.refs_5_.refs_10_) | copy-start | bytes 2383876
  15.0 19.8 %collective-permute-start.11 = (bf16[3104,128]{1,0:T(8,128)(2,1)S(1)}, bf16[3104,128]{1,0:T(8,128)(2,1)S(1)}, u32[]{:S(2)}, u32[]{:S(2)}) collective-permute-start(bf16[3104,128]{1,0:T(8,128)(2,1)S(1)} %constant_dynamic-update-slice_fusion.refs_5_.refs_10_), channel_id=1, source_target_pairs={{0,192},{64,0},{128,64},{192,128},{1,193},{65,1},{129,65},{193,129... | collective-permute-start | bytes 2383880 | tf_op jit(solution)/shard_map/ppermute | solution.py:333
  17.8 19.5 %collective-permute-start.12 = (bf16[3104,128]{1,0:T(8,128)(2,1)S(1)}, bf16[3104,128]{1,0:T(8,128)(2,1)S(1)}, u32[]{:S(2)}, u32[]{:S(2)}) collective-permute-start(bf16[3104,128]{1,0:T(8,128)(2,1)S(1)} %constant_dynamic-update-slice_fusion.refs_5_.refs_10_), channel_id=1, source_target_pairs={{0,64},{64,128},{128,192},{192,0},{1,65},{65,129},{129,193},{193,1... | collective-permute-start | bytes 2383880 | tf_op jit(solution)/shard_map/ppermute | solution.py:333
  17.8 16.9 %collective-permute-start = (bf16[2064,128]{1,0:T(8,128)(2,1)}, bf16[2064,128]{1,0:T(8,128)(2,1)S(1)}, u32[]{:S(2)}, u32[]{:S(2)}) collective-permute-start(bf16[2064,128]{1,0:T(8,128)(2,1)} %get-tuple-element.20.refs_0_), channel_id=1, source_target_pairs={{0,2},{2,4},{4,6},{6,8},{8,10},{10,12},{12,14},{14,0},{1,3},{3,5},... | collective-permute-start | bytes 1585160 | tf_op jit(solution)/shard_map/ppermute | solution.py:333
  21.3 16.0 %collective-permute-start.4 = (bf16[2064,128]{1,0:T(8,128)(2,1)S(1)}, bf16[2064,128]{1,0:T(8,128)(2,1)S(1)}, u32[]{:S(2)}, u32[]{:S(2)}) collective-permute-start(bf16[2064,128]{1,0:T(8,128)(2,1)S(1)} %collective-permute-done.3.refs_2_), channel_id=1, source_target_pairs={{0,14},{2,0},{4,2},{6,4},{8,6},{10,8},{12,10},{14,12},{1,15},{3,1}... | collective-permute-start | bytes 1585160 | tf_op jit(solution)/shard_map/ppermute | solution.py:333
  34.7 13.3 %collective-permute-start.1 = (bf16[2064,128]{1,0:T(8,128)(2,1)S(1)}, bf16[2064,128]{1,0:T(8,128)(2,1)}, u32[]{:S(2)}, u32[]{:S(2)}) collective-permute-start(bf16[2064,128]{1,0:T(8,128)(2,1)S(1)} %collective-permute-done.refs_1_), channel_id=1, source_target_pairs={{0,2},{2,4},{4,6},{6,8},{8,10},{10,12},{12,14},{14,0},{1,3},{3,5},... | collective-permute-start | bytes 1585160 | tf_op jit(solution)/shard_map/ppermute | solution.py:333
  34.7 36.1 %copy-start.11 = (bf16[3104,128]{1,0:T(8,128)(2,1)}, bf16[3104,128]{1,0:T(8,128)(2,1)S(1)}, u32[]{:S(2)}) copy-start(bf16[3104,128]{1,0:T(8,128)(2,1)S(1)} %collective-permute-done.11.refs_6_.refs_11_) | copy-start | bytes 2383876
  37.3 19.0 %collective-permute-start.13 = (bf16[3104,128]{1,0:T(8,128)(2,1)S(1)}, bf16[3104,128]{1,0:T(8,128)(2,1)}, u32[]{:S(2)}, u32[]{:S(2)}) collective-permute-start(bf16[3104,128]{1,0:T(8,128)(2,1)S(1)} %constant_dynamic-update-slice_fusion.refs_5_.refs_10_), channel_id=1, source_target_pairs={{0,128},{64,192},{128,0},{192,64},{1,129},{65,193},{129,1},{193,65... | collective-permute-start | bytes 2383880 | tf_op jit(solution)/shard_map/ppermute | solution.py:333
  37.3 15.1 %collective-permute-start.5 = (bf16[2064,128]{1,0:T(8,128)(2,1)S(1)}, bf16[2064,128]{1,0:T(8,128)(2,1)S(1)}, u32[]{:S(2)}, u32[]{:S(2)}) collective-permute-start(bf16[2064,128]{1,0:T(8,128)(2,1)S(1)} %collective-permute-done.4.refs_4_), channel_id=1, source_target_pairs={{0,14},{2,0},{4,2},{6,4},{8,6},{10,8},{12,10},{14,12},{1,15},{3,1}... | collective-permute-start | bytes 1585160 | tf_op jit(solution)/shard_map/ppermute | solution.py:333
  43.3 22.3 %collective-permute-start.17 = (bf16[3104,128]{1,0:T(8,128)(2,1)S(1)}, bf16[3104,128]{1,0:T(8,128)(2,1)}, u32[]{:S(2)}, u32[]{:S(2)}) collective-permute-start(bf16[3104,128]{1,0:T(8,128)(2,1)S(1)} %constant_dynamic-update-slice_fusion.refs_5_.refs_10_), channel_id=1, source_target_pairs={{0,32},{32,0},{1,33},{33,1},{2,34},{34,2},{3,35},{35,3},{4,36},{36... | collective-permute-start | bytes 2383880 | tf_op jit(solution)/shard_map/ppermute | solution.py:333
  43.3 25.6 %collective-permute-start.14 = (bf16[3104,128]{1,0:T(8,128)(2,1)S(1)}, bf16[3104,128]{1,0:T(8,128)(2,1)}, u32[]{:S(2)}, u32[]{:S(2)}) collective-permute-start(bf16[3104,128]{1,0:T(8,128)(2,1)S(1)} %collective-permute-done.11.refs_6_.refs_11_), channel_id=1, source_target_pairs={{0,32},{32,0},{1,33},{33,1},{2,34},{34,2},{3,35},{35,3},{4,36},{36... | collective-permute-start | bytes 2383880 | tf_op jit(solution)/shard_map/ppermute | solution.py:333
  48.0 22.3 %collective-permute-start.16 = (bf16[3104,128]{1,0:T(8,128)(2,1)S(1)}, bf16[3104,128]{1,0:T(8,128)(2,1)}, u32[]{:S(2)}, u32[]{:S(2)}) collective-permute-start(bf16[3104,128]{1,0:T(8,128)(2,1)S(1)} %collective-permute-done.12.refs_7_.refs_12_), channel_id=1, source_target_pairs={{0,32},{32,0},{1,33},{33,1},{2,34},{34,2},{3,35},{35,3},{4,36},{36... | collective-permute-start | bytes 2383880 | tf_op jit(solution)/shard_map/ppermute | solution.py:333
  52.5 13.0 %collective-permute-start.2 = (bf16[2064,128]{1,0:T(8,128)(2,1)}, bf16[2064,128]{1,0:T(8,128)(2,1)S(1)}, u32[]{:S(2)}, u32[]{:S(2)}) collective-permute-start(bf16[2064,128]{1,0:T(8,128)(2,1)} %collective-permute-done.1.refs_3_), channel_id=1, source_target_pairs={{0,2},{2,4},{4,6},{6,8},{8,10},{10,12},{12,14},{14,0},{1,3},{3,5},... | collective-permute-start | bytes 1585160 | tf_op jit(solution)/shard_map/ppermute | solution.py:333
  56.3 24.6 %collective-permute-start.15 = (bf16[3104,128]{1,0:T(8,128)(2,1)}, bf16[3104,128]{1,0:T(8,128)(2,1)}, u32[]{:S(2)}, u32[]{:S(2)}) collective-permute-start(bf16[3104,128]{1,0:T(8,128)(2,1)} %collective-permute-done.13.refs_4_.refs_8_), channel_id=1, source_target_pairs={{0,32},{32,0},{1,33},{33,1},{2,34},{34,2},{3,35},{35,3},{4,36},{36... | collective-permute-start | bytes 2383880 | tf_op jit(solution)/shard_map/ppermute | solution.py:333
  65.5 24.1 %collective-permute-start.8 = (bf16[1024,128]{1,0:T(8,128)(2,1)}, bf16[1024,128]{1,0:T(8,128)(2,1)S(1)}, u32[]{:S(2)}, u32[]{:S(2)}) collective-permute-start(bf16[1024,128]{1,0:T(8,128)(2,1)} %get-tuple-element.22.refs_5_), channel_id=1, source_target_pairs={{0,2},{2,4},{4,6},{6,8},{8,10},{10,12},{12,14},{14,0},{1,3},{3,5},... | collective-permute-start | bytes 786440 | tf_op jit(solution)/shard_map/ppermute | solution.py:333
  65.5 24.1 %collective-permute-start.9 = (bf16[1024,128]{1,0:T(8,128)(2,1)}, bf16[1024,128]{1,0:T(8,128)(2,1)S(1)}, u32[]{:S(2)}, u32[]{:S(2)}) collective-permute-start(bf16[1024,128]{1,0:T(8,128)(2,1)} %get-tuple-element.22.refs_5_), channel_id=1, source_target_pairs={{0,14},{2,0},{4,2},{6,4},{8,6},{10,8},{12,10},{14,12},{1,15},{3,1}... | collective-permute-start | bytes 786440 | tf_op jit(solution)/shard_map/ppermute | solution.py:333
  68.8 12.0 %collective-permute-start.7 = (bf16[1040,128]{1,0:T(8,128)(2,1)S(1)}, bf16[1040,128]{1,0:T(8,128)(2,1)S(1)}, u32[]{:S(2)}, u32[]{:S(2)}) collective-permute-start(bf16[1040,128]{1,0:T(8,128)(2,1)S(1)} %slice.17), channel_id=1, source_target_pairs={{0,14},{2,0},{4,2},{6,4},{8,6},{10,8},{12,10},{14,12},{1,15},{3,1}... | collective-permute-start | bytes 798728 | tf_op jit(solution)/shard_map/ppermute | solution.py:333
  70.3 10.6 %collective-permute-start.6 = (bf16[1024,128]{1,0:T(8,128)(2,1)S(1)}, bf16[1024,128]{1,0:T(8,128)(2,1)S(1)}, u32[]{:S(2)}, u32[]{:S(2)}) collective-permute-start(bf16[1024,128]{1,0:T(8,128)(2,1)S(1)} %slice.16), channel_id=1, source_target_pairs={{0,2},{2,4},{4,6},{6,8},{8,10},{10,12},{12,14},{14,0},{1,3},{3,5},... | collective-permute-start | bytes 786440 | tf_op jit(solution)/shard_map/ppermute | solution.py:333
  89.6 9.8 %collective-permute-start.18 = (bf16[1024,128]{1,0:T(8,128)(2,1)S(1)}, bf16[1024,128]{1,0:T(8,128)(2,1)S(1)}, u32[]{:S(2)}, u32[]{:S(2)}) collective-permute-start(bf16[1024,128]{1,0:T(8,128)(2,1)S(1)} %collective-permute-done.8.refs_6_), channel_id=1, source_target_pairs={{0,2},{2,4},{4,6},{6,8},{8,10},{10,12},{12,14},{14,0},{1,3},{3,5},... | collective-permute-start | bytes 786440 | tf_op jit(solution)/shard_map/ppermute | solution.py:333
  89.7 9.7 %collective-permute-start.20 = (bf16[1024,128]{1,0:T(8,128)(2,1)S(1)}, bf16[1024,128]{1,0:T(8,128)(2,1)S(1)}, u32[]{:S(2)}, u32[]{:S(2)}) collective-permute-start(bf16[1024,128]{1,0:T(8,128)(2,1)S(1)} %collective-permute-done.9.refs_7_), channel_id=1, source_target_pairs={{0,14},{2,0},{4,2},{6,4},{8,6},{10,8},{12,10},{14,12},{1,15},{3,1}... | collective-permute-start | bytes 786440 | tf_op jit(solution)/shard_map/ppermute | solution.py:333
  99.4 8.8 %collective-permute-start.19 = (bf16[1024,128]{1,0:T(8,128)(2,1)S(1)}, bf16[1024,128]{1,0:T(8,128)(2,1)S(1)}, u32[]{:S(2)}, u32[]{:S(2)}) collective-permute-start(bf16[1024,128]{1,0:T(8,128)(2,1)S(1)} %collective-permute-done.18.refs_8_), channel_id=1, source_target_pairs={{0,2},{2,4},{4,6},{6,8},{8,10},{10,12},{12,14},{14,0},{1,3},{3,5},... | collective-permute-start | bytes 786440 | tf_op jit(solution)/shard_map/ppermute | solution.py:333
  99.5 9.1 %collective-permute-start.21 = (bf16[1024,128]{1,0:T(8,128)(2,1)S(1)}, bf16[1024,128]{1,0:T(8,128)(2,1)S(1)}, u32[]{:S(2)}, u32[]{:S(2)}) collective-permute-start(bf16[1024,128]{1,0:T(8,128)(2,1)S(1)} %collective-permute-done.20.refs_9_), channel_id=1, source_target_pairs={{0,14},{2,0},{4,2},{6,4},{8,6},{10,8},{12,10},{14,12},{1,15},{3,1}... | collective-permute-start | bytes 786440 | tf_op jit(solution)/shard_map/ppermute | solution.py:333
  103.0 31.3 %collective-permute-start.27 = (s16[528,512]{1,0:T(8,128)(2,1)}, s16[528,512]{1,0:T(8,128)(2,1)S(1)}, u32[]{:S(2)}, u32[]{:S(2)}) collective-permute-start(s16[528,512]{1,0:T(8,128)(2,1)} %get-tuple-element.25), channel_id=1, source_target_pairs={{0,1},{16,17},{1,0},{17,16},{2,3},{18,19},{3,2},{19,18},{4,5},{20,... | collective-permute-start | bytes 1622024 | tf_op jit(solution)/shard_map/ppermute | solution.py:341
  105.5 30.8 %collective-permute-start.28 = (s16[528,512]{1,0:T(8,128)(2,1)}, s16[528,512]{1,0:T(8,128)(2,1)S(1)}, u32[]{:S(2)}, u32[]{:S(2)}) collective-permute-start(s16[528,512]{1,0:T(8,128)(2,1)} %get-tuple-element.33), channel_id=1, source_target_pairs={{0,16},{16,1},{1,17},{17,0},{2,18},{18,3},{3,19},{19,2},{4,20},{20... | collective-permute-start | bytes 1622024 | tf_op jit(solution)/shard_map/ppermute | solution.py:341
  105.5 30.8 %collective-permute-start.29 = (s16[528,512]{1,0:T(8,128)(2,1)}, s16[528,512]{1,0:T(8,128)(2,1)S(1)}, u32[]{:S(2)}, u32[]{:S(2)}) collective-permute-start(s16[528,512]{1,0:T(8,128)(2,1)} %get-tuple-element.34), channel_id=1, source_target_pairs={{0,17},{16,0},{1,16},{17,1},{2,19},{18,2},{3,18},{19,3},{4,21},{20... | collective-permute-start | bytes 1622024 | tf_op jit(solution)/shard_map/ppermute | solution.py:341
  108.3 14.0 %collective-permute-start.22 = (bf16[512,128]{1,0:T(8,128)(2,1)S(1)}, bf16[512,128]{1,0:T(8,128)(2,1)S(1)}, u32[]{:S(2)}, u32[]{:S(2)}) collective-permute-start(bf16[512,128]{1,0:T(8,128)(2,1)S(1)} %slice.18), channel_id=1, source_target_pairs={{0,2},{2,4},{4,6},{6,8},{8,10},{10,12},{12,14},{14,0},{1,3},{3,5},... | collective-permute-start | bytes 393224 | tf_op jit(solution)/shard_map/ppermute | solution.py:333
  108.6 13.7 %collective-permute-start.23 = (bf16[512,128]{1,0:T(8,128)(2,1)S(1)}, bf16[512,128]{1,0:T(8,128)(2,1)S(1)}, u32[]{:S(2)}, u32[]{:S(2)}) collective-permute-start(bf16[512,128]{1,0:T(8,128)(2,1)S(1)} %slice.19), channel_id=1, source_target_pairs={{0,14},{2,0},{4,2},{6,4},{8,6},{10,8},{12,10},{14,12},{1,15},{3,1}... | collective-permute-start | bytes 393224 | tf_op jit(solution)/shard_map/ppermute | solution.py:333
  131.6 13.2 %collective-permute-start.24 = (s16[528,512]{1,0:T(8,128)(2,1)}, s16[528,512]{1,0:T(8,128)(2,1)S(1)}, u32[]{:S(2)}, u32[]{:S(2)}) collective-permute-start(s16[528,512]{1,0:T(8,128)(2,1)} %get-tuple-element.29), channel_id=1, source_target_pairs={{0,1},{16,17},{1,0},{17,16},{2,3},{18,19},{3,2},{19,18},{4,5},{20,... | collective-permute-start | bytes 1622024 | tf_op jit(solution)/shard_map/ppermute | solution.py:341
  134.3 16.3 %collective-permute-start.25 = (s16[528,512]{1,0:T(8,128)(2,1)}, s16[528,512]{1,0:T(8,128)(2,1)S(1)}, u32[]{:S(2)}, u32[]{:S(2)}) collective-permute-start(s16[528,512]{1,0:T(8,128)(2,1)} %get-tuple-element.30), channel_id=1, source_target_pairs={{0,16},{16,1},{1,17},{17,0},{2,18},{18,3},{3,19},{19,2},{4,20},{20... | collective-permute-start | bytes 1622024 | tf_op jit(solution)/shard_map/ppermute | solution.py:341
  134.3 16.3 %collective-permute-start.26 = (s16[528,512]{1,0:T(8,128)(2,1)}, s16[528,512]{1,0:T(8,128)(2,1)S(1)}, u32[]{:S(2)}, u32[]{:S(2)}) collective-permute-start(s16[528,512]{1,0:T(8,128)(2,1)} %get-tuple-element.31), channel_id=1, source_target_pairs={{0,17},{16,0},{1,16},{17,1},{2,19},{18,2},{3,18},{19,3},{4,21},{20... | collective-permute-start | bytes 1622024 | tf_op jit(solution)/shard_map/ppermute | solution.py:341
  (22 other events, 264.2 us)

commit v2 on v1

v2 whole, which is shorter than its diff:
```python
import functools
import math

import jax
import jax.numpy as jnp
from jax import lax
from jax.experimental import pallas as pl
from jax.experimental.pallas import tpu as pltpu
from jax.sharding import Mesh
from jax.sharding import PartitionSpec as P

BLOCK = 128
KB = 4
CB = 8
RB = 8
SA = 24
SB = 6
HALF = RB // 2
META = 16
SPARE = 64
ROWS_A = SA * BLOCK + SPARE + META
ROWS_B = SB * BLOCK + META
OFFSETS = (0, -1, 1, -2, 2, -3, 3, 4)
HEIGHT = HALF * BLOCK
ROW = ("x", "core")
NEAR = (0, 1, 2)
NEXT = (3, 4)
FAR = (5, 6, 7)
STEPS = 64.0
TOP = 32760.0
LOWEST = -120.0
MIB = 1024 * 1024

HBM = pl.BlockSpec(memory_space=pltpu.HBM)
ANY = pl.BlockSpec(memory_space=pl.ANY)
SMEM = pl.BlockSpec(memory_space=pltpu.SMEM)
VMEM = pl.BlockSpec(memory_space=pltpu.VMEM)


def pack_kernel(a_pos, a_count, b_pos, b_count, a_vals, b_vals, pa, pb, place):
    lane = lax.broadcasted_iota(jnp.int32, (META, BLOCK), 1)
    for h in range(2):
        start = h * ROWS_B
        pb[start : start + SB * BLOCK, :] = b_vals[h * SB * BLOCK : (h + 1) * SB * BLOCK, :]
        words = jnp.zeros((META, BLOCK), jnp.int32)
        for s in range(SB):
            words = jnp.where(lane == s, b_pos[h, s], words)
        words = jnp.where(lane == SB, b_count[h], words)
        pb[start + SB * BLOCK : start + ROWS_B, :] = words.astype(jnp.float32).astype(jnp.bfloat16)
    pa[...] = jnp.zeros_like(pa)
    for p in range(KB * RB):
        place[p] = -1
    for s in range(SA):
        place[a_pos[s]] = jnp.where(s < a_count[0], s, -1)

    def send(p, carry):
        rank, low, words = carry
        slot = place[p]
        live = slot >= 0
        start = pl.ds(pl.multiple_of(jnp.maximum(slot, 0) * BLOCK, BLOCK), BLOCK)

        @pl.when(live)
        def _():
            pa[pl.ds(pl.multiple_of(rank * BLOCK, BLOCK), BLOCK), :] = a_vals[start, :]

        one = live.astype(jnp.int32)
        words = jnp.where((lane == rank) & live, p, words)
        return rank + one, low + jnp.where(p < HALF * KB, one, 0), words

    words = jnp.zeros((META, BLOCK), jnp.int32)
    total, low, words = lax.fori_loop(0, KB * RB, send, (jnp.int32(0), jnp.int32(0), words))
    words = jnp.where(lane == SA, low, words)
    words = jnp.where(lane == SA + 1, total, words)
    pa[ROWS_A - META :, :] = words.astype(jnp.float32).astype(jnp.bfloat16)


def pack(a_pos, a_count, b_pos, b_count, a_vals, b_vals):
    return pl.pallas_call(
        pack_kernel,
        out_shape=[
            jax.ShapeDtypeStruct((ROWS_A, BLOCK), jnp.bfloat16),
            jax.ShapeDtypeStruct((2 * ROWS_B, BLOCK), jnp.bfloat16),
        ],
        in_specs=[SMEM, SMEM, SMEM, SMEM, VMEM, VMEM],
        out_specs=[VMEM] * 2,
        scratch_shapes=[pltpu.SMEM((KB * RB,), jnp.int32)],
        name="pack",
    )(a_pos, a_count, b_pos, b_count, a_vals, b_vals)


def product_kernel(upper, panels, first, last, place, *refs):
    count = len(panels)
    refs = list(refs)
    density = {p: refs.pop(0) for p in panels}
    gram = {p: [refs.pop(0) for _ in range(1 if p < 7 else 2)] for p in panels}
    so_far = refs.pop(0) if upper else None
    acc_in = None if first else refs.pop(0)
    outs = [refs.pop(0) for _ in range(4 if last else 1)]
    a_buf, b_buf, dense, acc, meta, words, said = refs[:7]
    sem_a, sem_b, sem_am, sem_bm, sem_w = refs[7:]
    yl, yh, i, z = (place[k] for k in range(4))

    def a_copy(n, p):
        return pltpu.make_async_copy(density[p], a_buf.at[n], sem_a.at[n])

    def a_meta(n, p):
        return pltpu.make_async_copy(density[p].at[pl.ds(ROWS_A - META, META)], meta.at[n], sem_am.at[n])

    def gram_rows(p, group, start, rows):
        residue = lax.rem(i + z + OFFSETS[p] + 8, 8)
        stack = jnp.where(residue < i, 1 - yl, yl)
        start = (group * 2 * (2 - len(gram[p])) + stack) * ROWS_B + start
        return gram[p][group % len(gram[p])].at[pl.ds(pl.multiple_of(start, META), rows)]

    def b_meta(n, p, group):
        k = n * 2 + group
        return pltpu.make_async_copy(gram_rows(p, group, SB * BLOCK, META), meta.at[count + k], sem_bm.at[k])

    def b_copy(n, p, group):
        source = gram_rows(p, group, 0, SB * BLOCK)
        return pltpu.make_async_copy(source, b_buf.at[n, group], sem_b.at[n * 2 + group])

    for n, p in enumerate(panels):
        a_meta(n, p).start()
        for group in range(2):
            b_meta(n, p, group).start()
    if not first:
        acc_copy = pltpu.make_async_copy(acc_in, acc, sem_w.at[1])
        acc_copy.start()
    for n, p in enumerate(panels):
        a_copy(n, p).start()
        for group in range(2):
            b_copy(n, p, group).start()

    for n, p in enumerate(panels):
        a_meta(n, p).wait()
        for group in range(2):
            b_meta(n, p, group).wait()
    for k in range(3 * count):
        words[pl.ds(k, 1), :] = meta[k].astype(jnp.float32)[:1].astype(jnp.int32)
    to_scalars = pltpu.make_async_copy(words, said, sem_w.at[0])
    to_scalars.start()
    dense[...] = jnp.zeros_like(dense)
    if first:
        acc[...] = jnp.zeros_like(acc)
    to_scalars.wait()
    if not first:
        acc_copy.wait()

    blank = jnp.zeros((BLOCK, BLOCK), jnp.bfloat16)
    for n, p in enumerate(panels):
        a_copy(n, p).wait()
        for group in range(2):
            b_copy(n, p, group).wait()

        def put(s, carry, n=n):
            at = said[n, s]
            row = lax.shift_right_logical(at, 2) - (HALF if upper else 0)
            to = pl.multiple_of(row * BLOCK, BLOCK)
            start = pl.multiple_of(s * BLOCK, BLOCK)
            dense[n, lax.rem(at, KB), pl.ds(to, BLOCK), :] = a_buf[n, pl.ds(start, BLOCK), :]
            return carry

        low, total = said[n, SA], said[n, SA + 1]
        lax.fori_loop(*((low, total) if upper else (0, low)), put, 0)

        for s in range(SB):
            for group in range(2):
                k = count + 2 * n + group
                at = said[k, s]
                live = s < said[k, SB]
                right = jnp.where(live, b_buf[n, group, s * BLOCK : (s + 1) * BLOCK, :], blank)
                left = dense[n, lax.shift_right_logical(at, 3)]
                acc[group * CB + lax.rem(at, CB)] += jnp.dot(left, right, preferred_element_type=jnp.float32)

    if not last:
        out_copy = pltpu.make_async_copy(acc, outs[0], sem_w.at[2])
        out_copy.start()
        out_copy.wait()
        return
    own_out, q2_out, qp_out, qm_out = outs
    rows = pl.ds(HEIGHT if upper else 0, HEIGHT)
    own_copies = [
        pltpu.make_async_copy(acc.at[yh * (CB // 2) + c], own_out.at[rows, pl.ds(c * BLOCK, BLOCK)], sem_w.at[3 + c])
        for c in range(CB // 2)
    ]
    for copy in own_copies:
        copy.start()
    row = lax.broadcasted_iota(jnp.int32, (META, BLOCK), 0)
    for q_out, group, side in (
        (q2_out, 0, 1 - yh),
        (qp_out, 1, jnp.where(yl == 1, 1 - yh, yh)),
        (qm_out, 1, jnp.where(yl == 1, yh, 1 - yh)),
    ):
        for c in range(CB // 2):
            columns = slice(c * BLOCK, (c + 1) * BLOCK)
            codes = jnp.zeros((META, BLOCK), jnp.float32)
            for r in range(HALF):
                rows = slice(r * BLOCK, (r + 1) * BLOCK)
                value = acc[group * CB + side * (CB // 2) + c, rows, :]
                peak = jnp.max(jnp.max(jnp.abs(value), axis=0, keepdims=True), axis=1, keepdims=True)
                code = jnp.ceil(jnp.maximum(jnp.log2(peak), LOWEST) * STEPS)
                scaled = value * (TOP * jnp.exp2(code * (-1.0 / STEPS)))
                q_out[rows, columns] = jnp.round(scaled).astype(jnp.int32).astype(jnp.int16)
                codes = jnp.where(row == r, code, codes)
            q_out[HEIGHT:, columns] = codes.astype(jnp.int32).astype(jnp.int16)
    for copy in own_copies:
        copy.wait()


def product(upper, panels, place, density, gram, so_far, last, out=None):
    sent = jax.ShapeDtypeStruct((HEIGHT + META, CB // 2 * BLOCK), jnp.int16)
    count = len(panels)
    arrays = [density[p] for p in panels] + [one for p in panels for one in (gram[p : p + 1] if p < 7 else gram[7:9])]
    if upper:
        arrays.append(out)
    first = so_far is None
    if not first:
        arrays.append(so_far)
    if last:
        outs = [jax.ShapeDtypeStruct((RB * BLOCK, CB // 2 * BLOCK), jnp.float32), sent, sent, sent]
    else:
        outs = jax.ShapeDtypeStruct((2 * CB, HEIGHT, BLOCK), jnp.float32)
    return pl.pallas_call(
        functools.partial(product_kernel, upper, panels, first, last),
        out_shape=outs,
        in_specs=[SMEM] + [HBM] * (len(arrays) - (not first)) + [ANY] * (not first),
        out_specs=[HBM, VMEM, VMEM, VMEM] if last else ANY,
        input_output_aliases={len(arrays): 0} if upper else {},
        scratch_shapes=[
            pltpu.VMEM((count, ROWS_A, BLOCK), jnp.bfloat16),
            pltpu.VMEM((count, 2, SB * BLOCK, BLOCK), jnp.bfloat16),
            pltpu.VMEM((count, KB, HEIGHT, BLOCK), jnp.bfloat16),
            pltpu.VMEM((2 * CB, HEIGHT, BLOCK), jnp.float32),
            pltpu.VMEM((3 * count, META, BLOCK), jnp.bfloat16),
            pltpu.VMEM((24, BLOCK), jnp.int32),
            pltpu.SMEM((24, BLOCK), jnp.int32),
            pltpu.SemaphoreType.DMA((count,)),
            pltpu.SemaphoreType.DMA((2 * count,)),
            pltpu.SemaphoreType.DMA((count,)),
            pltpu.SemaphoreType.DMA((2 * count,)),
            pltpu.SemaphoreType.DMA((3 + CB // 2,)),
        ],
        compiler_params=pltpu.CompilerParams(vmem_limit_bytes=(8 + 2 * count) * MIB),
        cost_estimate=pl.CostEstimate(flops=1_000_000_000 * count, bytes_accessed=2_000_000 * count, transcendentals=0),
        name=("upper" if upper else "lower") + str(count) + ("_last" if last else ""),
    )(place, *arrays)


def sum_kernel(skip, *refs):
    parts, so_far, out, own, got, sem_part, sem_in, sem_out = refs[:3], *refs[3:]

    def part(k, r):
        rows = pl.ds(r * BLOCK, BLOCK if r < HALF else META)
        return pltpu.make_async_copy(parts[k].at[rows], got.at[k, rows], sem_part.at[k, r])

    def read(r):
        rows = pl.ds(r * BLOCK, BLOCK)
        return pltpu.make_async_copy(so_far.at[pl.ds((skip + r) * BLOCK, BLOCK)], own.at[rows], sem_in.at[r])

    def write(r):
        rows = pl.ds(r * BLOCK, BLOCK)
        return pltpu.make_async_copy(own.at[rows], out.at[pl.ds((skip + r) * BLOCK, BLOCK)], sem_out.at[r])

    for r in (HALF, *range(HALF)):
        for k in range(3):
            part(k, r).start()
        if r < HALF:
            read(r).start()
    scales = []
    for k in range(3):
        part(k, HALF).wait()
        codes = got[k, HEIGHT:, :].astype(jnp.int32).astype(jnp.float32)
        scales.append(jnp.exp2(codes * (1.0 / STEPS)) * (1.0 / TOP))
    for r in range(HALF):
        rows = pl.ds(r * BLOCK, BLOCK)
        read(r).wait()
        value = own[rows, :]
        for k in range(3):
            part(k, r).wait()
            value = value + got[k, rows, :].astype(jnp.int32).astype(jnp.float32) * scales[k][r : r + 1]
        own[rows, :] = value
        write(r).start()
    for r in range(HALF):
        write(r).wait()


def add_up(upper, parts, so_far):
    width = CB // 2 * BLOCK
    return pl.pallas_call(
        functools.partial(sum_kernel, HALF if upper else 0),
        out_shape=jax.ShapeDtypeStruct((RB * BLOCK, width), jnp.float32),
        in_specs=[ANY] * 3 + [HBM],
        out_specs=HBM,
        input_output_aliases={3: 0},
        scratch_shapes=[
            pltpu.VMEM((HEIGHT, width), jnp.float32),
            pltpu.VMEM((3, HEIGHT + META, width), jnp.int16),
            pltpu.SemaphoreType.DMA((3, HALF + 1)),
            pltpu.SemaphoreType.DMA((HALF,)),
            pltpu.SemaphoreType.DMA((HALF,)),
        ],
        name="add_up",
    )(*parts, so_far)


def shift(value, axis, distance):
    size = math.prod(lax.axis_size(one) for one in (axis if isinstance(axis, tuple) else (axis,)))
    return lax.ppermute(value, axis, [(k, (k + distance) % size) for k in range(size)])


def shift_y(value, distance):
    pairs = []
    for y in range(4):
        to = (y + distance) % 4
        pairs.append((y % 2 * 2 + y // 2, to % 2 * 2 + to // 2))
    return lax.ppermute(value, ("yl", "yh"), pairs)


def tie(*values):
    return lax.optimization_barrier(values)


def per_device(a_vals, a_pos, a_count, b_vals, b_pos, b_count):
    row = lax.axis_index(ROW)
    place = jnp.stack([lax.axis_index("yl"), lax.axis_index("yh"), row, lax.axis_index("z")]).astype(jnp.int32)
    pa, pb = pack(
        a_pos.reshape(SA),
        a_count.reshape(1),
        b_pos.reshape(2, SB),
        b_count.reshape(2),
        a_vals.reshape(SA * BLOCK, BLOCK),
        b_vals.reshape(2 * SB * BLOCK, BLOCK),
    )
    up1, down1, swapped, facing = tie(
        shift(pa, "z", 1), shift(pa, "z", -1), shift(pb, "yl", 1), shift(pb, ROW, 4)
    )
    both = jnp.concatenate([pb, swapped], axis=0)
    up2, down2, high1, low1, other_facing = tie(
        shift(up1, "z", 1),
        shift(down1, "z", -1),
        shift(both, ROW, 1),
        shift(both, ROW, -1),
        shift(facing, "yl", 1),
    )
    density = [pa, up1, down1, up2, down2]
    gram = [both, high1, low1]
    lower = product(False, NEAR, place, density, gram, None, False)
    high2, low2 = shift(high1, ROW, 1), shift(low1, ROW, -1)
    up3, down3, lower = tie(shift(up2, "z", 1), shift(down2, "z", -1), lower)
    gram += [high2, low2]
    size = lax.axis_size("z")
    pairs = [(c * size + k, c * size + (k + 1 - 2 * c) % size) for c in range(2) for k in range(size)]
    opposite = lax.ppermute(jnp.where(lax.axis_index("core") == 0, up3, down3), ("core", "z"), pairs)
    high3, low3 = shift(high2, ROW, 1), shift(low2, ROW, -1)
    lower = product(False, NEXT, place, density, gram, lower, False)
    opposite, high3, low3, lower = tie(opposite, high3, low3, lower)
    density += [up3, down3, opposite]
    gram += [high3, low3, facing, other_facing]

    def exchange(own, q2, qp, qm):
        return own, (shift_y(q2, 2), shift_y(qp, 1), shift_y(qm, -1)), q2

    out, parts1, done = exchange(*product(False, FAR, place, density, gram, lower, True))
    density[0], _ = tie(pa, done)
    out, parts2, _ = exchange(*product(True, NEAR + NEXT + FAR, place, density, gram, None, True, out))
    return add_up(True, parts2, add_up(False, parts1, out))


def solution(mesh):
    cores = 2
    x = mesh.shape["row"] // cores
    z = mesh.shape["col"] // 2
    split = Mesh(mesh.devices.reshape(x, cores, 2, z, mesh.shape["layer"]), ("x", "core", "yl", "z", "yh"))
    lead = (("x", "core"), ("yl", "z"), "yh")
    return jax.shard_map(
        per_device,
        mesh=split,
        in_specs=(P(*lead), P(*lead), P(*lead), P(*lead), P(*lead), P(*lead)),
        out_specs=P(("x", "core"), ("yl", "z", "yh")),
        check_vma=False,
    )
```

time: 156 us -> 150 us (0.962)
  starting transfers between devices: 46 us -> 31.3 us
  local copies, waits for them, and re-layouts: 5.93 us -> 15.9 us
  Pallas kernels: 47.1 us -> 43.7 us
    ppermute x24 -> x15, starting transfers between devices: 36.9 us -> 22.7 us  [shift(): lax.ppermute(value, axis, [(k, (k + distance) % size) for k in range(size)])]
    ppermute x6, waiting for transfers between devices: 9.35 us -> 21.7 us  [shift_y(): return lax.ppermute(value, ('yl', 'yh'), pairs)]
    ppermute x24 -> x15, waiting for transfers between devices: 46.1 us -> 34 us  [shift(): lax.ppermute(value, axis, [(k, (k + distance) % size) for k in range(size)])]
    unnamed x49 -> x55, local copies, waits for them, and re-layouts: 5.16 us -> 15.9 us
    pallas_call x3, Pallas kernels: 10.9 us -> 8.77 us  [the longest x2 5.86 us: add_up(): pl.pallas_call(functools.partial(sum_kernel, HALF if upper else 0), out_s...]
  transfers between devices with their start and end apart: 30 -> 22, of which waited for: 12 -> 13; matrix products, arithmetic and copies ran while one was open for 1% -> 1% of each run, Pallas kernels for 26% -> 20%
where the time goes in v2:
time: 150 us; the launch traced here: 148 us
  waiting for transfers between devices  56.3 us (38%)
  Pallas kernels  43.7 us (29%)
  starting transfers between devices  31.3 us (21%)
  local copies, waits for them, and re-layouts  15.9 us (11%)
    pallas_call x4, Pallas kernels, product(): pl.pallas_call(functools.partial(product_kernel, upper, panels, first, la...  34.9 us
    ppermute x15, waiting for transfers between devices, shift(): lax.ppermute(value, axis, [(k, (k + distance) % size) for k in range(size)])  34 us
    ppermute x15, starting transfers between devices, shift(): lax.ppermute(value, axis, [(k, (k + distance) % size) for k in range(size)])  22.7 us
    ppermute x6, waiting for transfers between devices, shift_y(): return lax.ppermute(value, ('yl', 'yh'), pairs)  21.7 us
    unnamed x55, local copies, waits for them, and re-layouts  15.9 us
    ppermute x6, starting transfers between devices, shift_y(): return lax.ppermute(value, ('yl', 'yh'), pairs)  8.55 us
    pallas_call x2, Pallas kernels, add_up(): pl.pallas_call(functools.partial(sum_kernel, HALF if upper else 0), out_s...  5.86 us
  transfers between devices with their start and end apart: 22, of which 13 were waited for; matrix products, arithmetic and copies ran while one was open for 1% of the time, Pallas kernels for 20%

profile of v2, /device:TPU:8, one launch (start us, length us, event | category | flops | bytes accessed | tf_op | source)
XLA Modules:
  0.0 148.4 jit_solution(3507427834519491440)
XLA Ops:
  0.7 2.9 %pack.1 = (bf16[3152,128]{1,0:T(8,128)(2,1)}, bf16[1568,128]{1,0:T(8,128)(2,1)}) custom-call(s32[24]{0:T(128)} %bitcast.14, s32[1]{0:T(128)} %bitcast.10.a_count, s32[2,6]{1,0:T(2,128)} %bitcast.13, s32[2]{0:T(128)} %bitcast.15, bf16[3072,128]{1,0:T(8,128)(2,1)} %bitcast.11, bf16[1536,128]{1,0:T(8,128)(2,1)} %bitcast.12), custom_call_target="tpu_custom_call" | custom-call | tf_op jit(solution)/shard_map/pack/pallas_call | solution.py:78
  3.6 5.9 %collective-permute-start.1 = (bf16[3152,128]{1,0:T(8,128)(2,1)}, bf16[3152,128]{1,0:T(8,128)(2,1)S(1)}, u32[]{:S(2)}, u32[]{:S(2)}) collective-permute-start(bf16[3152,128]{1,0:T(8,128)(2,1)} %get-tuple-element.51.refs_0_), channel_id=1, source_target_pairs={{0,14},{2,0},{4,2},{6,4},{8,6},{10,8},{12,10},{14,12},{1,15},{3,1}... | collective-permute-start | bytes 2420744 | tf_op jit(solution)/shard_map/ppermute | solution.py:309
  9.4 3.0 %collective-permute-start.3 = (bf16[1568,128]{1,0:T(8,128)(2,1)}, bf16[1568,128]{1,0:T(8,128)(2,1)S(1)}, u32[]{:S(2)}, u32[]{:S(2)}) collective-permute-start(bf16[1568,128]{1,0:T(8,128)(2,1)} %get-tuple-element.33), channel_id=1, source_target_pairs={{0,128},{32,160},{64,192},{96,224},{128,0},{160,32},{192,64},{224,... | collective-permute-start | bytes 1204232 | tf_op jit(solution)/shard_map/ppermute | solution.py:309
  13.9 7.9 %collective-permute-done.3.refs_5_.refs_15_ = bf16[1568,128]{1,0:T(8,128)(2,1)S(1)} collective-permute-done((bf16[1568,128]{1,0:T(8,128)(2,1)}, bf16[1568,128]{1,0:T(8,128)(2,1)S(1)}, u32[]{:S(2)}, u32[]{:S(2)}) %collective-permute-start.3) | collective-permute-done | bytes 401440 | tf_op jit(solution)/shard_map/ppermute | solution.py:309
  21.9 1.2 collective-permute-done.2
  23.1 3.9 %collective-permute-done.1.refs_2_ = bf16[3152,128]{1,0:T(8,128)(2,1)S(1)} collective-permute-done((bf16[3152,128]{1,0:T(8,128)(2,1)}, bf16[3152,128]{1,0:T(8,128)(2,1)S(1)}, u32[]{:S(2)}, u32[]{:S(2)}) %collective-permute-start.1) | collective-permute-done | bytes 806944 | tf_op jit(solution)/shard_map/ppermute | solution.py:309
  27.0 3.3 %collective-permute-done.refs_1_ = bf16[3152,128]{1,0:T(8,128)(2,1)S(1)} collective-permute-done((bf16[3152,128]{1,0:T(8,128)(2,1)}, bf16[3152,128]{1,0:T(8,128)(2,1)S(1)}, u32[]{:S(2)}, u32[]{:S(2)}) %collective-permute-start) | collective-permute-done | bytes 806944 | tf_op jit(solution)/shard_map/ppermute | solution.py:309
  31.2 3.2 %collective-permute-start.5 = (bf16[3152,128]{1,0:T(8,128)(2,1)S(1)}, bf16[3152,128]{1,0:T(8,128)(2,1)S(1)}, u32[]{:S(2)}, u32[]{:S(2)}) collective-permute-start(bf16[3152,128]{1,0:T(8,128)(2,1)S(1)} %collective-permute-done.1.refs_2_), channel_id=1, source_target_pairs={{0,14},{2,0},{4,2},{6,4},{8,6},{10,8},{12,10},{14,12},{1,15},{3,1}... | collective-permute-start | bytes 2420744 | tf_op jit(solution)/shard_map/ppermute | solution.py:309
  38.0 10.8 %collective-permute-done.8.refs_6_.refs_16_ = bf16[1568,128]{1,0:T(8,128)(2,1)S(1)} collective-permute-done((bf16[1568,128]{1,0:T(8,128)(2,1)S(1)}, bf16[1568,128]{1,0:T(8,128)(2,1)S(1)}, u32[]{:S(2)}, u32[]{:S(2)}) %collective-permute-start.8) | collective-permute-done | bytes 401440 | tf_op jit(solution)/shard_map/ppermute | solution.py:309
  50.7 3.2 %collective-permute-start.10 = (bf16[3152,128]{1,0:T(8,128)(2,1)S(1)}, bf16[3152,128]{1,0:T(8,128)(2,1)S(1)}, u32[]{:S(2)}, u32[]{:S(2)}) collective-permute-start(bf16[3152,128]{1,0:T(8,128)(2,1)S(1)} %collective-permute-done.5.refs_1_.refs_4_), channel_id=1, source_target_pairs={{0,14},{2,0},{4,2},{6,4},{8,6},{10,8},{12,10},{14,12},{1,15},{3,1}... | collective-permute-start | bytes 2420744 | tf_op jit(solution)/shard_map/ppermute | solution.py:309
  54.0 3.0 %collective-permute-start.14 = (bf16[3136,128]{1,0:T(8,128)(2,1)}, bf16[3136,128]{1,0:T(8,128)(2,1)S(1)}, u32[]{:S(2)}, u32[]{:S(2)}) collective-permute-start(bf16[3136,128]{1,0:T(8,128)(2,1)} %copy-done.11), channel_id=1, source_target_pairs={{0,224},{32,0},{64,32},{96,64},{128,96},{160,128},{192,160},{224,1... | collective-permute-start | bytes 2408456 | tf_op jit(solution)/shard_map/ppermute | solution.py:309
  57.0 1.1 copy-done.1
  58.1 1.1 copy-done.3
  59.2 1.1 copy-done.6
  60.4 1.1 copy-done.9
  63.8 6.5 %lower3.1.refs_4_ = f32[16,512,128]{2,1,0:T(8,128)S(1)} custom-call(s32[4]{0:T(128)S(1)} %pad_add_fusion.place, bf16[3152,128]{1,0:T(8,128)(2,1)S(1)} %copy-done.3, bf16[3152,128]{1,0:T(8,128)(2,1)S(1)} %copy-done.9, bf16[3152,128]{1,0:T(8,128)(2,1)S(1)} %copy-done.6, bf16[3136,128]{1,0:T(8,128)(2,1)S(1)} %copy-done.1, bf16[3136,128]{1,0:T(8,128)(2,1)S(1)} %copy-done.15, ...), custom_call_target="tpu_custom_call" | custom-call | flops 3000000000 | bytes 6000000 | tf_op jit(solution)/shard_map/lower3/pallas_call | solution.py:224
  70.3 1.6 %collective-permute-done.9.refs_0_.refs_5_ = bf16[3152,128]{1,0:T(8,128)(2,1)S(1)} collective-permute-done((bf16[3152,128]{1,0:T(8,128)(2,1)S(1)}, bf16[3152,128]{1,0:T(8,128)(2,1)S(1)}, u32[]{:S(2)}, u32[]{:S(2)}) %collective-permute-start.9) | collective-permute-done | bytes 806944 | tf_op jit(solution)/shard_map/ppermute | solution.py:309
  72.0 1.5 %collective-permute-start.13 = (bf16[3136,128]{1,0:T(8,128)(2,1)S(1)}, bf16[3136,128]{1,0:T(8,128)(2,1)S(1)}, u32[]{:S(2)}, u32[]{:S(2)}) collective-permute-start(bf16[3136,128]{1,0:T(8,128)(2,1)S(1)} %collective-permute-done.12.refs_2_.refs_11_), channel_id=1, source_target_pairs={{0,32},{32,64},{64,96},{96,128},{128,160},{160,192},{192,224},{224... | collective-permute-start | bytes 2408456 | tf_op jit(solution)/shard_map/ppermute | solution.py:309
  73.6 1.4 collective-permute-start.15
  75.0 5.0 %lower2.1.refs_7_ = f32[16,512,128]{2,1,0:T(8,128)S(1)} custom-call(s32[4]{0:T(128)S(1)} %pad_add_fusion.place, bf16[3152,128]{1,0:T(8,128)(2,1)S(1)} %collective-permute-done.4.refs_0_.refs_3_, bf16[3152,128]{1,0:T(8,128)(2,1)S(1)} %collective-permute-done.5.refs_1_.refs_4_, bf16[3136,128]{1,0:T(8,128)(2,1)S(1)} %collective-permute-done.12.refs_2_.refs_11_, ...), custom_call_target="tpu_custom_call" | custom-call | flops 2000000000 | bytes 4000000 | tf_op jit(solution)/shard_map/lower2/pallas_call | solution.py:224
  80.1 4.7 %collective-permute-done.13.refs_3_.refs_13_ = bf16[3136,128]{1,0:T(8,128)(2,1)S(1)} collective-permute-done((bf16[3136,128]{1,0:T(8,128)(2,1)S(1)}, bf16[3136,128]{1,0:T(8,128)(2,1)S(1)}, u32[]{:S(2)}, u32[]{:S(2)}) %collective-permute-start.13) | collective-permute-done | bytes 802848 | tf_op jit(solution)/shard_map/ppermute | solution.py:309
  85.4 7.4 %lower3_last.1 = (f32[1024,512]{1,0:T(8,128)}, s16[528,512]{1,0:T(8,128)(2,1)S(1)}, s16[528,512]{1,0:T(8,128)(2,1)S(1)}, s16[528,512]{1,0:T(8,128)(2,1)S(1)}) custom-call(s32[4]{0:T(128)S(1)} %pad_add_fusion.place, bf16[3152,128]{1,0:T(8,128)(2,1)S(1)} %collective-permute-done.9.refs_0_.refs_5_, ...), custom_call_target="tpu_custom_call" | custom-call | flops 3000000000 | bytes 6000000 | tf_op jit(solution)/shard_map/lower3_last/pallas_call | solution.py:224
  92.9 2.3 %collective-permute-start.19 = (s16[528,512]{1,0:T(8,128)(2,1)S(1)}, s16[528,512]{1,0:T(8,128)(2,1)S(1)}, u32[]{:S(2)}, u32[]{:S(2)}) collective-permute-start(s16[528,512]{1,0:T(8,128)(2,1)S(1)} %get-tuple-element.50), channel_id=1, source_target_pairs={{0,1},{16,17},{1,0},{17,16},{2,3},{18,19},{3,2},{19,18},{4,5},{20,... | collective-permute-start | bytes 1622024 | tf_op jit(solution)/shard_map/ppermute | solution.py:317
  95.2 2.0 %collective-permute-start.21 = (s16[528,512]{1,0:T(8,128)(2,1)S(1)}, s16[528,512]{1,0:T(8,128)(2,1)S(1)}, u32[]{:S(2)}, u32[]{:S(2)}) collective-permute-start(s16[528,512]{1,0:T(8,128)(2,1)S(1)} %get-tuple-element.57), channel_id=1, source_target_pairs={{0,17},{16,0},{1,16},{17,1},{2,19},{18,2},{3,18},{19,3},{4,21},{20... | collective-permute-start | bytes 1622024 | tf_op jit(solution)/shard_map/ppermute | solution.py:317
  97.2 16.0 %upper8_last.1 = (f32[1024,512]{1,0:T(8,128)}, s16[528,512]{1,0:T(8,128)(2,1)}, s16[528,512]{1,0:T(8,128)(2,1)}, s16[528,512]{1,0:T(8,128)(2,1)}) custom-call(s32[4]{0:T(128)S(1)} %pad_add_fusion.place, bf16[3152,128]{1,0:T(8,128)(2,1)S(1)} %copy-done.4, bf16[3152,128]{1,0:T(8,128)(2,1)S(1)} %copy-done.10, ...), custom_call_target="tpu_custom_call", output_to_operand_aliasing={{0}: (18, {})} | custom-call | flops 8000000000 | bytes 16000000 | tf_op jit(solution)/shard_map/upper8_last/pallas_call | solution.py:224
  113.2 1.3 collective-permute-start.16
  114.5 2.5 %collective-permute-start.17 = (s16[528,512]{1,0:T(8,128)(2,1)}, s16[528,512]{1,0:T(8,128)(2,1)S(1)}, u32[]{:S(2)}, u32[]{:S(2)}) collective-permute-start(s16[528,512]{1,0:T(8,128)(2,1)} %get-tuple-element.54), channel_id=1, source_target_pairs={{0,16},{16,1},{1,17},{17,0},{2,18},{18,3},{3,19},{19,2},{4,20},{20... | collective-permute-start | bytes 1622024 | tf_op jit(solution)/shard_map/ppermute | solution.py:317
  117.0 4.2 %collective-permute-done.20.refs_1_ = s16[528,512]{1,0:T(8,128)(2,1)S(1)} collective-permute-done((s16[528,512]{1,0:T(8,128)(2,1)S(1)}, s16[528,512]{1,0:T(8,128)(2,1)S(1)}, u32[]{:S(2)}, u32[]{:S(2)}) %collective-permute-start.20) | collective-permute-done | bytes 540704 | tf_op jit(solution)/shard_map/ppermute | solution.py:317
  123.2 2.9 %add_up.2.refs_3_ = f32[1024,512]{1,0:T(8,128)} custom-call(s16[528,512]{1,0:T(8,128)(2,1)} %copy-done.21, s16[528,512]{1,0:T(8,128)(2,1)} %copy-done.22, s16[528,512]{1,0:T(8,128)(2,1)} %copy-done.23, f32[1024,512]{1,0:T(8,128)} %get-tuple-element.58.refs_3_), custom_call_target="tpu_custom_call", output_to_operand_aliasing={{}: (3, {})} | custom-call | tf_op jit(solution)/shard_map/add_up/pallas_call | solution.py:290
  126.1 6.7 %collective-permute-done.16.refs_0_ = s16[528,512]{1,0:T(8,128)(2,1)S(1)} collective-permute-done((s16[528,512]{1,0:T(8,128)(2,1)}, s16[528,512]{1,0:T(8,128)(2,1)S(1)}, u32[]{:S(2)}, u32[]{:S(2)}) %collective-permute-start.16) | collective-permute-done | bytes 540704 | tf_op jit(solution)/shard_map/ppermute | solution.py:317
  132.9 10.8 %collective-permute-done.17.refs_1_ = s16[528,512]{1,0:T(8,128)(2,1)S(1)} collective-permute-done((s16[528,512]{1,0:T(8,128)(2,1)}, s16[528,512]{1,0:T(8,128)(2,1)S(1)}, u32[]{:S(2)}, u32[]{:S(2)}) %collective-permute-start.17) | collective-permute-done | bytes 540704 | tf_op jit(solution)/shard_map/ppermute | solution.py:317
  145.3 2.9 %add_up.3 = f32[1024,512]{1,0:T(8,128)} custom-call(s16[528,512]{1,0:T(8,128)(2,1)} %copy-done.24, s16[528,512]{1,0:T(8,128)(2,1)} %copy-done.25, s16[528,512]{1,0:T(8,128)(2,1)} %copy-done.26, f32[1024,512]{1,0:T(8,128)} %add_up.2.refs_3_), custom_call_target="tpu_custom_call", output_to_operand_aliasing={{}: (3, {})} | custom-call | tf_op jit(solution)/shard_map/add_up/pallas_call | solution.py:290
  (77 shorter events, 14.7 us)
Async XLA Ops:
  3.6 23.4 %collective-permute-start.1 = (bf16[3152,128]{1,0:T(8,128)(2,1)}, bf16[3152,128]{1,0:T(8,128)(2,1)S(1)}, u32[]{:S(2)}, u32[]{:S(2)}) collective-permute-start(bf16[3152,128]{1,0:T(8,128)(2,1)} %get-tuple-element.51.refs_0_), channel_id=1, source_target_pairs={{0,14},{2,0},{4,2},{6,4},{8,6},{10,8},{12,10},{14,12},{1,15},{3,1}... | collective-permute-start | bytes 2420744 | tf_op jit(solution)/shard_map/ppermute | solution.py:309
  9.4 20.8 %collective-permute-start = (bf16[3152,128]{1,0:T(8,128)(2,1)}, bf16[3152,128]{1,0:T(8,128)(2,1)S(1)}, u32[]{:S(2)}, u32[]{:S(2)}) collective-permute-start(bf16[3152,128]{1,0:T(8,128)(2,1)} %get-tuple-element.51.refs_0_), channel_id=1, source_target_pairs={{0,2},{2,4},{4,6},{6,8},{8,10},{10,12},{12,14},{14,0},{1,3},{3,5},... | collective-permute-start | bytes 2420744 | tf_op jit(solution)/shard_map/ppermute | solution.py:309
  9.4 12.4 %collective-permute-start.3 = (bf16[1568,128]{1,0:T(8,128)(2,1)}, bf16[1568,128]{1,0:T(8,128)(2,1)S(1)}, u32[]{:S(2)}, u32[]{:S(2)}) collective-permute-start(bf16[1568,128]{1,0:T(8,128)(2,1)} %get-tuple-element.33), channel_id=1, source_target_pairs={{0,128},{32,160},{64,192},{96,224},{128,0},{160,32},{192,64},{224,... | collective-permute-start | bytes 1204232 | tf_op jit(solution)/shard_map/ppermute | solution.py:309
  12.4 10.7 %collective-permute-start.2 = (bf16[1568,128]{1,0:T(8,128)(2,1)}, bf16[1568,128]{1,0:T(8,128)(2,1)S(1)}, u32[]{:S(2)}, u32[]{:S(2)}) collective-permute-start(bf16[1568,128]{1,0:T(8,128)(2,1)} %get-tuple-element.33), channel_id=1, source_target_pairs={{0,16},{16,0},{1,17},{17,1},{2,18},{18,2},{3,19},{19,3},{4,20},{20... | collective-permute-start | bytes 1204232 | tf_op jit(solution)/shard_map/ppermute | solution.py:309
  30.3 19.7 %collective-permute-start.4 = (bf16[3152,128]{1,0:T(8,128)(2,1)S(1)}, bf16[3152,128]{1,0:T(8,128)(2,1)S(1)}, u32[]{:S(2)}, u32[]{:S(2)}) collective-permute-start(bf16[3152,128]{1,0:T(8,128)(2,1)S(1)} %collective-permute-done.refs_1_), channel_id=1, source_target_pairs={{0,2},{2,4},{4,6},{6,8},{8,10},{10,12},{12,14},{14,0},{1,3},{3,5},... | collective-permute-start | bytes 2420744 | tf_op jit(solution)/shard_map/ppermute | solution.py:309
  31.2 19.0 %collective-permute-start.5 = (bf16[3152,128]{1,0:T(8,128)(2,1)S(1)}, bf16[3152,128]{1,0:T(8,128)(2,1)S(1)}, u32[]{:S(2)}, u32[]{:S(2)}) collective-permute-start(bf16[3152,128]{1,0:T(8,128)(2,1)S(1)} %collective-permute-done.1.refs_2_), channel_id=1, source_target_pairs={{0,14},{2,0},{4,2},{6,4},{8,6},{10,8},{12,10},{14,12},{1,15},{3,1}... | collective-permute-start | bytes 2420744 | tf_op jit(solution)/shard_map/ppermute | solution.py:309
  35.3 14.2 %collective-permute-start.7 = (bf16[3136,128]{1,0:T(8,128)(2,1)S(1)}, bf16[3136,128]{1,0:T(8,128)(2,1)S(1)}, u32[]{:S(2)}, u32[]{:S(2)}) collective-permute-start(bf16[3136,128]{1,0:T(8,128)(2,1)S(1)} %constant_dynamic-update-slice_fusion.refs_3_.refs_8_), channel_id=1, source_target_pairs={{0,224},{32,0},{64,32},{96,64},{128,96},{160,128},{192,160},{224,1... | collective-permute-start | bytes 2408456 | tf_op jit(solution)/shard_map/ppermute | solution.py:309
  35.8 13.7 %collective-permute-start.6 = (bf16[3136,128]{1,0:T(8,128)(2,1)S(1)}, bf16[3136,128]{1,0:T(8,128)(2,1)S(1)}, u32[]{:S(2)}, u32[]{:S(2)}) collective-permute-start(bf16[3136,128]{1,0:T(8,128)(2,1)S(1)} %constant_dynamic-update-slice_fusion.refs_3_.refs_8_), channel_id=1, source_target_pairs={{0,32},{32,64},{64,96},{96,128},{128,160},{160,192},{192,224},{224... | collective-permute-start | bytes 2408456 | tf_op jit(solution)/shard_map/ppermute | solution.py:309
  36.8 12.0 %collective-permute-start.8 = (bf16[1568,128]{1,0:T(8,128)(2,1)S(1)}, bf16[1568,128]{1,0:T(8,128)(2,1)S(1)}, u32[]{:S(2)}, u32[]{:S(2)}) collective-permute-start(bf16[1568,128]{1,0:T(8,128)(2,1)S(1)} %collective-permute-done.3.refs_5_.refs_15_), channel_id=1, source_target_pairs={{0,16},{16,0},{1,17},{17,1},{2,18},{18,2},{3,19},{19,3},{4,20},{20... | collective-permute-start | bytes 1204232 | tf_op jit(solution)/shard_map/ppermute | solution.py:309
  50.4 21.4 %collective-permute-start.9 = (bf16[3152,128]{1,0:T(8,128)(2,1)S(1)}, bf16[3152,128]{1,0:T(8,128)(2,1)S(1)}, u32[]{:S(2)}, u32[]{:S(2)}) collective-permute-start(bf16[3152,128]{1,0:T(8,128)(2,1)S(1)} %collective-permute-done.4.refs_0_.refs_3_), channel_id=1, source_target_pairs={{0,2},{2,4},{4,6},{6,8},{8,10},{10,12},{12,14},{14,0},{1,3},{3,5},... | collective-permute-start | bytes 2420744 | tf_op jit(solution)/shard_map/ppermute | solution.py:309
  50.7 21.1 %collective-permute-start.10 = (bf16[3152,128]{1,0:T(8,128)(2,1)S(1)}, bf16[3152,128]{1,0:T(8,128)(2,1)S(1)}, u32[]{:S(2)}, u32[]{:S(2)}) collective-permute-start(bf16[3152,128]{1,0:T(8,128)(2,1)S(1)} %collective-permute-done.5.refs_1_.refs_4_), channel_id=1, source_target_pairs={{0,14},{2,0},{4,2},{6,4},{8,6},{10,8},{12,10},{14,12},{1,15},{3,1}... | collective-permute-start | bytes 2420744 | tf_op jit(solution)/shard_map/ppermute | solution.py:309
  54.0 18.0 %collective-permute-start.12 = (bf16[3136,128]{1,0:T(8,128)(2,1)}, bf16[3136,128]{1,0:T(8,128)(2,1)S(1)}, u32[]{:S(2)}, u32[]{:S(2)}) collective-permute-start(bf16[3136,128]{1,0:T(8,128)(2,1)} %copy-done.14), channel_id=1, source_target_pairs={{0,32},{32,64},{64,96},{96,128},{128,160},{160,192},{192,224},{224... | collective-permute-start | bytes 2408456 | tf_op jit(solution)/shard_map/ppermute | solution.py:309
  54.0 19.6 %collective-permute-start.14 = (bf16[3136,128]{1,0:T(8,128)(2,1)}, bf16[3136,128]{1,0:T(8,128)(2,1)S(1)}, u32[]{:S(2)}, u32[]{:S(2)}) collective-permute-start(bf16[3136,128]{1,0:T(8,128)(2,1)} %copy-done.11), channel_id=1, source_target_pairs={{0,224},{32,0},{64,32},{96,64},{128,96},{160,128},{192,160},{224,1... | collective-permute-start | bytes 2408456 | tf_op jit(solution)/shard_map/ppermute | solution.py:309
  58.1 1.1 copy-start.3
  71.9 13.5 %copy-start.18 = (bf16[1568,128]{1,0:T(8,128)(2,1)S(1)}, bf16[1568,128]{1,0:T(8,128)(2,1)}, u32[]{:S(2)}) copy-start(bf16[1568,128]{1,0:T(8,128)(2,1)} %copy-done.17) | copy-start | bytes 1204228
  71.9 13.5 %copy-start.20 = (bf16[1568,128]{1,0:T(8,128)(2,1)S(1)}, bf16[1568,128]{1,0:T(8,128)(2,1)}, u32[]{:S(2)}) copy-start(bf16[1568,128]{1,0:T(8,128)(2,1)} %copy-done.19) | copy-start | bytes 1204228
  71.9 13.5 %collective-permute-start.11 = (bf16[3152,128]{1,0:T(8,128)(2,1)S(1)}, bf16[3152,128]{1,0:T(8,128)(2,1)S(1)}, u32[]{:S(2)}, u32[]{:S(2)}) collective-permute-start(bf16[3152,128]{1,0:T(8,128)(2,1)S(1)} %broadcast_select_fusion), channel_id=1, source_target_pairs={{0,2},{2,4},{4,6},{6,8},{8,10},{10,12},{12,14},{14,0},{32,46},{34,... | collective-permute-start | bytes 2420744 | tf_op jit(solution)/shard_map/ppermute | solution.py:354
  72.0 12.8 %collective-permute-start.13 = (bf16[3136,128]{1,0:T(8,128)(2,1)S(1)}, bf16[3136,128]{1,0:T(8,128)(2,1)S(1)}, u32[]{:S(2)}, u32[]{:S(2)}) collective-permute-start(bf16[3136,128]{1,0:T(8,128)(2,1)S(1)} %collective-permute-done.12.refs_2_.refs_11_), channel_id=1, source_target_pairs={{0,32},{32,64},{64,96},{96,128},{128,160},{160,192},{192,224},{224... | collective-permute-start | bytes 2408456 | tf_op jit(solution)/shard_map/ppermute | solution.py:309
  73.6 11.3 %collective-permute-start.15 = (bf16[3136,128]{1,0:T(8,128)(2,1)S(1)}, bf16[3136,128]{1,0:T(8,128)(2,1)S(1)}, u32[]{:S(2)}, u32[]{:S(2)}) collective-permute-start(bf16[3136,128]{1,0:T(8,128)(2,1)S(1)} %collective-permute-done.14.refs_3_.refs_12_), channel_id=1, source_target_pairs={{0,224},{32,0},{64,32},{96,64},{128,96},{160,128},{192,160},{224,1... | collective-permute-start | bytes 2408456 | tf_op jit(solution)/shard_map/ppermute | solution.py:309
  80.1 17.1 %copy-start.2 = (bf16[3136,128]{1,0:T(8,128)(2,1)S(1)}, bf16[3136,128]{1,0:T(8,128)(2,1)}, u32[]{:S(2)}) copy-start(bf16[3136,128]{1,0:T(8,128)(2,1)} %copy-done) | copy-start | bytes 2408452
  80.1 17.1 %copy-start.4 = (bf16[3152,128]{1,0:T(8,128)(2,1)S(1)}, bf16[3152,128]{1,0:T(8,128)(2,1)}, u32[]{:S(2)}) copy-start(bf16[3152,128]{1,0:T(8,128)(2,1)} %get-tuple-element.51.refs_0_) | copy-start | bytes 2420740
  80.1 17.1 %copy-start.7 = (bf16[3152,128]{1,0:T(8,128)(2,1)S(1)}, bf16[3152,128]{1,0:T(8,128)(2,1)}, u32[]{:S(2)}) copy-start(bf16[3152,128]{1,0:T(8,128)(2,1)} %copy-done.5) | copy-start | bytes 2420740
  80.1 17.1 %copy-start.10 = (bf16[3152,128]{1,0:T(8,128)(2,1)S(1)}, bf16[3152,128]{1,0:T(8,128)(2,1)}, u32[]{:S(2)}) copy-start(bf16[3152,128]{1,0:T(8,128)(2,1)} %copy-done.8) | copy-start | bytes 2420740
  80.1 17.1 %copy-start.13 = (bf16[3136,128]{1,0:T(8,128)(2,1)S(1)}, bf16[3136,128]{1,0:T(8,128)(2,1)}, u32[]{:S(2)}) copy-start(bf16[3136,128]{1,0:T(8,128)(2,1)} %copy-done.11) | copy-start | bytes 2408452
  80.1 17.1 %copy-start.16 = (bf16[3136,128]{1,0:T(8,128)(2,1)S(1)}, bf16[3136,128]{1,0:T(8,128)(2,1)}, u32[]{:S(2)}) copy-start(bf16[3136,128]{1,0:T(8,128)(2,1)} %copy-done.14) | copy-start | bytes 2408452
  92.9 28.7 %collective-permute-start.19 = (s16[528,512]{1,0:T(8,128)(2,1)S(1)}, s16[528,512]{1,0:T(8,128)(2,1)S(1)}, u32[]{:S(2)}, u32[]{:S(2)}) collective-permute-start(s16[528,512]{1,0:T(8,128)(2,1)S(1)} %get-tuple-element.50), channel_id=1, source_target_pairs={{0,1},{16,17},{1,0},{17,16},{2,3},{18,19},{3,2},{19,18},{4,5},{20,... | collective-permute-start | bytes 1622024 | tf_op jit(solution)/shard_map/ppermute | solution.py:317
  95.2 26.0 %collective-permute-start.20 = (s16[528,512]{1,0:T(8,128)(2,1)S(1)}, s16[528,512]{1,0:T(8,128)(2,1)S(1)}, u32[]{:S(2)}, u32[]{:S(2)}) collective-permute-start(s16[528,512]{1,0:T(8,128)(2,1)S(1)} %get-tuple-element.56), channel_id=1, source_target_pairs={{0,16},{16,1},{1,17},{17,0},{2,18},{18,3},{3,19},{19,2},{4,20},{20... | collective-permute-start | bytes 1622024 | tf_op jit(solution)/shard_map/ppermute | solution.py:317
  95.2 26.4 %collective-permute-start.21 = (s16[528,512]{1,0:T(8,128)(2,1)S(1)}, s16[528,512]{1,0:T(8,128)(2,1)S(1)}, u32[]{:S(2)}, u32[]{:S(2)}) collective-permute-start(s16[528,512]{1,0:T(8,128)(2,1)S(1)} %get-tuple-element.57), channel_id=1, source_target_pairs={{0,17},{16,0},{1,16},{17,1},{2,19},{18,2},{3,18},{19,3},{4,21},{20... | collective-permute-start | bytes 1622024 | tf_op jit(solution)/shard_map/ppermute | solution.py:317
  113.2 19.7 %collective-permute-start.16 = (s16[528,512]{1,0:T(8,128)(2,1)}, s16[528,512]{1,0:T(8,128)(2,1)S(1)}, u32[]{:S(2)}, u32[]{:S(2)}) collective-permute-start(s16[528,512]{1,0:T(8,128)(2,1)} %get-tuple-element.53), channel_id=1, source_target_pairs={{0,1},{16,17},{1,0},{17,16},{2,3},{18,19},{3,2},{19,18},{4,5},{20,... | collective-permute-start | bytes 1622024 | tf_op jit(solution)/shard_map/ppermute | solution.py:317
  114.5 29.2 %collective-permute-start.17 = (s16[528,512]{1,0:T(8,128)(2,1)}, s16[528,512]{1,0:T(8,128)(2,1)S(1)}, u32[]{:S(2)}, u32[]{:S(2)}) collective-permute-start(s16[528,512]{1,0:T(8,128)(2,1)} %get-tuple-element.54), channel_id=1, source_target_pairs={{0,16},{16,1},{1,17},{17,0},{2,18},{18,3},{3,19},{19,2},{4,20},{20... | collective-permute-start | bytes 1622024 | tf_op jit(solution)/shard_map/ppermute | solution.py:317
  121.2 22.5 %collective-permute-start.18 = (s16[528,512]{1,0:T(8,128)(2,1)}, s16[528,512]{1,0:T(8,128)(2,1)S(1)}, u32[]{:S(2)}, u32[]{:S(2)}) collective-permute-start(s16[528,512]{1,0:T(8,128)(2,1)} %get-tuple-element.55), channel_id=1, source_target_pairs={{0,17},{16,0},{1,16},{17,1},{2,19},{18,2},{3,18},{19,3},{4,21},{20... | collective-permute-start | bytes 1622024 | tf_op jit(solution)/shard_map/ppermute | solution.py:317
  132.9 10.8 %copy-start.24 = (s16[528,512]{1,0:T(8,128)(2,1)}, s16[528,512]{1,0:T(8,128)(2,1)S(1)}, u32[]{:S(2)}) copy-start(s16[528,512]{1,0:T(8,128)(2,1)S(1)} %collective-permute-done.16.refs_0_) | copy-start | bytes 1622020
  (17 other events, 15.9 us)

commit v3 on v2

--- a/solution.py
+++ b/solution.py
@@ -248,11 +248,7 @@
 
 
 def sum_kernel(skip, *refs):
-    parts, so_far, out, own, got, sem_part, sem_in, sem_out = refs[:3], *refs[3:]
-
-    def part(k, r):
-        rows = pl.ds(r * BLOCK, BLOCK if r < HALF else META)
-        return pltpu.make_async_copy(parts[k].at[rows], got.at[k, rows], sem_part.at[k, r])
+    parts, so_far, out, own, sem_in, sem_out = refs[:3], *refs[3:]
 
     def read(r):
         rows = pl.ds(r * BLOCK, BLOCK)
@@ -262,23 +258,18 @@
         rows = pl.ds(r * BLOCK, BLOCK)
         return pltpu.make_async_copy(own.at[rows], out.at[pl.ds((skip + r) * BLOCK, BLOCK)], sem_out.at[r])
 
-    for r in (HALF, *range(HALF)):
-        for k in range(3):
-            part(k, r).start()
-        if r < HALF:
-            read(r).start()
+    for r in range(HALF):
+        read(r).start()
     scales = []
     for k in range(3):
-        part(k, HALF).wait()
-        codes = got[k, HEIGHT:, :].astype(jnp.int32).astype(jnp.float32)
+        codes = parts[k][HEIGHT:, :].astype(jnp.int32).astype(jnp.float32)
         scales.append(jnp.exp2(codes * (1.0 / STEPS)) * (1.0 / TOP))
     for r in range(HALF):
         rows = pl.ds(r * BLOCK, BLOCK)
         read(r).wait()
         value = own[rows, :]
         for k in range(3):
-            part(k, r).wait()
-            value = value + got[k, rows, :].astype(jnp.int32).astype(jnp.float32) * scales[k][r : r + 1]
+            value = value + parts[k][rows, :].astype(jnp.int32).astype(jnp.float32) * scales[k][r : r + 1]
         own[rows, :] = value
         write(r).start()
     for r in range(HALF):
@@ -290,16 +281,15 @@
     return pl.pallas_call(
         functools.partial(sum_kernel, HALF if upper else 0),
         out_shape=jax.ShapeDtypeStruct((RB * BLOCK, width), jnp.float32),
-        in_specs=[ANY] * 3 + [HBM],
+        in_specs=[VMEM] * 3 + [HBM],
         out_specs=HBM,
         input_output_aliases={3: 0},
         scratch_shapes=[
             pltpu.VMEM((HEIGHT, width), jnp.float32),
-            pltpu.VMEM((3, HEIGHT + META, width), jnp.int16),
-            pltpu.SemaphoreType.DMA((3, HALF + 1)),
             pltpu.SemaphoreType.DMA((HALF,)),
             pltpu.SemaphoreType.DMA((HALF,)),
         ],
+        compiler_params=pltpu.CompilerParams(vmem_limit_bytes=6 * MIB),
         name="add_up",
     )(*parts, so_far)
 
@@ -332,17 +322,10 @@
         a_vals.reshape(SA * BLOCK, BLOCK),
         b_vals.reshape(2 * SB * BLOCK, BLOCK),
     )
-    up1, down1, swapped, facing = tie(
-        shift(pa, "z", 1), shift(pa, "z", -1), shift(pb, "yl", 1), shift(pb, ROW, 4)
-    )
-    both = jnp.concatenate([pb, swapped], axis=0)
-    up2, down2, high1, low1, other_facing = tie(
-        shift(up1, "z", 1),
-        shift(down1, "z", -1),
-        shift(both, ROW, 1),
-        shift(both, ROW, -1),
-        shift(facing, "yl", 1),
-    )
+    up1, down1, facing = tie(shift(pa, "z", 1), shift(pa, "z", -1), shift(pb, ROW, 4))
+    both = jnp.concatenate([pb, shift(pb, "yl", 1)], axis=0)
+    high1, low1 = shift(both, ROW, 1), shift(both, ROW, -1)
+    up2, down2, other_facing = tie(shift(up1, "z", 1), shift(down1, "z", -1), shift(facing, "yl", 1))
     density = [pa, up1, down1, up2, down2]
     gram = [both, high1, low1]
     lower = product(False, NEAR, place, density, gram, None, False)
@@ -354,7 +337,7 @@
     opposite = lax.ppermute(jnp.where(lax.axis_index("core") == 0, up3, down3), ("core", "z"), pairs)
     high3, low3 = shift(high2, ROW, 1), shift(low2, ROW, -1)
     lower = product(False, NEXT, place, density, gram, lower, False)
-    opposite, high3, low3, lower = tie(opposite, high3, low3, lower)
+    opposite, lower = tie(opposite, lower)
     density += [up3, down3, opposite]
     gram += [high3, low3, facing, other_facing]
 

time: 150 us -> 144 us (0.960)
  waiting for transfers between devices: 56.3 us -> 66.6 us
  local copies, waits for them, and re-layouts: 15.9 us -> 8.45 us
  Pallas kernels: 43.7 us -> 38.2 us
  starting transfers between devices: 31.3 us -> 28.1 us
    unnamed x55 -> x25, local copies, waits for them, and re-layouts: 15.9 us -> 7.66 us
    ppermute x1, waiting for transfers between devices: 0.58 us -> 6.91 us  [per_device(): lax.ppermute(jnp.where(lax.axis_index('core') == 0, up3, down3), ('core',...]
    ppermute x15, starting transfers between devices: 22.7 us -> 18.6 us  [shift(): lax.ppermute(value, axis, [(k, (k + distance) % size) for k in range(size)])]
    pallas_call x4, Pallas kernels: 34.9 us -> 31 us  [product(): pl.pallas_call(functools.partial(product_kernel, upper, panels, first, la...]
    ppermute x6, waiting for transfers between devices: 21.7 us -> 24.3 us  [shift_y(): return lax.ppermute(value, ('yl', 'yh'), pairs)]
    pallas_call x2, Pallas kernels: 5.86 us -> 4.31 us  [add_up(): pl.pallas_call(functools.partial(sum_kernel, HALF if upper else 0), out_s...]
  transfers between devices with their start and end apart: 22 -> 22, of which waited for: 13 -> 12; matrix products, arithmetic and copies ran while one was open for 1% -> 2% of each run, Pallas kernels for 20% -> 18%
where the time goes in v3:
time: 144 us; the launch traced here: 142 us
  waiting for transfers between devices  66.6 us (46%)
  Pallas kernels  38.2 us (27%)
  starting transfers between devices  28.1 us (20%)
  local copies, waits for them, and re-layouts  8.45 us (6%)
    ppermute x15, waiting for transfers between devices, shift(): lax.ppermute(value, axis, [(k, (k + distance) % size) for k in range(size)])  35.4 us
    pallas_call x4, Pallas kernels, product(): pl.pallas_call(functools.partial(product_kernel, upper, panels, first, la...  31 us
    ppermute x6, waiting for transfers between devices, shift_y(): return lax.ppermute(value, ('yl', 'yh'), pairs)  24.3 us
    ppermute x15, starting transfers between devices, shift(): lax.ppermute(value, axis, [(k, (k + distance) % size) for k in range(size)])  18.6 us
    ppermute x6, starting transfers between devices, shift_y(): return lax.ppermute(value, ('yl', 'yh'), pairs)  8.9 us
    unnamed x25, local copies, waits for them, and re-layouts  7.66 us
    ppermute x1, waiting for transfers between devices, per_device(): lax.ppermute(jnp.where(lax.axis_index('core') == 0, up3, down3), ('core',...  6.91 us
    pallas_call x2, Pallas kernels, add_up(): pl.pallas_call(functools.partial(sum_kernel, HALF if upper else 0), out_s...  4.31 us
  transfers between devices with their start and end apart: 22, of which 12 were waited for; matrix products, arithmetic and copies ran while one was open for 2% of the time, Pallas kernels for 18%

profile of v3, /device:TPU:8, one launch (start us, length us, event | category | flops | bytes accessed | tf_op | source)
XLA Modules:
  0.0 142.4 jit_solution(15780145803179070848)
XLA Ops:
  0.7 2.9 %pack.1 = (bf16[3152,128]{1,0:T(8,128)(2,1)}, bf16[1568,128]{1,0:T(8,128)(2,1)}) custom-call(s32[24]{0:T(128)} %bitcast.14, s32[1]{0:T(128)} %bitcast.10.a_count, s32[2,6]{1,0:T(2,128)} %bitcast.13, s32[2]{0:T(128)} %bitcast.15, bf16[3072,128]{1,0:T(8,128)(2,1)} %bitcast.11, bf16[1536,128]{1,0:T(8,128)(2,1)} %bitcast.12), custom_call_target="tpu_custom_call" | custom-call | tf_op jit(solution)/shard_map/pack/pallas_call | solution.py:78
  3.5 5.8 %collective-permute-start.1 = (bf16[3152,128]{1,0:T(8,128)(2,1)}, bf16[3152,128]{1,0:T(8,128)(2,1)S(1)}, u32[]{:S(2)}, u32[]{:S(2)}) collective-permute-start(bf16[3152,128]{1,0:T(8,128)(2,1)} %get-tuple-element.41.refs_0_), channel_id=1, source_target_pairs={{0,14},{2,0},{4,2},{6,4},{8,6},{10,8},{12,10},{14,12},{1,15},{3,1}... | collective-permute-start | bytes 2420744 | tf_op jit(solution)/shard_map/ppermute | solution.py:299
  9.4 3.0 %collective-permute-start.2 = (bf16[1568,128]{1,0:T(8,128)(2,1)}, bf16[1568,128]{1,0:T(8,128)(2,1)S(1)}, u32[]{:S(2)}, u32[]{:S(2)}) collective-permute-start(bf16[1568,128]{1,0:T(8,128)(2,1)} %get-tuple-element.28), channel_id=1, source_target_pairs={{0,128},{32,160},{64,192},{96,224},{128,0},{160,32},{192,64},{224,... | collective-permute-start | bytes 1204232 | tf_op jit(solution)/shard_map/ppermute | solution.py:299
  12.9 9.0 %collective-permute-done.2.refs_5_.refs_15_ = bf16[1568,128]{1,0:T(8,128)(2,1)S(1)} collective-permute-done((bf16[1568,128]{1,0:T(8,128)(2,1)}, bf16[1568,128]{1,0:T(8,128)(2,1)S(1)}, u32[]{:S(2)}, u32[]{:S(2)}) %collective-permute-start.2) | collective-permute-done | bytes 401440 | tf_op jit(solution)/shard_map/ppermute | solution.py:299
  21.8 5.1 %collective-permute-done.1.refs_2_ = bf16[3152,128]{1,0:T(8,128)(2,1)S(1)} collective-permute-done((bf16[3152,128]{1,0:T(8,128)(2,1)}, bf16[3152,128]{1,0:T(8,128)(2,1)S(1)}, u32[]{:S(2)}, u32[]{:S(2)}) %collective-permute-start.1) | collective-permute-done | bytes 806944 | tf_op jit(solution)/shard_map/ppermute | solution.py:299
  26.9 3.3 %collective-permute-done.refs_1_ = bf16[3152,128]{1,0:T(8,128)(2,1)S(1)} collective-permute-done((bf16[3152,128]{1,0:T(8,128)(2,1)}, bf16[3152,128]{1,0:T(8,128)(2,1)S(1)}, u32[]{:S(2)}, u32[]{:S(2)}) %collective-permute-start) | collective-permute-done | bytes 806944 | tf_op jit(solution)/shard_map/ppermute | solution.py:299
  30.2 0.9 copy-done.5
  31.2 3.2 %collective-permute-start.4 = (bf16[3152,128]{1,0:T(8,128)(2,1)S(1)}, bf16[3152,128]{1,0:T(8,128)(2,1)S(1)}, u32[]{:S(2)}, u32[]{:S(2)}) collective-permute-start(bf16[3152,128]{1,0:T(8,128)(2,1)S(1)} %collective-permute-done.1.refs_2_), channel_id=1, source_target_pairs={{0,14},{2,0},{4,2},{6,4},{8,6},{10,8},{12,10},{14,12},{1,15},{3,1}... | collective-permute-start | bytes 2420744 | tf_op jit(solution)/shard_map/ppermute | solution.py:299
  34.4 1.8 %constant_dynamic-update-slice_fusion.1 = bf16[3136,128]{1,0:T(8,128)(2,1)} fusion(bf16[1568,128]{1,0:T(8,128)(2,1)} %get-tuple-element.28), kind=kLoop, calls=%fused_computation.2 | loop fusion | bytes 802816
  37.4 0.8 constant_dynamic-update-slice_fusion.refs_3_.refs_8_
  38.7 6.7 %collective-permute-done.5.refs_6_.refs_16_ = bf16[1568,128]{1,0:T(8,128)(2,1)S(1)} collective-permute-done((bf16[1568,128]{1,0:T(8,128)(2,1)S(1)}, bf16[1568,128]{1,0:T(8,128)(2,1)S(1)}, u32[]{:S(2)}, u32[]{:S(2)}) %collective-permute-start.5) | collective-permute-done | bytes 401440 | tf_op jit(solution)/shard_map/ppermute | solution.py:299
  46.2 3.8 %collective-permute-done.3.refs_0_.refs_3_ = bf16[3152,128]{1,0:T(8,128)(2,1)S(1)} collective-permute-done((bf16[3152,128]{1,0:T(8,128)(2,1)S(1)}, bf16[3152,128]{1,0:T(8,128)(2,1)S(1)}, u32[]{:S(2)}, u32[]{:S(2)}) %collective-permute-start.3) | collective-permute-done | bytes 806944 | tf_op jit(solution)/shard_map/ppermute | solution.py:299
  50.2 3.7 %collective-permute-start.7 = (bf16[3152,128]{1,0:T(8,128)(2,1)S(1)}, bf16[3152,128]{1,0:T(8,128)(2,1)S(1)}, u32[]{:S(2)}, u32[]{:S(2)}) collective-permute-start(bf16[3152,128]{1,0:T(8,128)(2,1)S(1)} %collective-permute-done.4.refs_1_.refs_4_), channel_id=1, source_target_pairs={{0,14},{2,0},{4,2},{6,4},{8,6},{10,8},{12,10},{14,12},{1,15},{3,1}... | collective-permute-start | bytes 2420744 | tf_op jit(solution)/shard_map/ppermute | solution.py:299
  54.5 1.1 copy-done
  55.6 1.1 copy-done.3
  56.7 1.1 copy-done.6
  57.9 5.1 %lower3.1.refs_4_ = f32[16,512,128]{2,1,0:T(8,128)S(1)} custom-call(s32[4]{0:T(128)S(1)} %pad_add_fusion.place, bf16[3152,128]{1,0:T(8,128)(2,1)S(1)} %copy-done, bf16[3152,128]{1,0:T(8,128)(2,1)S(1)} %copy-done.6, bf16[3152,128]{1,0:T(8,128)(2,1)S(1)} %copy-done.3, bf16[3136,128]{1,0:T(8,128)(2,1)} %constant_dynamic-update-slice_fusion.refs_3_.refs_8_, ...), custom_call_target="tpu_custom_call" | custom-call | flops 3000000000 | bytes 6000000 | tf_op jit(solution)/shard_map/lower3/pallas_call | solution.py:224
  63.0 6.5 %collective-permute-done.6.refs_0_.refs_5_ = bf16[3152,128]{1,0:T(8,128)(2,1)S(1)} collective-permute-done((bf16[3152,128]{1,0:T(8,128)(2,1)S(1)}, bf16[3152,128]{1,0:T(8,128)(2,1)S(1)}, u32[]{:S(2)}, u32[]{:S(2)}) %collective-permute-start.6) | collective-permute-done | bytes 806944 | tf_op jit(solution)/shard_map/ppermute | solution.py:299
  70.3 0.9 collective-permute-start.15
  71.2 5.1 %lower2.1.refs_7_ = f32[16,512,128]{2,1,0:T(8,128)S(1)} custom-call(s32[4]{0:T(128)S(1)} %pad_add_fusion.place, bf16[3152,128]{1,0:T(8,128)(2,1)S(1)} %collective-permute-done.3.refs_0_.refs_3_, bf16[3152,128]{1,0:T(8,128)(2,1)S(1)} %collective-permute-done.4.refs_1_.refs_4_, bf16[3136,128]{1,0:T(8,128)(2,1)S(1)} %collective-permute-done.12.refs_2_.refs_11_, ...), custom_call_target="tpu_custom_call" | custom-call | flops 2000000000 | bytes 4000000 | tf_op jit(solution)/shard_map/lower2/pallas_call | solution.py:224
  76.3 6.9 %collective-permute-done.11.refs_2_.refs_7_ = bf16[3152,128]{1,0:T(8,128)(2,1)S(1)} collective-permute-done((bf16[3152,128]{1,0:T(8,128)(2,1)S(1)}, bf16[3152,128]{1,0:T(8,128)(2,1)S(1)}, u32[]{:S(2)}, u32[]{:S(2)}) %collective-permute-start.11) | collective-permute-done | bytes 806944 | tf_op jit(solution)/shard_map/ppermute | solution.py:337
  84.0 7.4 %lower3_last.1 = (f32[1024,512]{1,0:T(8,128)}, s16[528,512]{1,0:T(8,128)(2,1)S(1)}, s16[528,512]{1,0:T(8,128)(2,1)S(1)}, s16[528,512]{1,0:T(8,128)(2,1)S(1)}) custom-call(s32[4]{0:T(128)S(1)} %pad_add_fusion.place, bf16[3152,128]{1,0:T(8,128)(2,1)S(1)} %collective-permute-done.6.refs_0_.refs_5_, ...), custom_call_target="tpu_custom_call" | custom-call | flops 3000000000 | bytes 6000000 | tf_op jit(solution)/shard_map/lower3_last/pallas_call | solution.py:224
  91.4 2.4 %collective-permute-start.19 = (s16[528,512]{1,0:T(8,128)(2,1)S(1)}, s16[528,512]{1,0:T(8,128)(2,1)S(1)}, u32[]{:S(2)}, u32[]{:S(2)}) collective-permute-start(s16[528,512]{1,0:T(8,128)(2,1)S(1)} %get-tuple-element.40), channel_id=1, source_target_pairs={{0,1},{16,17},{1,0},{17,16},{2,3},{18,19},{3,2},{19,18},{4,5},{20,... | collective-permute-start | bytes 1622024 | tf_op jit(solution)/shard_map/ppermute | solution.py:307
  93.8 2.0 %collective-permute-start.21 = (s16[528,512]{1,0:T(8,128)(2,1)S(1)}, s16[528,512]{1,0:T(8,128)(2,1)S(1)}, u32[]{:S(2)}, u32[]{:S(2)}) collective-permute-start(s16[528,512]{1,0:T(8,128)(2,1)S(1)} %get-tuple-element.47), channel_id=1, source_target_pairs={{0,17},{16,0},{1,16},{17,1},{2,19},{18,2},{3,18},{19,3},{4,21},{20... | collective-permute-start | bytes 1622024 | tf_op jit(solution)/shard_map/ppermute | solution.py:307
  95.8 13.4 %upper8_last.1 = (f32[1024,512]{1,0:T(8,128)}, s16[528,512]{1,0:T(8,128)(2,1)S(1)}, s16[528,512]{1,0:T(8,128)(2,1)S(1)}, s16[528,512]{1,0:T(8,128)(2,1)S(1)}) custom-call(s32[4]{0:T(128)S(1)} %pad_add_fusion.place, bf16[3152,128]{1,0:T(8,128)(2,1)S(1)} %copy-done.1, bf16[3152,128]{1,0:T(8,128)(2,1)S(1)} %copy-done.7, ...), custom_call_target="tpu_custom_call", output_to_operand_aliasing={{0}: (18, {})} | custom-call | flops 8000000000 | bytes 16000000 | tf_op jit(solution)/shard_map/upper8_last/pallas_call | solution.py:224
  109.2 1.5 %collective-permute-start.16 = (s16[528,512]{1,0:T(8,128)(2,1)S(1)}, s16[528,512]{1,0:T(8,128)(2,1)S(1)}, u32[]{:S(2)}, u32[]{:S(2)}) collective-permute-start(s16[528,512]{1,0:T(8,128)(2,1)S(1)} %get-tuple-element.43), channel_id=1, source_target_pairs={{0,1},{16,17},{1,0},{17,16},{2,3},{18,19},{3,2},{19,18},{4,5},{20,... | collective-permute-start | bytes 1622024 | tf_op jit(solution)/shard_map/ppermute | solution.py:307
  110.7 2.5 %collective-permute-start.17 = (s16[528,512]{1,0:T(8,128)(2,1)S(1)}, s16[528,512]{1,0:T(8,128)(2,1)S(1)}, u32[]{:S(2)}, u32[]{:S(2)}) collective-permute-start(s16[528,512]{1,0:T(8,128)(2,1)S(1)} %get-tuple-element.44), channel_id=1, source_target_pairs={{0,16},{16,1},{1,17},{17,0},{2,18},{18,3},{3,19},{19,2},{4,20},{20... | collective-permute-start | bytes 1622024 | tf_op jit(solution)/shard_map/ppermute | solution.py:307
  113.3 6.7 %collective-permute-done.20.refs_1_ = s16[528,512]{1,0:T(8,128)(2,1)S(1)} collective-permute-done((s16[528,512]{1,0:T(8,128)(2,1)S(1)}, s16[528,512]{1,0:T(8,128)(2,1)S(1)}, u32[]{:S(2)}, u32[]{:S(2)}) %collective-permute-start.20) | collective-permute-done | bytes 540704 | tf_op jit(solution)/shard_map/ppermute | solution.py:307
  120.3 2.2 %add_up.2.refs_3_ = f32[1024,512]{1,0:T(8,128)} custom-call(s16[528,512]{1,0:T(8,128)(2,1)S(1)} %collective-permute-done.19.refs_0_, s16[528,512]{1,0:T(8,128)(2,1)S(1)} %collective-permute-done.20.refs_1_, s16[528,512]{1,0:T(8,128)(2,1)S(1)} %collective-permute-done.21.refs_2_, f32[1024,512]{1,0:T(8,128)} %get-tuple-element.48.refs_3_), custom_call_target="tpu_custom_call", output_to_operand_aliasing={{}: (3, {})} | custom-call | tf_op jit(solution)/shard_map/add_up/pallas_call | solution.py:281
  122.5 8.9 %collective-permute-done.16.refs_0_ = s16[528,512]{1,0:T(8,128)(2,1)S(1)} collective-permute-done((s16[528,512]{1,0:T(8,128)(2,1)S(1)}, s16[528,512]{1,0:T(8,128)(2,1)S(1)}, u32[]{:S(2)}, u32[]{:S(2)}) %collective-permute-start.16) | collective-permute-done | bytes 540704 | tf_op jit(solution)/shard_map/ppermute | solution.py:307
  131.4 8.7 %collective-permute-done.17.refs_1_ = s16[528,512]{1,0:T(8,128)(2,1)S(1)} collective-permute-done((s16[528,512]{1,0:T(8,128)(2,1)S(1)}, s16[528,512]{1,0:T(8,128)(2,1)S(1)}, u32[]{:S(2)}, u32[]{:S(2)}) %collective-permute-start.17) | collective-permute-done | bytes 540704 | tf_op jit(solution)/shard_map/ppermute | solution.py:307
  140.1 2.2 %add_up.3 = f32[1024,512]{1,0:T(8,128)} custom-call(s16[528,512]{1,0:T(8,128)(2,1)S(1)} %collective-permute-done.16.refs_0_, s16[528,512]{1,0:T(8,128)(2,1)S(1)} %collective-permute-done.17.refs_1_, s16[528,512]{1,0:T(8,128)(2,1)S(1)} %collective-permute-done.18.refs_2_, f32[1024,512]{1,0:T(8,128)} %add_up.2.refs_3_), custom_call_target="tpu_custom_call", output_to_operand_aliasing={{}: (3, {})} | custom-call | tf_op jit(solution)/shard_map/add_up/pallas_call | solution.py:281
  (47 shorter events, 5.6 us)
Async XLA Ops:
  3.5 23.4 %collective-permute-start.1 = (bf16[3152,128]{1,0:T(8,128)(2,1)}, bf16[3152,128]{1,0:T(8,128)(2,1)S(1)}, u32[]{:S(2)}, u32[]{:S(2)}) collective-permute-start(bf16[3152,128]{1,0:T(8,128)(2,1)} %get-tuple-element.41.refs_0_), channel_id=1, source_target_pairs={{0,14},{2,0},{4,2},{6,4},{8,6},{10,8},{12,10},{14,12},{1,15},{3,1}... | collective-permute-start | bytes 2420744 | tf_op jit(solution)/shard_map/ppermute | solution.py:299
  9.4 20.9 %collective-permute-start = (bf16[3152,128]{1,0:T(8,128)(2,1)}, bf16[3152,128]{1,0:T(8,128)(2,1)S(1)}, u32[]{:S(2)}, u32[]{:S(2)}) collective-permute-start(bf16[3152,128]{1,0:T(8,128)(2,1)} %get-tuple-element.41.refs_0_), channel_id=1, source_target_pairs={{0,2},{2,4},{4,6},{6,8},{8,10},{10,12},{12,14},{14,0},{1,3},{3,5},... | collective-permute-start | bytes 2420744 | tf_op jit(solution)/shard_map/ppermute | solution.py:299
  9.4 12.5 %collective-permute-start.2 = (bf16[1568,128]{1,0:T(8,128)(2,1)}, bf16[1568,128]{1,0:T(8,128)(2,1)S(1)}, u32[]{:S(2)}, u32[]{:S(2)}) collective-permute-start(bf16[1568,128]{1,0:T(8,128)(2,1)} %get-tuple-element.28), channel_id=1, source_target_pairs={{0,128},{32,160},{64,192},{96,224},{128,0},{160,32},{192,64},{224,... | collective-permute-start | bytes 1204232 | tf_op jit(solution)/shard_map/ppermute | solution.py:299
  12.4 25.0 %collective-permute-start.8 = (bf16[1568,128]{1,0:T(8,128)(2,1)}, bf16[1568,128]{1,0:T(8,128)(2,1)S(1)}, u32[]{:S(2)}, u32[]{:S(2)}) collective-permute-start(bf16[1568,128]{1,0:T(8,128)(2,1)} %get-tuple-element.28), channel_id=1, source_target_pairs={{0,16},{16,0},{1,17},{17,1},{2,18},{18,2},{3,19},{19,3},{4,20},{20... | collective-permute-start | bytes 1204232 | tf_op jit(solution)/shard_map/ppermute | solution.py:299
  26.9 23.2 %copy-start.2 = (bf16[3152,128]{1,0:T(8,128)(2,1)}, bf16[3152,128]{1,0:T(8,128)(2,1)S(1)}, u32[]{:S(2)}) copy-start(bf16[3152,128]{1,0:T(8,128)(2,1)S(1)} %collective-permute-done.1.refs_2_) | copy-start | bytes 2420740
  30.2 19.7 %collective-permute-start.3 = (bf16[3152,128]{1,0:T(8,128)(2,1)S(1)}, bf16[3152,128]{1,0:T(8,128)(2,1)S(1)}, u32[]{:S(2)}, u32[]{:S(2)}) collective-permute-start(bf16[3152,128]{1,0:T(8,128)(2,1)S(1)} %collective-permute-done.refs_1_), channel_id=1, source_target_pairs={{0,2},{2,4},{4,6},{6,8},{8,10},{10,12},{12,14},{14,0},{1,3},{3,5},... | collective-permute-start | bytes 2420744 | tf_op jit(solution)/shard_map/ppermute | solution.py:299
  30.2 0.9 copy-start.5
  31.2 19.0 %collective-permute-start.4 = (bf16[3152,128]{1,0:T(8,128)(2,1)S(1)}, bf16[3152,128]{1,0:T(8,128)(2,1)S(1)}, u32[]{:S(2)}, u32[]{:S(2)}) collective-permute-start(bf16[3152,128]{1,0:T(8,128)(2,1)S(1)} %collective-permute-done.1.refs_2_), channel_id=1, source_target_pairs={{0,14},{2,0},{4,2},{6,4},{8,6},{10,8},{12,10},{14,12},{1,15},{3,1}... | collective-permute-start | bytes 2420744 | tf_op jit(solution)/shard_map/ppermute | solution.py:299
  36.2 9.3 %collective-permute-start.5 = (bf16[1568,128]{1,0:T(8,128)(2,1)S(1)}, bf16[1568,128]{1,0:T(8,128)(2,1)S(1)}, u32[]{:S(2)}, u32[]{:S(2)}) collective-permute-start(bf16[1568,128]{1,0:T(8,128)(2,1)S(1)} %collective-permute-done.2.refs_5_.refs_15_), channel_id=1, source_target_pairs={{0,16},{16,0},{1,17},{17,1},{2,18},{18,2},{3,19},{19,3},{4,20},{20... | collective-permute-start | bytes 1204232 | tf_op jit(solution)/shard_map/ppermute | solution.py:299
  38.2 15.7 %collective-permute-start.10 = (bf16[3136,128]{1,0:T(8,128)(2,1)}, bf16[3136,128]{1,0:T(8,128)(2,1)}, u32[]{:S(2)}, u32[]{:S(2)}) collective-permute-start(bf16[3136,128]{1,0:T(8,128)(2,1)} %constant_dynamic-update-slice_fusion.refs_3_.refs_8_), channel_id=1, source_target_pairs={{0,224},{32,0},{64,32},{96,64},{128,96},{160,128},{192,160},{224,1... | collective-permute-start | bytes 2408456 | tf_op jit(solution)/shard_map/ppermute | solution.py:299
  38.4 15.6 %collective-permute-start.9 = (bf16[3136,128]{1,0:T(8,128)(2,1)}, bf16[3136,128]{1,0:T(8,128)(2,1)}, u32[]{:S(2)}, u32[]{:S(2)}) collective-permute-start(bf16[3136,128]{1,0:T(8,128)(2,1)} %constant_dynamic-update-slice_fusion.refs_3_.refs_8_), channel_id=1, source_target_pairs={{0,32},{32,64},{64,96},{96,128},{128,160},{160,192},{192,224},{224... | collective-permute-start | bytes 2408456 | tf_op jit(solution)/shard_map/ppermute | solution.py:299
  50.2 19.4 %collective-permute-start.6 = (bf16[3152,128]{1,0:T(8,128)(2,1)S(1)}, bf16[3152,128]{1,0:T(8,128)(2,1)S(1)}, u32[]{:S(2)}, u32[]{:S(2)}) collective-permute-start(bf16[3152,128]{1,0:T(8,128)(2,1)S(1)} %collective-permute-done.3.refs_0_.refs_3_), channel_id=1, source_target_pairs={{0,2},{2,4},{4,6},{6,8},{8,10},{10,12},{12,14},{14,0},{1,3},{3,5},... | collective-permute-start | bytes 2420744 | tf_op jit(solution)/shard_map/ppermute | solution.py:299
  50.2 19.4 %collective-permute-start.7 = (bf16[3152,128]{1,0:T(8,128)(2,1)S(1)}, bf16[3152,128]{1,0:T(8,128)(2,1)S(1)}, u32[]{:S(2)}, u32[]{:S(2)}) collective-permute-start(bf16[3152,128]{1,0:T(8,128)(2,1)S(1)} %collective-permute-done.4.refs_1_.refs_4_), channel_id=1, source_target_pairs={{0,14},{2,0},{4,2},{6,4},{8,6},{10,8},{12,10},{14,12},{1,15},{3,1}... | collective-permute-start | bytes 2420744 | tf_op jit(solution)/shard_map/ppermute | solution.py:299
  53.9 16.3 %collective-permute-start.13 = (bf16[3136,128]{1,0:T(8,128)(2,1)}, bf16[3136,128]{1,0:T(8,128)(2,1)S(1)}, u32[]{:S(2)}, u32[]{:S(2)}) collective-permute-start(bf16[3136,128]{1,0:T(8,128)(2,1)} %collective-permute-done.10.refs_5_.refs_10_), channel_id=1, source_target_pairs={{0,224},{32,0},{64,32},{96,64},{128,96},{160,128},{192,160},{224,1... | collective-permute-start | bytes 2408456 | tf_op jit(solution)/shard_map/ppermute | solution.py:299
  53.9 17.2 %collective-permute-start.12 = (bf16[3136,128]{1,0:T(8,128)(2,1)}, bf16[3136,128]{1,0:T(8,128)(2,1)S(1)}, u32[]{:S(2)}, u32[]{:S(2)}) collective-permute-start(bf16[3136,128]{1,0:T(8,128)(2,1)} %collective-permute-done.9.refs_4_.refs_9_), channel_id=1, source_target_pairs={{0,32},{32,64},{64,96},{96,128},{128,160},{160,192},{192,224},{224... | collective-permute-start | bytes 2408456 | tf_op jit(solution)/shard_map/ppermute | solution.py:299
  54.5 1.1 copy-start
  55.6 1.1 copy-start.3
  56.7 1.1 copy-start.6
  69.7 14.3 %copy-start.9 = (bf16[1568,128]{1,0:T(8,128)(2,1)S(1)}, bf16[1568,128]{1,0:T(8,128)(2,1)}, u32[]{:S(2)}) copy-start(bf16[1568,128]{1,0:T(8,128)(2,1)} %copy-done.8) | copy-start | bytes 1204228
  69.7 14.3 %copy-start.11 = (bf16[1568,128]{1,0:T(8,128)(2,1)S(1)}, bf16[1568,128]{1,0:T(8,128)(2,1)}, u32[]{:S(2)}) copy-start(bf16[1568,128]{1,0:T(8,128)(2,1)} %copy-done.10) | copy-start | bytes 1204228
  69.7 13.5 %collective-permute-start.11 = (bf16[3152,128]{1,0:T(8,128)(2,1)S(1)}, bf16[3152,128]{1,0:T(8,128)(2,1)S(1)}, u32[]{:S(2)}, u32[]{:S(2)}) collective-permute-start(bf16[3152,128]{1,0:T(8,128)(2,1)S(1)} %broadcast_select_fusion), channel_id=1, source_target_pairs={{0,2},{2,4},{4,6},{6,8},{8,10},{10,12},{12,14},{14,0},{32,46},{34,... | collective-permute-start | bytes 2420744 | tf_op jit(solution)/shard_map/ppermute | solution.py:337
  70.3 12.9 %collective-permute-start.15 = (bf16[3136,128]{1,0:T(8,128)(2,1)S(1)}, bf16[3136,128]{1,0:T(8,128)(2,1)S(1)}, u32[]{:S(2)}, u32[]{:S(2)}) collective-permute-start(bf16[3136,128]{1,0:T(8,128)(2,1)S(1)} %collective-permute-done.13.refs_3_.refs_12_), channel_id=1, source_target_pairs={{0,224},{32,0},{64,32},{96,64},{128,96},{160,128},{192,160},{224,1... | collective-permute-start | bytes 2408456 | tf_op jit(solution)/shard_map/ppermute | solution.py:299
  71.1 12.8 %collective-permute-start.14 = (bf16[3136,128]{1,0:T(8,128)(2,1)S(1)}, bf16[3136,128]{1,0:T(8,128)(2,1)S(1)}, u32[]{:S(2)}, u32[]{:S(2)}) collective-permute-start(bf16[3136,128]{1,0:T(8,128)(2,1)S(1)} %collective-permute-done.12.refs_2_.refs_11_), channel_id=1, source_target_pairs={{0,32},{32,64},{64,96},{96,128},{128,160},{160,192},{192,224},{224... | collective-permute-start | bytes 2408456 | tf_op jit(solution)/shard_map/ppermute | solution.py:299
  76.2 19.6 %copy-start.1 = (bf16[3152,128]{1,0:T(8,128)(2,1)S(1)}, bf16[3152,128]{1,0:T(8,128)(2,1)}, u32[]{:S(2)}) copy-start(bf16[3152,128]{1,0:T(8,128)(2,1)} %get-tuple-element.41.refs_0_) | copy-start | bytes 2420740
  76.2 19.6 %copy-start.4 = (bf16[3152,128]{1,0:T(8,128)(2,1)S(1)}, bf16[3152,128]{1,0:T(8,128)(2,1)}, u32[]{:S(2)}) copy-start(bf16[3152,128]{1,0:T(8,128)(2,1)} %copy-done.2) | copy-start | bytes 2420740
  76.3 19.6 %copy-start.7 = (bf16[3152,128]{1,0:T(8,128)(2,1)S(1)}, bf16[3152,128]{1,0:T(8,128)(2,1)}, u32[]{:S(2)}) copy-start(bf16[3152,128]{1,0:T(8,128)(2,1)} %copy-done.5) | copy-start | bytes 2420740
  91.4 29.0 %collective-permute-start.19 = (s16[528,512]{1,0:T(8,128)(2,1)S(1)}, s16[528,512]{1,0:T(8,128)(2,1)S(1)}, u32[]{:S(2)}, u32[]{:S(2)}) collective-permute-start(s16[528,512]{1,0:T(8,128)(2,1)S(1)} %get-tuple-element.40), channel_id=1, source_target_pairs={{0,1},{16,17},{1,0},{17,16},{2,3},{18,19},{3,2},{19,18},{4,5},{20,... | collective-permute-start | bytes 1622024 | tf_op jit(solution)/shard_map/ppermute | solution.py:307
  93.8 26.1 %collective-permute-start.20 = (s16[528,512]{1,0:T(8,128)(2,1)S(1)}, s16[528,512]{1,0:T(8,128)(2,1)S(1)}, u32[]{:S(2)}, u32[]{:S(2)}) collective-permute-start(s16[528,512]{1,0:T(8,128)(2,1)S(1)} %get-tuple-element.46), channel_id=1, source_target_pairs={{0,16},{16,1},{1,17},{17,0},{2,18},{18,3},{3,19},{19,2},{4,20},{20... | collective-permute-start | bytes 1622024 | tf_op jit(solution)/shard_map/ppermute | solution.py:307
  93.8 26.5 %collective-permute-start.21 = (s16[528,512]{1,0:T(8,128)(2,1)S(1)}, s16[528,512]{1,0:T(8,128)(2,1)S(1)}, u32[]{:S(2)}, u32[]{:S(2)}) collective-permute-start(s16[528,512]{1,0:T(8,128)(2,1)S(1)} %get-tuple-element.47), channel_id=1, source_target_pairs={{0,17},{16,0},{1,16},{17,1},{2,19},{18,2},{3,18},{19,3},{4,21},{20... | collective-permute-start | bytes 1622024 | tf_op jit(solution)/shard_map/ppermute | solution.py:307
  109.2 22.2 %collective-permute-start.16 = (s16[528,512]{1,0:T(8,128)(2,1)S(1)}, s16[528,512]{1,0:T(8,128)(2,1)S(1)}, u32[]{:S(2)}, u32[]{:S(2)}) collective-permute-start(s16[528,512]{1,0:T(8,128)(2,1)S(1)} %get-tuple-element.43), channel_id=1, source_target_pairs={{0,1},{16,17},{1,0},{17,16},{2,3},{18,19},{3,2},{19,18},{4,5},{20,... | collective-permute-start | bytes 1622024 | tf_op jit(solution)/shard_map/ppermute | solution.py:307
  110.7 29.4 %collective-permute-start.17 = (s16[528,512]{1,0:T(8,128)(2,1)S(1)}, s16[528,512]{1,0:T(8,128)(2,1)S(1)}, u32[]{:S(2)}, u32[]{:S(2)}) collective-permute-start(s16[528,512]{1,0:T(8,128)(2,1)S(1)} %get-tuple-element.44), channel_id=1, source_target_pairs={{0,16},{16,1},{1,17},{17,0},{2,18},{18,3},{3,19},{19,2},{4,20},{20... | collective-permute-start | bytes 1622024 | tf_op jit(solution)/shard_map/ppermute | solution.py:307
  119.9 20.2 %collective-permute-start.18 = (s16[528,512]{1,0:T(8,128)(2,1)S(1)}, s16[528,512]{1,0:T(8,128)(2,1)S(1)}, u32[]{:S(2)}, u32[]{:S(2)}) collective-permute-start(s16[528,512]{1,0:T(8,128)(2,1)S(1)} %get-tuple-element.45), channel_id=1, source_target_pairs={{0,17},{16,0},{1,16},{17,1},{2,19},{18,2},{3,18},{19,3},{4,21},{20... | collective-permute-start | bytes 1622024 | tf_op jit(solution)/shard_map/ppermute | solution.py:307
  (2 other events, 1.5 us)

commit v4 on v3

--- a/solution.py
+++ b/solution.py
@@ -25,7 +25,8 @@
 ROW = ("x", "core")
 NEAR = (0, 1, 2)
 NEXT = (3, 4)
-FAR = (5, 6, 7)
+LATE = (5, 6)
+FAR = (7,)
 STEPS = 64.0
 TOP = 32760.0
 LOWEST = -120.0
@@ -337,16 +338,19 @@
     opposite = lax.ppermute(jnp.where(lax.axis_index("core") == 0, up3, down3), ("core", "z"), pairs)
     high3, low3 = shift(high2, ROW, 1), shift(low2, ROW, -1)
     lower = product(False, NEXT, place, density, gram, lower, False)
+    density += [up3, down3]
+    gram += [high3, low3]
+    lower = product(False, LATE, place, density, gram, lower, False)
     opposite, lower = tie(opposite, lower)
-    density += [up3, down3, opposite]
-    gram += [high3, low3, facing, other_facing]
+    density.append(opposite)
+    gram += [facing, other_facing]
 
     def exchange(own, q2, qp, qm):
         return own, (shift_y(q2, 2), shift_y(qp, 1), shift_y(qm, -1)), q2
 
     out, parts1, done = exchange(*product(False, FAR, place, density, gram, lower, True))
     density[0], _ = tie(pa, done)
-    out, parts2, _ = exchange(*product(True, NEAR + NEXT + FAR, place, density, gram, None, True, out))
+    out, parts2, _ = exchange(*product(True, NEAR + NEXT + LATE + FAR, place, density, gram, None, True, out))
     return add_up(True, parts2, add_up(False, parts1, out))
 
 

time: 144 us -> 142 us (0.986)
  waiting for transfers between devices: 66.6 us -> 61.9 us
    ppermute x1, waiting for transfers between devices: 6.91 us -> 0.01 us  [per_device(): lax.ppermute(jnp.where(lax.axis_index('core') == 0, up3, down3), ('core',...]
    ppermute x15, starting transfers between devices: 18.6 us -> 20.8 us  [shift(): lax.ppermute(value, axis, [(k, (k + distance) % size) for k in range(size)])]
    ppermute x15, waiting for transfers between devices: 35.4 us -> 37.2 us  [shift(): lax.ppermute(value, axis, [(k, (k + distance) % size) for k in range(size)])]
    unnamed x25 -> x31, local copies, waits for them, and re-layouts: 7.66 us -> 9.07 us
    pallas_call x4 -> x5, Pallas kernels: 31 us -> 31.8 us  [product(): pl.pallas_call(functools.partial(product_kernel, upper, panels, first, la...]
  transfers between devices with their start and end apart: 22 -> 22, of which waited for: 12 -> 12; matrix products, arithmetic and copies ran while one was open for 2% -> 1% of each run, Pallas kernels for 18% -> 21%
where the time goes in v4:
time: 142 us; the launch traced here: 141 us
  waiting for transfers between devices  61.9 us (44%)
  Pallas kernels  38.9 us (27%)
  starting transfers between devices  29.5 us (21%)
  local copies, waits for them, and re-layouts  9.12 us (6%)
    ppermute x15, waiting for transfers between devices, shift(): lax.ppermute(value, axis, [(k, (k + distance) % size) for k in range(size)])  37.2 us
    pallas_call x5, Pallas kernels, product(): pl.pallas_call(functools.partial(product_kernel, upper, panels, first, la...  31.8 us
    ppermute x6, waiting for transfers between devices, shift_y(): return lax.ppermute(value, ('yl', 'yh'), pairs)  24.8 us
    ppermute x15, starting transfers between devices, shift(): lax.ppermute(value, axis, [(k, (k + distance) % size) for k in range(size)])  20.8 us
    unnamed x31, local copies, waits for them, and re-layouts  9.07 us
    ppermute x6, starting transfers between devices, shift_y(): return lax.ppermute(value, ('yl', 'yh'), pairs)  8.57 us
    pallas_call x2, Pallas kernels, add_up(): pl.pallas_call(functools.partial(sum_kernel, HALF if upper else 0), out_s...  4.31 us
    pallas_call x1, Pallas kernels, pack(): pl.pallas_call(pack_kernel, out_shape=[jax.ShapeDtypeStruct((ROWS_A, BLOC...  2.87 us
  transfers between devices with their start and end apart: 22, of which 12 were waited for; matrix products, arithmetic and copies ran while one was open for 1% of the time, Pallas kernels for 21%

profile of v4, /device:TPU:8, one launch (start us, length us, event | category | flops | bytes accessed | tf_op | source)
XLA Modules:
  0.0 140.6 jit_solution(10577476241507764491)
XLA Ops:
  0.7 2.9 %pack.1 = (bf16[3152,128]{1,0:T(8,128)(2,1)}, bf16[1568,128]{1,0:T(8,128)(2,1)}) custom-call(s32[24]{0:T(128)} %bitcast.14, s32[1]{0:T(128)} %bitcast.10.a_count, s32[2,6]{1,0:T(2,128)} %bitcast.13, s32[2]{0:T(128)} %bitcast.15, bf16[3072,128]{1,0:T(8,128)(2,1)} %bitcast.11, bf16[1536,128]{1,0:T(8,128)(2,1)} %bitcast.12), custom_call_target="tpu_custom_call" | custom-call | tf_op jit(solution)/shard_map/pack/pallas_call | solution.py:79
  3.5 5.9 %collective-permute-start.1 = (bf16[3152,128]{1,0:T(8,128)(2,1)}, bf16[3152,128]{1,0:T(8,128)(2,1)S(1)}, u32[]{:S(2)}, u32[]{:S(2)}) collective-permute-start(bf16[3152,128]{1,0:T(8,128)(2,1)} %get-tuple-element.41.refs_0_), channel_id=1, source_target_pairs={{0,14},{2,0},{4,2},{6,4},{8,6},{10,8},{12,10},{14,12},{1,15},{3,1}... | collective-permute-start | bytes 2420744 | tf_op jit(solution)/shard_map/ppermute | solution.py:300
  9.4 3.0 %collective-permute-start.2 = (bf16[1568,128]{1,0:T(8,128)(2,1)}, bf16[1568,128]{1,0:T(8,128)(2,1)S(1)}, u32[]{:S(2)}, u32[]{:S(2)}) collective-permute-start(bf16[1568,128]{1,0:T(8,128)(2,1)} %get-tuple-element.28), channel_id=1, source_target_pairs={{0,128},{32,160},{64,192},{96,224},{128,0},{160,32},{192,64},{224,... | collective-permute-start | bytes 1204232 | tf_op jit(solution)/shard_map/ppermute | solution.py:300
  12.9 1.1 constant_dynamic-update-slice_fusion.1
  13.9 7.9 %collective-permute-done.2.refs_1_.refs_15_ = bf16[1568,128]{1,0:T(8,128)(2,1)S(1)} collective-permute-done((bf16[1568,128]{1,0:T(8,128)(2,1)}, bf16[1568,128]{1,0:T(8,128)(2,1)S(1)}, u32[]{:S(2)}, u32[]{:S(2)}) %collective-permute-start.2) | collective-permute-done | bytes 401440 | tf_op jit(solution)/shard_map/ppermute | solution.py:300
  21.9 5.1 %collective-permute-done.1.refs_2_ = bf16[3152,128]{1,0:T(8,128)(2,1)S(1)} collective-permute-done((bf16[3152,128]{1,0:T(8,128)(2,1)}, bf16[3152,128]{1,0:T(8,128)(2,1)S(1)}, u32[]{:S(2)}, u32[]{:S(2)}) %collective-permute-start.1) | collective-permute-done | bytes 806944 | tf_op jit(solution)/shard_map/ppermute | solution.py:300
  27.0 3.3 %collective-permute-done.refs_1_ = bf16[3152,128]{1,0:T(8,128)(2,1)S(1)} collective-permute-done((bf16[3152,128]{1,0:T(8,128)(2,1)}, bf16[3152,128]{1,0:T(8,128)(2,1)S(1)}, u32[]{:S(2)}, u32[]{:S(2)}) %collective-permute-start) | collective-permute-done | bytes 806944 | tf_op jit(solution)/shard_map/ppermute | solution.py:300
  31.2 3.2 %collective-permute-start.4 = (bf16[3152,128]{1,0:T(8,128)(2,1)S(1)}, bf16[3152,128]{1,0:T(8,128)(2,1)S(1)}, u32[]{:S(2)}, u32[]{:S(2)}) collective-permute-start(bf16[3152,128]{1,0:T(8,128)(2,1)S(1)} %collective-permute-done.1.refs_2_), channel_id=1, source_target_pairs={{0,14},{2,0},{4,2},{6,4},{8,6},{10,8},{12,10},{14,12},{1,15},{3,1}... | collective-permute-start | bytes 2420744 | tf_op jit(solution)/shard_map/ppermute | solution.py:300
  37.2 11.6 %collective-permute-done.5.refs_2_.refs_16_ = bf16[1568,128]{1,0:T(8,128)(2,1)S(1)} collective-permute-done((bf16[1568,128]{1,0:T(8,128)(2,1)S(1)}, bf16[1568,128]{1,0:T(8,128)(2,1)S(1)}, u32[]{:S(2)}, u32[]{:S(2)}) %collective-permute-start.5) | collective-permute-done | bytes 401440 | tf_op jit(solution)/shard_map/ppermute | solution.py:300
  50.2 3.7 %collective-permute-start.7 = (bf16[3152,128]{1,0:T(8,128)(2,1)S(1)}, bf16[3152,128]{1,0:T(8,128)(2,1)S(1)}, u32[]{:S(2)}, u32[]{:S(2)}) collective-permute-start(bf16[3152,128]{1,0:T(8,128)(2,1)S(1)} %collective-permute-done.4.refs_1_.refs_4_), channel_id=1, source_target_pairs={{0,14},{2,0},{4,2},{6,4},{8,6},{10,8},{12,10},{14,12},{1,15},{3,1}... | collective-permute-start | bytes 2420744 | tf_op jit(solution)/shard_map/ppermute | solution.py:300
  54.5 1.1 copy-done.5
  55.6 1.1 copy-done.7
  56.8 1.1 copy-done.10
  57.9 1.1 copy-done.13
  59.0 5.3 %lower3.1.refs_4_ = f32[16,512,128]{2,1,0:T(8,128)S(1)} custom-call(s32[4]{0:T(128)S(1)} %pad_add_fusion.place, bf16[3152,128]{1,0:T(8,128)(2,1)S(1)} %copy-done.7, bf16[3152,128]{1,0:T(8,128)(2,1)S(1)} %copy-done.13, bf16[3152,128]{1,0:T(8,128)(2,1)S(1)} %copy-done.10, bf16[3136,128]{1,0:T(8,128)(2,1)S(1)} %copy-done.5, ...), custom_call_target="tpu_custom_call" | custom-call | flops 3000000000 | bytes 6000000 | tf_op jit(solution)/shard_map/lower3/pallas_call | solution.py:225
  64.3 3.1 %collective-permute-start.15 = (bf16[3136,128]{1,0:T(8,128)(2,1)}, bf16[3136,128]{1,0:T(8,128)(2,1)S(1)}, u32[]{:S(2)}, u32[]{:S(2)}) collective-permute-start(bf16[3136,128]{1,0:T(8,128)(2,1)} %collective-permute-done.14.refs_3_.refs_12_), channel_id=1, source_target_pairs={{0,224},{32,0},{64,32},{96,64},{128,96},{160,128},{192,160},{224,1... | collective-permute-start | bytes 2408456 | tf_op jit(solution)/shard_map/ppermute | solution.py:300
  67.4 3.6 %collective-permute-done.6.refs_0_.refs_5_ = bf16[3152,128]{1,0:T(8,128)(2,1)S(1)} collective-permute-done((bf16[3152,128]{1,0:T(8,128)(2,1)S(1)}, bf16[3152,128]{1,0:T(8,128)(2,1)S(1)}, u32[]{:S(2)}, u32[]{:S(2)}) %collective-permute-start.6) | collective-permute-done | bytes 806944 | tf_op jit(solution)/shard_map/ppermute | solution.py:300
  71.2 4.2 %lower2.2.refs_4_ = f32[16,512,128]{2,1,0:T(8,128)S(1)} custom-call(s32[4]{0:T(128)S(1)} %pad_add_fusion.place, bf16[3152,128]{1,0:T(8,128)(2,1)S(1)} %collective-permute-done.3.refs_0_.refs_3_, bf16[3152,128]{1,0:T(8,128)(2,1)S(1)} %collective-permute-done.4.refs_1_.refs_4_, bf16[3136,128]{1,0:T(8,128)(2,1)} %collective-permute-done.12.refs_2_.refs_11_, ...), custom_call_target="tpu_custom_call" | custom-call | flops 2000000000 | bytes 4000000 | tf_op jit(solution)/shard_map/lower2/pallas_call | solution.py:225
  75.4 2.0 %collective-permute-done.15.refs_3_.refs_14_ = bf16[3136,128]{1,0:T(8,128)(2,1)S(1)} collective-permute-done((bf16[3136,128]{1,0:T(8,128)(2,1)}, bf16[3136,128]{1,0:T(8,128)(2,1)S(1)}, u32[]{:S(2)}, u32[]{:S(2)}) %collective-permute-start.15) | collective-permute-done | bytes 802848 | tf_op jit(solution)/shard_map/ppermute | solution.py:300
  77.4 3.0 %collective-permute-done.13.refs_2_.refs_13_ = bf16[3136,128]{1,0:T(8,128)(2,1)S(1)} collective-permute-done((bf16[3136,128]{1,0:T(8,128)(2,1)}, bf16[3136,128]{1,0:T(8,128)(2,1)S(1)}, u32[]{:S(2)}, u32[]{:S(2)}) %collective-permute-start.13) | collective-permute-done | bytes 802848 | tf_op jit(solution)/shard_map/ppermute | solution.py:300
  80.4 5.1 %lower2.3.refs_3_ = f32[16,512,128]{2,1,0:T(8,128)S(1)} custom-call(s32[4]{0:T(128)S(1)} %pad_add_fusion.place, bf16[3152,128]{1,0:T(8,128)(2,1)S(1)} %collective-permute-done.6.refs_0_.refs_5_, bf16[3152,128]{1,0:T(8,128)(2,1)S(1)} %collective-permute-done.7.refs_1_.refs_6_, bf16[3136,128]{1,0:T(8,128)(2,1)S(1)} %collective-permute-done.13.refs_2_.refs_13_, ...), custom_call_target="tpu_custom_call" | custom-call | flops 2000000000 | bytes 4000000 | tf_op jit(solution)/shard_map/lower2/pallas_call | solution.py:225
  85.6 4.4 %lower1_last.1 = (f32[1024,512]{1,0:T(8,128)}, s16[528,512]{1,0:T(8,128)(2,1)S(1)}, s16[528,512]{1,0:T(8,128)(2,1)S(1)}, s16[528,512]{1,0:T(8,128)(2,1)S(1)}) custom-call(s32[4]{0:T(128)S(1)} %pad_add_fusion.place, bf16[3152,128]{1,0:T(8,128)(2,1)S(1)} %collective-permute-done.11.refs_0_.refs_7_, bf16[1568,128]{1,0:T(8,128)(2,1)S(1)} %copy-done.1, ...), custom_call_target="tpu_custom_call" | custom-call | flops 1000000000 | bytes 2000000 | tf_op jit(solution)/shard_map/lower1_last/pallas_call | solution.py:225
  90.1 2.2 %collective-permute-start.19 = (s16[528,512]{1,0:T(8,128)(2,1)S(1)}, s16[528,512]{1,0:T(8,128)(2,1)S(1)}, u32[]{:S(2)}, u32[]{:S(2)}) collective-permute-start(s16[528,512]{1,0:T(8,128)(2,1)S(1)} %get-tuple-element.40), channel_id=1, source_target_pairs={{0,1},{16,17},{1,0},{17,16},{2,3},{18,19},{3,2},{19,18},{4,5},{20,... | collective-permute-start | bytes 1622024 | tf_op jit(solution)/shard_map/ppermute | solution.py:308
  92.3 2.0 %collective-permute-start.21 = (s16[528,512]{1,0:T(8,128)(2,1)S(1)}, s16[528,512]{1,0:T(8,128)(2,1)S(1)}, u32[]{:S(2)}, u32[]{:S(2)}) collective-permute-start(s16[528,512]{1,0:T(8,128)(2,1)S(1)} %get-tuple-element.47), channel_id=1, source_target_pairs={{0,17},{16,0},{1,16},{17,1},{2,19},{18,2},{3,18},{19,3},{4,21},{20... | collective-permute-start | bytes 1622024 | tf_op jit(solution)/shard_map/ppermute | solution.py:308
  94.3 12.7 %upper8_last.1 = (f32[1024,512]{1,0:T(8,128)}, s16[528,512]{1,0:T(8,128)(2,1)S(1)}, s16[528,512]{1,0:T(8,128)(2,1)S(1)}, s16[528,512]{1,0:T(8,128)(2,1)S(1)}) custom-call(s32[4]{0:T(128)S(1)} %pad_add_fusion.place, bf16[3152,128]{1,0:T(8,128)(2,1)S(1)} %copy-done.8, bf16[3152,128]{1,0:T(8,128)(2,1)S(1)} %copy-done.14, ...), custom_call_target="tpu_custom_call", output_to_operand_aliasing={{0}: (18, {})} | custom-call | flops 8000000000 | bytes 16000000 | tf_op jit(solution)/shard_map/upper8_last/pallas_call | solution.py:225
  107.1 1.6 %collective-permute-start.16 = (s16[528,512]{1,0:T(8,128)(2,1)S(1)}, s16[528,512]{1,0:T(8,128)(2,1)S(1)}, u32[]{:S(2)}, u32[]{:S(2)}) collective-permute-start(s16[528,512]{1,0:T(8,128)(2,1)S(1)} %get-tuple-element.43), channel_id=1, source_target_pairs={{0,1},{16,17},{1,0},{17,16},{2,3},{18,19},{3,2},{19,18},{4,5},{20,... | collective-permute-start | bytes 1622024 | tf_op jit(solution)/shard_map/ppermute | solution.py:308
  108.6 2.6 %collective-permute-start.17 = (s16[528,512]{1,0:T(8,128)(2,1)S(1)}, s16[528,512]{1,0:T(8,128)(2,1)S(1)}, u32[]{:S(2)}, u32[]{:S(2)}) collective-permute-start(s16[528,512]{1,0:T(8,128)(2,1)S(1)} %get-tuple-element.44), channel_id=1, source_target_pairs={{0,16},{16,1},{1,17},{17,0},{2,18},{18,3},{3,19},{19,2},{4,20},{20... | collective-permute-start | bytes 1622024 | tf_op jit(solution)/shard_map/ppermute | solution.py:308
  111.2 7.4 %collective-permute-done.20.refs_1_ = s16[528,512]{1,0:T(8,128)(2,1)S(1)} collective-permute-done((s16[528,512]{1,0:T(8,128)(2,1)S(1)}, s16[528,512]{1,0:T(8,128)(2,1)S(1)}, u32[]{:S(2)}, u32[]{:S(2)}) %collective-permute-start.20) | collective-permute-done | bytes 540704 | tf_op jit(solution)/shard_map/ppermute | solution.py:308
  118.8 2.2 %add_up.2.refs_3_ = f32[1024,512]{1,0:T(8,128)} custom-call(s16[528,512]{1,0:T(8,128)(2,1)S(1)} %collective-permute-done.19.refs_0_, s16[528,512]{1,0:T(8,128)(2,1)S(1)} %collective-permute-done.20.refs_1_, s16[528,512]{1,0:T(8,128)(2,1)S(1)} %collective-permute-done.21.refs_2_, f32[1024,512]{1,0:T(8,128)} %get-tuple-element.48.refs_3_), custom_call_target="tpu_custom_call", output_to_operand_aliasing={{}: (3, {})} | custom-call | tf_op jit(solution)/shard_map/add_up/pallas_call | solution.py:282
  121.0 9.1 %collective-permute-done.16.refs_0_ = s16[528,512]{1,0:T(8,128)(2,1)S(1)} collective-permute-done((s16[528,512]{1,0:T(8,128)(2,1)S(1)}, s16[528,512]{1,0:T(8,128)(2,1)S(1)}, u32[]{:S(2)}, u32[]{:S(2)}) %collective-permute-start.16) | collective-permute-done | bytes 540704 | tf_op jit(solution)/shard_map/ppermute | solution.py:308
  130.1 8.2 %collective-permute-done.17.refs_1_ = s16[528,512]{1,0:T(8,128)(2,1)S(1)} collective-permute-done((s16[528,512]{1,0:T(8,128)(2,1)S(1)}, s16[528,512]{1,0:T(8,128)(2,1)S(1)}, u32[]{:S(2)}, u32[]{:S(2)}) %collective-permute-start.17) | collective-permute-done | bytes 540704 | tf_op jit(solution)/shard_map/ppermute | solution.py:308
  138.3 2.2 %add_up.3 = f32[1024,512]{1,0:T(8,128)} custom-call(s16[528,512]{1,0:T(8,128)(2,1)S(1)} %collective-permute-done.16.refs_0_, s16[528,512]{1,0:T(8,128)(2,1)S(1)} %collective-permute-done.17.refs_1_, s16[528,512]{1,0:T(8,128)(2,1)S(1)} %collective-permute-done.18.refs_2_, f32[1024,512]{1,0:T(8,128)} %add_up.2.refs_3_), custom_call_target="tpu_custom_call", output_to_operand_aliasing={{}: (3, {})} | custom-call | tf_op jit(solution)/shard_map/add_up/pallas_call | solution.py:282
  (54 shorter events, 6.6 us)
Async XLA Ops:
  3.5 23.4 %collective-permute-start.1 = (bf16[3152,128]{1,0:T(8,128)(2,1)}, bf16[3152,128]{1,0:T(8,128)(2,1)S(1)}, u32[]{:S(2)}, u32[]{:S(2)}) collective-permute-start(bf16[3152,128]{1,0:T(8,128)(2,1)} %get-tuple-element.41.refs_0_), channel_id=1, source_target_pairs={{0,14},{2,0},{4,2},{6,4},{8,6},{10,8},{12,10},{14,12},{1,15},{3,1}... | collective-permute-start | bytes 2420744 | tf_op jit(solution)/shard_map/ppermute | solution.py:300
  9.4 20.9 %collective-permute-start = (bf16[3152,128]{1,0:T(8,128)(2,1)}, bf16[3152,128]{1,0:T(8,128)(2,1)S(1)}, u32[]{:S(2)}, u32[]{:S(2)}) collective-permute-start(bf16[3152,128]{1,0:T(8,128)(2,1)} %get-tuple-element.41.refs_0_), channel_id=1, source_target_pairs={{0,2},{2,4},{4,6},{6,8},{8,10},{10,12},{12,14},{14,0},{1,3},{3,5},... | collective-permute-start | bytes 2420744 | tf_op jit(solution)/shard_map/ppermute | solution.py:300
  9.4 12.5 %collective-permute-start.2 = (bf16[1568,128]{1,0:T(8,128)(2,1)}, bf16[1568,128]{1,0:T(8,128)(2,1)S(1)}, u32[]{:S(2)}, u32[]{:S(2)}) collective-permute-start(bf16[1568,128]{1,0:T(8,128)(2,1)} %get-tuple-element.28), channel_id=1, source_target_pairs={{0,128},{32,160},{64,192},{96,224},{128,0},{160,32},{192,64},{224,... | collective-permute-start | bytes 1204232 | tf_op jit(solution)/shard_map/ppermute | solution.py:300
  12.4 22.9 %collective-permute-start.8 = (bf16[1568,128]{1,0:T(8,128)(2,1)}, bf16[1568,128]{1,0:T(8,128)(2,1)S(1)}, u32[]{:S(2)}, u32[]{:S(2)}) collective-permute-start(bf16[1568,128]{1,0:T(8,128)(2,1)} %get-tuple-element.28), channel_id=1, source_target_pairs={{0,16},{16,0},{1,17},{17,1},{2,18},{18,2},{3,19},{19,3},{4,20},{20... | collective-permute-start | bytes 1204232 | tf_op jit(solution)/shard_map/ppermute | solution.py:300
  21.9 28.3 %copy-start = (bf16[1568,128]{1,0:T(8,128)(2,1)}, bf16[1568,128]{1,0:T(8,128)(2,1)S(1)}, u32[]{:S(2)}) copy-start(bf16[1568,128]{1,0:T(8,128)(2,1)S(1)} %collective-permute-done.2.refs_1_.refs_15_) | copy-start | bytes 1204228
  30.3 19.8 %collective-permute-start.3 = (bf16[3152,128]{1,0:T(8,128)(2,1)S(1)}, bf16[3152,128]{1,0:T(8,128)(2,1)S(1)}, u32[]{:S(2)}, u32[]{:S(2)}) collective-permute-start(bf16[3152,128]{1,0:T(8,128)(2,1)S(1)} %collective-permute-done.refs_1_), channel_id=1, source_target_pairs={{0,2},{2,4},{4,6},{6,8},{8,10},{10,12},{12,14},{14,0},{1,3},{3,5},... | collective-permute-start | bytes 2420744 | tf_op jit(solution)/shard_map/ppermute | solution.py:300
  31.2 19.0 %collective-permute-start.4 = (bf16[3152,128]{1,0:T(8,128)(2,1)S(1)}, bf16[3152,128]{1,0:T(8,128)(2,1)S(1)}, u32[]{:S(2)}, u32[]{:S(2)}) collective-permute-start(bf16[3152,128]{1,0:T(8,128)(2,1)S(1)} %collective-permute-done.1.refs_2_), channel_id=1, source_target_pairs={{0,14},{2,0},{4,2},{6,4},{8,6},{10,8},{12,10},{14,12},{1,15},{3,1}... | collective-permute-start | bytes 2420744 | tf_op jit(solution)/shard_map/ppermute | solution.py:300
  35.3 18.5 %collective-permute-start.10 = (bf16[3136,128]{1,0:T(8,128)(2,1)S(1)}, bf16[3136,128]{1,0:T(8,128)(2,1)}, u32[]{:S(2)}, u32[]{:S(2)}) collective-permute-start(bf16[3136,128]{1,0:T(8,128)(2,1)S(1)} %constant_dynamic-update-slice_fusion.refs_3_.refs_8_), channel_id=1, source_target_pairs={{0,224},{32,0},{64,32},{96,64},{128,96},{160,128},{192,160},{224,1... | collective-permute-start | bytes 2408456 | tf_op jit(solution)/shard_map/ppermute | solution.py:300
  35.8 18.3 %collective-permute-start.9 = (bf16[3136,128]{1,0:T(8,128)(2,1)S(1)}, bf16[3136,128]{1,0:T(8,128)(2,1)}, u32[]{:S(2)}, u32[]{:S(2)}) collective-permute-start(bf16[3136,128]{1,0:T(8,128)(2,1)S(1)} %constant_dynamic-update-slice_fusion.refs_3_.refs_8_), channel_id=1, source_target_pairs={{0,32},{32,64},{64,96},{96,128},{128,160},{160,192},{192,224},{224... | collective-permute-start | bytes 2408456 | tf_op jit(solution)/shard_map/ppermute | solution.py:300
  36.8 12.0 %collective-permute-start.5 = (bf16[1568,128]{1,0:T(8,128)(2,1)S(1)}, bf16[1568,128]{1,0:T(8,128)(2,1)S(1)}, u32[]{:S(2)}, u32[]{:S(2)}) collective-permute-start(bf16[1568,128]{1,0:T(8,128)(2,1)S(1)} %collective-permute-done.2.refs_1_.refs_15_), channel_id=1, source_target_pairs={{0,16},{16,0},{1,17},{17,1},{2,18},{18,2},{3,19},{19,3},{4,20},{20... | collective-permute-start | bytes 1204232 | tf_op jit(solution)/shard_map/ppermute | solution.py:300
  50.2 20.8 %collective-permute-start.6 = (bf16[3152,128]{1,0:T(8,128)(2,1)S(1)}, bf16[3152,128]{1,0:T(8,128)(2,1)S(1)}, u32[]{:S(2)}, u32[]{:S(2)}) collective-permute-start(bf16[3152,128]{1,0:T(8,128)(2,1)S(1)} %collective-permute-done.3.refs_0_.refs_3_), channel_id=1, source_target_pairs={{0,2},{2,4},{4,6},{6,8},{8,10},{10,12},{12,14},{14,0},{1,3},{3,5},... | collective-permute-start | bytes 2420744 | tf_op jit(solution)/shard_map/ppermute | solution.py:300
  50.2 20.8 %collective-permute-start.7 = (bf16[3152,128]{1,0:T(8,128)(2,1)S(1)}, bf16[3152,128]{1,0:T(8,128)(2,1)S(1)}, u32[]{:S(2)}, u32[]{:S(2)}) collective-permute-start(bf16[3152,128]{1,0:T(8,128)(2,1)S(1)} %collective-permute-done.4.refs_1_.refs_4_), channel_id=1, source_target_pairs={{0,14},{2,0},{4,2},{6,4},{8,6},{10,8},{12,10},{14,12},{1,15},{3,1}... | collective-permute-start | bytes 2420744 | tf_op jit(solution)/shard_map/ppermute | solution.py:300
  53.9 10.5 %collective-permute-start.14 = (bf16[3136,128]{1,0:T(8,128)(2,1)}, bf16[3136,128]{1,0:T(8,128)(2,1)}, u32[]{:S(2)}, u32[]{:S(2)}) collective-permute-start(bf16[3136,128]{1,0:T(8,128)(2,1)} %collective-permute-done.10.refs_5_.refs_10_), channel_id=1, source_target_pairs={{0,224},{32,0},{64,32},{96,64},{128,96},{160,128},{192,160},{224,1... | collective-permute-start | bytes 2408456 | tf_op jit(solution)/shard_map/ppermute | solution.py:300
  54.1 13.3 %collective-permute-start.12 = (bf16[3136,128]{1,0:T(8,128)(2,1)}, bf16[3136,128]{1,0:T(8,128)(2,1)}, u32[]{:S(2)}, u32[]{:S(2)}) collective-permute-start(bf16[3136,128]{1,0:T(8,128)(2,1)} %collective-permute-done.9.refs_4_.refs_9_), channel_id=1, source_target_pairs={{0,32},{32,64},{64,96},{96,128},{128,160},{160,192},{192,224},{224... | collective-permute-start | bytes 2408456 | tf_op jit(solution)/shard_map/ppermute | solution.py:300
  54.5 1.1 copy-start.5
  55.6 1.1 copy-start.7
  56.8 1.1 copy-start.10
  64.3 13.1 %collective-permute-start.15 = (bf16[3136,128]{1,0:T(8,128)(2,1)}, bf16[3136,128]{1,0:T(8,128)(2,1)S(1)}, u32[]{:S(2)}, u32[]{:S(2)}) collective-permute-start(bf16[3136,128]{1,0:T(8,128)(2,1)} %collective-permute-done.14.refs_3_.refs_12_), channel_id=1, source_target_pairs={{0,224},{32,0},{64,32},{96,64},{128,96},{160,128},{192,160},{224,1... | collective-permute-start | bytes 2408456 | tf_op jit(solution)/shard_map/ppermute | solution.py:300
  67.4 13.0 %collective-permute-start.13 = (bf16[3136,128]{1,0:T(8,128)(2,1)}, bf16[3136,128]{1,0:T(8,128)(2,1)S(1)}, u32[]{:S(2)}, u32[]{:S(2)}) collective-permute-start(bf16[3136,128]{1,0:T(8,128)(2,1)} %collective-permute-done.12.refs_2_.refs_11_), channel_id=1, source_target_pairs={{0,32},{32,64},{64,96},{96,128},{128,160},{160,192},{192,224},{224... | collective-permute-start | bytes 2408456 | tf_op jit(solution)/shard_map/ppermute | solution.py:300
  71.1 14.5 %collective-permute-start.11 = (bf16[3152,128]{1,0:T(8,128)(2,1)S(1)}, bf16[3152,128]{1,0:T(8,128)(2,1)S(1)}, u32[]{:S(2)}, u32[]{:S(2)}) collective-permute-start(bf16[3152,128]{1,0:T(8,128)(2,1)S(1)} %broadcast_select_fusion), channel_id=1, source_target_pairs={{0,2},{2,4},{4,6},{6,8},{8,10},{10,12},{12,14},{14,0},{32,46},{34,... | collective-permute-start | bytes 2420744 | tf_op jit(solution)/shard_map/ppermute | solution.py:338
  75.4 10.3 %copy-start.1 = (bf16[1568,128]{1,0:T(8,128)(2,1)S(1)}, bf16[1568,128]{1,0:T(8,128)(2,1)}, u32[]{:S(2)}) copy-start(bf16[1568,128]{1,0:T(8,128)(2,1)} %copy-done) | copy-start | bytes 1204228
  75.4 10.3 %copy-start.3 = (bf16[1568,128]{1,0:T(8,128)(2,1)S(1)}, bf16[1568,128]{1,0:T(8,128)(2,1)}, u32[]{:S(2)}) copy-start(bf16[1568,128]{1,0:T(8,128)(2,1)} %copy-done.2) | copy-start | bytes 1204228
  85.6 8.8 %copy-start.6 = (bf16[3136,128]{1,0:T(8,128)(2,1)S(1)}, bf16[3136,128]{1,0:T(8,128)(2,1)}, u32[]{:S(2)}) copy-start(bf16[3136,128]{1,0:T(8,128)(2,1)} %copy-done.4) | copy-start | bytes 2408452
  85.6 8.8 %copy-start.8 = (bf16[3152,128]{1,0:T(8,128)(2,1)S(1)}, bf16[3152,128]{1,0:T(8,128)(2,1)}, u32[]{:S(2)}) copy-start(bf16[3152,128]{1,0:T(8,128)(2,1)} %get-tuple-element.41.refs_0_) | copy-start | bytes 2420740
  85.6 8.7 %copy-start.11 = (bf16[3152,128]{1,0:T(8,128)(2,1)S(1)}, bf16[3152,128]{1,0:T(8,128)(2,1)}, u32[]{:S(2)}) copy-start(bf16[3152,128]{1,0:T(8,128)(2,1)} %copy-done.9) | copy-start | bytes 2420740
  85.6 8.7 %copy-start.14 = (bf16[3152,128]{1,0:T(8,128)(2,1)S(1)}, bf16[3152,128]{1,0:T(8,128)(2,1)}, u32[]{:S(2)}) copy-start(bf16[3152,128]{1,0:T(8,128)(2,1)} %copy-done.12) | copy-start | bytes 2420740
  90.1 28.7 %collective-permute-start.19 = (s16[528,512]{1,0:T(8,128)(2,1)S(1)}, s16[528,512]{1,0:T(8,128)(2,1)S(1)}, u32[]{:S(2)}, u32[]{:S(2)}) collective-permute-start(s16[528,512]{1,0:T(8,128)(2,1)S(1)} %get-tuple-element.40), channel_id=1, source_target_pairs={{0,1},{16,17},{1,0},{17,16},{2,3},{18,19},{3,2},{19,18},{4,5},{20,... | collective-permute-start | bytes 1622024 | tf_op jit(solution)/shard_map/ppermute | solution.py:308
  92.3 26.3 %collective-permute-start.20 = (s16[528,512]{1,0:T(8,128)(2,1)S(1)}, s16[528,512]{1,0:T(8,128)(2,1)S(1)}, u32[]{:S(2)}, u32[]{:S(2)}) collective-permute-start(s16[528,512]{1,0:T(8,128)(2,1)S(1)} %get-tuple-element.46), channel_id=1, source_target_pairs={{0,16},{16,1},{1,17},{17,0},{2,18},{18,3},{3,19},{19,2},{4,20},{20... | collective-permute-start | bytes 1622024 | tf_op jit(solution)/shard_map/ppermute | solution.py:308
  92.3 26.5 %collective-permute-start.21 = (s16[528,512]{1,0:T(8,128)(2,1)S(1)}, s16[528,512]{1,0:T(8,128)(2,1)S(1)}, u32[]{:S(2)}, u32[]{:S(2)}) collective-permute-start(s16[528,512]{1,0:T(8,128)(2,1)S(1)} %get-tuple-element.47), channel_id=1, source_target_pairs={{0,17},{16,0},{1,16},{17,1},{2,19},{18,2},{3,18},{19,3},{4,21},{20... | collective-permute-start | bytes 1622024 | tf_op jit(solution)/shard_map/ppermute | solution.py:308
  107.1 23.0 %collective-permute-start.16 = (s16[528,512]{1,0:T(8,128)(2,1)S(1)}, s16[528,512]{1,0:T(8,128)(2,1)S(1)}, u32[]{:S(2)}, u32[]{:S(2)}) collective-permute-start(s16[528,512]{1,0:T(8,128)(2,1)S(1)} %get-tuple-element.43), channel_id=1, source_target_pairs={{0,1},{16,17},{1,0},{17,16},{2,3},{18,19},{3,2},{19,18},{4,5},{20,... | collective-permute-start | bytes 1622024 | tf_op jit(solution)/shard_map/ppermute | solution.py:308
  108.6 29.7 %collective-permute-start.17 = (s16[528,512]{1,0:T(8,128)(2,1)S(1)}, s16[528,512]{1,0:T(8,128)(2,1)S(1)}, u32[]{:S(2)}, u32[]{:S(2)}) collective-permute-start(s16[528,512]{1,0:T(8,128)(2,1)S(1)} %get-tuple-element.44), channel_id=1, source_target_pairs={{0,16},{16,1},{1,17},{17,0},{2,18},{18,3},{3,19},{19,2},{4,20},{20... | collective-permute-start | bytes 1622024 | tf_op jit(solution)/shard_map/ppermute | solution.py:308
  118.6 19.7 %collective-permute-start.18 = (s16[528,512]{1,0:T(8,128)(2,1)S(1)}, s16[528,512]{1,0:T(8,128)(2,1)S(1)}, u32[]{:S(2)}, u32[]{:S(2)}) collective-permute-start(s16[528,512]{1,0:T(8,128)(2,1)S(1)} %get-tuple-element.45), channel_id=1, source_target_pairs={{0,17},{16,0},{1,16},{17,1},{2,19},{18,2},{3,18},{19,3},{4,21},{20... | collective-permute-start | bytes 1622024 | tf_op jit(solution)/shard_map/ppermute | solution.py:308
  (5 other events, 4.6 us)

commit v5 on v4

--- a/solution.py
+++ b/solution.py
@@ -23,7 +23,8 @@
 OFFSETS = (0, -1, 1, -2, 2, -3, 3, 4)
 HEIGHT = HALF * BLOCK
 ROW = ("x", "core")
-NEAR = (0, 1, 2)
+OWN = (0,)
+NEAR = (1, 2)
 NEXT = (3, 4)
 LATE = (5, 6)
 FAR = (7,)
@@ -326,10 +327,13 @@
     up1, down1, facing = tie(shift(pa, "z", 1), shift(pa, "z", -1), shift(pb, ROW, 4))
     both = jnp.concatenate([pb, shift(pb, "yl", 1)], axis=0)
     high1, low1 = shift(both, ROW, 1), shift(both, ROW, -1)
-    up2, down2, other_facing = tie(shift(up1, "z", 1), shift(down1, "z", -1), shift(facing, "yl", 1))
+    lower = product(False, OWN, place, [pa], [both], None, False)
+    up2, down2, other_facing, lower = tie(
+        shift(up1, "z", 1), shift(down1, "z", -1), shift(facing, "yl", 1), lower
+    )
     density = [pa, up1, down1, up2, down2]
     gram = [both, high1, low1]
-    lower = product(False, NEAR, place, density, gram, None, False)
+    lower = product(False, NEAR, place, density, gram, lower, False)
     high2, low2 = shift(high1, ROW, 1), shift(low1, ROW, -1)
     up3, down3, lower = tie(shift(up2, "z", 1), shift(down2, "z", -1), lower)
     gram += [high2, low2]
@@ -350,7 +354,7 @@
 
     out, parts1, done = exchange(*product(False, FAR, place, density, gram, lower, True))
     density[0], _ = tie(pa, done)
-    out, parts2, _ = exchange(*product(True, NEAR + NEXT + LATE + FAR, place, density, gram, None, True, out))
+    out, parts2, _ = exchange(*product(True, OWN + NEAR + NEXT + LATE + FAR, place, density, gram, None, True, out))
     return add_up(True, parts2, add_up(False, parts1, out))
 
 

time: 142 us -> 142 us (level)
    pallas_call x5 -> x6, Pallas kernels: 31.8 us -> 32.9 us  [product(): pl.pallas_call(functools.partial(product_kernel, upper, panels, first, la...]
    unnamed x31 -> x19, local copies, waits for them, and re-layouts: 9.07 us -> 8.38 us
  transfers between devices with their start and end apart: 22 -> 22, of which waited for: 12 -> 12; matrix products, arithmetic and copies ran while one was open for 1% -> 1% of each run, Pallas kernels for 21% -> 22%
where the time goes in v5:
time: 142 us; the launch traced here: 141 us
  waiting for transfers between devices  61.4 us (43%)
  Pallas kernels  40.1 us (28%)
  starting transfers between devices  29.8 us (21%)
  local copies, waits for them, and re-layouts  8.43 us (6%)
    ppermute x15, waiting for transfers between devices, shift(): lax.ppermute(value, axis, [(k, (k + distance) % size) for k in range(size)])  36.1 us
    pallas_call x6, Pallas kernels, product(): pl.pallas_call(functools.partial(product_kernel, upper, panels, first, la...  32.9 us
    ppermute x6, waiting for transfers between devices, shift_y(): return lax.ppermute(value, ('yl', 'yh'), pairs)  25.3 us
    ppermute x15, starting transfers between devices, shift(): lax.ppermute(value, axis, [(k, (k + distance) % size) for k in range(size)])  20.6 us
    ppermute x6, starting transfers between devices, shift_y(): return lax.ppermute(value, ('yl', 'yh'), pairs)  9.11 us
    unnamed x19, local copies, waits for them, and re-layouts  8.38 us
    pallas_call x2, Pallas kernels, add_up(): pl.pallas_call(functools.partial(sum_kernel, HALF if upper else 0), out_s...  4.32 us
    pallas_call x1, Pallas kernels, pack(): pl.pallas_call(pack_kernel, out_shape=[jax.ShapeDtypeStruct((ROWS_A, BLOC...  2.87 us
  transfers between devices with their start and end apart: 22, of which 12 were waited for; matrix products, arithmetic and copies ran while one was open for 1% of the time, Pallas kernels for 22%

profile of v5, /device:TPU:8, one launch (start us, length us, event | category | flops | bytes accessed | tf_op | source)
XLA Modules:
  0.0 140.8 jit_solution(11537059822106858990)
XLA Ops:
  0.7 2.9 %pack.1 = (bf16[3152,128]{1,0:T(8,128)(2,1)}, bf16[1568,128]{1,0:T(8,128)(2,1)}) custom-call(s32[24]{0:T(128)} %bitcast.14, s32[1]{0:T(128)} %bitcast.10.a_count, s32[2,6]{1,0:T(2,128)} %bitcast.13, s32[2]{0:T(128)} %bitcast.15, bf16[3072,128]{1,0:T(8,128)(2,1)} %bitcast.11, bf16[1536,128]{1,0:T(8,128)(2,1)} %bitcast.12), custom_call_target="tpu_custom_call" | custom-call | tf_op jit(solution)/shard_map/pack/pallas_call | solution.py:80
  3.5 5.9 %collective-permute-start.1 = (bf16[3152,128]{1,0:T(8,128)(2,1)}, bf16[3152,128]{1,0:T(8,128)(2,1)S(1)}, u32[]{:S(2)}, u32[]{:S(2)}) collective-permute-start(bf16[3152,128]{1,0:T(8,128)(2,1)} %get-tuple-element.43.refs_0_), channel_id=1, source_target_pairs={{0,14},{2,0},{4,2},{6,4},{8,6},{10,8},{12,10},{14,12},{1,15},{3,1}... | collective-permute-start | bytes 2420744 | tf_op jit(solution)/shard_map/ppermute | solution.py:301
  9.4 3.0 %collective-permute-start.2 = (bf16[1568,128]{1,0:T(8,128)(2,1)}, bf16[1568,128]{1,0:T(8,128)(2,1)}, u32[]{:S(2)}, u32[]{:S(2)}) collective-permute-start(bf16[1568,128]{1,0:T(8,128)(2,1)} %get-tuple-element.29), channel_id=1, source_target_pairs={{0,128},{32,160},{64,192},{96,224},{128,0},{160,32},{192,64},{224,... | collective-permute-start | bytes 1204232 | tf_op jit(solution)/shard_map/ppermute | solution.py:301
  13.9 8.0 %collective-permute-done.2.refs_1_.refs_15_ = bf16[1568,128]{1,0:T(8,128)(2,1)} collective-permute-done((bf16[1568,128]{1,0:T(8,128)(2,1)}, bf16[1568,128]{1,0:T(8,128)(2,1)}, u32[]{:S(2)}, u32[]{:S(2)}) %collective-permute-start.2) | collective-permute-done | bytes 401440 | tf_op jit(solution)/shard_map/ppermute | solution.py:301
  22.0 5.0 %collective-permute-done.1.refs_1_.refs_2_ = bf16[3152,128]{1,0:T(8,128)(2,1)S(1)} collective-permute-done((bf16[3152,128]{1,0:T(8,128)(2,1)}, bf16[3152,128]{1,0:T(8,128)(2,1)S(1)}, u32[]{:S(2)}, u32[]{:S(2)}) %collective-permute-start.1) | collective-permute-done | bytes 806944 | tf_op jit(solution)/shard_map/ppermute | solution.py:301
  26.9 3.3 %collective-permute-done.refs_0_.refs_1_ = bf16[3152,128]{1,0:T(8,128)(2,1)S(1)} collective-permute-done((bf16[3152,128]{1,0:T(8,128)(2,1)}, bf16[3152,128]{1,0:T(8,128)(2,1)S(1)}, u32[]{:S(2)}, u32[]{:S(2)}) %collective-permute-start) | collective-permute-done | bytes 806944 | tf_op jit(solution)/shard_map/ppermute | solution.py:301
  30.3 3.2 %collective-permute-start.4 = (bf16[3152,128]{1,0:T(8,128)(2,1)S(1)}, bf16[3152,128]{1,0:T(8,128)(2,1)S(1)}, u32[]{:S(2)}, u32[]{:S(2)}) collective-permute-start(bf16[3152,128]{1,0:T(8,128)(2,1)S(1)} %collective-permute-done.1.refs_1_.refs_2_), channel_id=1, source_target_pairs={{0,14},{2,0},{4,2},{6,4},{8,6},{10,8},{12,10},{14,12},{1,15},{3,1}... | collective-permute-start | bytes 2420744 | tf_op jit(solution)/shard_map/ppermute | solution.py:301
  35.7 3.3 %lower1.1.refs_4_ = f32[16,512,128]{2,1,0:T(8,128)S(1)} custom-call(s32[4]{0:T(128)S(1)} %pad_add_fusion.place, bf16[3152,128]{1,0:T(8,128)(2,1)S(1)} %copy-done.7, bf16[3136,128]{1,0:T(8,128)(2,1)S(1)} %constant_dynamic-update-slice_fusion.refs_1_.refs_8_), custom_call_target="tpu_custom_call" | custom-call | flops 1000000000 | bytes 2000000 | tf_op jit(solution)/shard_map/lower1/pallas_call | solution.py:226
  39.1 1.9 %copy-done = f32[16,512,128]{2,1,0:T(8,128)} copy-done((f32[16,512,128]{2,1,0:T(8,128)}, f32[16,512,128]{2,1,0:T(8,128)S(1)}, u32[]{:S(2)}) %copy-start) | copy-done | bytes 4194328
  41.1 5.3 %collective-permute-done.5.refs_2_.refs_16_ = bf16[1568,128]{1,0:T(8,128)(2,1)} collective-permute-done((bf16[1568,128]{1,0:T(8,128)(2,1)}, bf16[1568,128]{1,0:T(8,128)(2,1)}, u32[]{:S(2)}, u32[]{:S(2)}) %collective-permute-start.5) | collective-permute-done | bytes 401440 | tf_op jit(solution)/shard_map/ppermute | solution.py:301
  46.4 3.7 %collective-permute-done.3.refs_0_.refs_3_ = bf16[3152,128]{1,0:T(8,128)(2,1)} collective-permute-done((bf16[3152,128]{1,0:T(8,128)(2,1)S(1)}, bf16[3152,128]{1,0:T(8,128)(2,1)}, u32[]{:S(2)}, u32[]{:S(2)}) %collective-permute-start.3) | collective-permute-done | bytes 806944 | tf_op jit(solution)/shard_map/ppermute | solution.py:301
  51.0 3.2 %collective-permute-start.8 = (bf16[3152,128]{1,0:T(8,128)(2,1)}, bf16[3152,128]{1,0:T(8,128)(2,1)S(1)}, u32[]{:S(2)}, u32[]{:S(2)}) collective-permute-start(bf16[3152,128]{1,0:T(8,128)(2,1)} %copy-done.5), channel_id=1, source_target_pairs={{0,14},{2,0},{4,2},{6,4},{8,6},{10,8},{12,10},{14,12},{1,15},{3,1}... | collective-permute-start | bytes 2420744 | tf_op jit(solution)/shard_map/ppermute | solution.py:301
  54.7 2.2 %copy-done.1 = f32[16,512,128]{2,1,0:T(8,128)S(1)} copy-done((f32[16,512,128]{2,1,0:T(8,128)S(1)}, f32[16,512,128]{2,1,0:T(8,128)}, u32[]{:S(2)}) %copy-start.1) | copy-done | bytes 4194328
  58.1 4.1 %lower2.3.refs_4_ = f32[16,512,128]{2,1,0:T(8,128)S(1)} custom-call(s32[4]{0:T(128)S(1)} %pad_add_fusion.place, bf16[3152,128]{1,0:T(8,128)(2,1)S(1)} %copy-done.3, bf16[3152,128]{1,0:T(8,128)(2,1)S(1)} %collective-permute-done.1.refs_1_.refs_2_, bf16[3136,128]{1,0:T(8,128)(2,1)} %collective-permute-done.9.refs_2_.refs_9_, ...), custom_call_target="tpu_custom_call" | custom-call | flops 2000000000 | bytes 4000000 | tf_op jit(solution)/shard_map/lower2/pallas_call | solution.py:226
  62.1 2.1 %collective-permute-done.14.refs_3_.refs_12_ = bf16[3136,128]{1,0:T(8,128)(2,1)} collective-permute-done((bf16[3136,128]{1,0:T(8,128)(2,1)}, bf16[3136,128]{1,0:T(8,128)(2,1)}, u32[]{:S(2)}, u32[]{:S(2)}) %collective-permute-start.14) | collective-permute-done | bytes 802848 | tf_op jit(solution)/shard_map/ppermute | solution.py:301
  64.2 3.3 %collective-permute-start.15 = (bf16[3136,128]{1,0:T(8,128)(2,1)}, bf16[3136,128]{1,0:T(8,128)(2,1)S(1)}, u32[]{:S(2)}, u32[]{:S(2)}) collective-permute-start(bf16[3136,128]{1,0:T(8,128)(2,1)} %collective-permute-done.14.refs_3_.refs_12_), channel_id=1, source_target_pairs={{0,224},{32,0},{64,32},{96,64},{128,96},{160,128},{192,160},{224,1... | collective-permute-start | bytes 2408456 | tf_op jit(solution)/shard_map/ppermute | solution.py:301
  67.5 2.5 %collective-permute-done.7.refs_0_.refs_5_ = bf16[3152,128]{1,0:T(8,128)(2,1)S(1)} collective-permute-done((bf16[3152,128]{1,0:T(8,128)(2,1)}, bf16[3152,128]{1,0:T(8,128)(2,1)S(1)}, u32[]{:S(2)}, u32[]{:S(2)}) %collective-permute-start.7) | collective-permute-done | bytes 806944 | tf_op jit(solution)/shard_map/ppermute | solution.py:301
  70.2 4.1 %lower2.4.refs_4_ = f32[16,512,128]{2,1,0:T(8,128)S(1)} custom-call(s32[4]{0:T(128)S(1)} %pad_add_fusion.place, bf16[3152,128]{1,0:T(8,128)(2,1)} %collective-permute-done.3.refs_0_.refs_3_, bf16[3152,128]{1,0:T(8,128)(2,1)S(1)} %copy-done.6, bf16[3136,128]{1,0:T(8,128)(2,1)} %collective-permute-done.12.refs_2_.refs_11_, ...), custom_call_target="tpu_custom_call" | custom-call | flops 2000000000 | bytes 4000000 | tf_op jit(solution)/shard_map/lower2/pallas_call | solution.py:226
  74.3 3.2 %collective-permute-done.15.refs_3_.refs_14_ = bf16[3136,128]{1,0:T(8,128)(2,1)S(1)} collective-permute-done((bf16[3136,128]{1,0:T(8,128)(2,1)}, bf16[3136,128]{1,0:T(8,128)(2,1)S(1)}, u32[]{:S(2)}, u32[]{:S(2)}) %collective-permute-start.15) | collective-permute-done | bytes 802848 | tf_op jit(solution)/shard_map/ppermute | solution.py:301
  77.5 3.0 %collective-permute-done.13.refs_2_.refs_13_ = bf16[3136,128]{1,0:T(8,128)(2,1)S(1)} collective-permute-done((bf16[3136,128]{1,0:T(8,128)(2,1)}, bf16[3136,128]{1,0:T(8,128)(2,1)S(1)}, u32[]{:S(2)}, u32[]{:S(2)}) %collective-permute-start.13) | collective-permute-done | bytes 802848 | tf_op jit(solution)/shard_map/ppermute | solution.py:301
  80.5 5.0 %lower2.5.refs_3_ = f32[16,512,128]{2,1,0:T(8,128)S(1)} custom-call(s32[4]{0:T(128)S(1)} %pad_add_fusion.place, bf16[3152,128]{1,0:T(8,128)(2,1)S(1)} %collective-permute-done.7.refs_0_.refs_5_, bf16[3152,128]{1,0:T(8,128)(2,1)S(1)} %collective-permute-done.8.refs_1_.refs_6_, bf16[3136,128]{1,0:T(8,128)(2,1)S(1)} %collective-permute-done.13.refs_2_.refs_13_, ...), custom_call_target="tpu_custom_call" | custom-call | flops 2000000000 | bytes 4000000 | tf_op jit(solution)/shard_map/lower2/pallas_call | solution.py:226
  85.6 4.3 %lower1_last.1 = (f32[1024,512]{1,0:T(8,128)}, s16[528,512]{1,0:T(8,128)(2,1)S(1)}, s16[528,512]{1,0:T(8,128)(2,1)S(1)}, s16[528,512]{1,0:T(8,128)(2,1)S(1)}) custom-call(s32[4]{0:T(128)S(1)} %pad_add_fusion.place, bf16[3152,128]{1,0:T(8,128)(2,1)S(1)} %collective-permute-done.11.refs_0_.refs_7_, bf16[1568,128]{1,0:T(8,128)(2,1)} %collective-permute-done.2.refs_1_.refs_15_, ...), custom_call_target="tpu_custom_call" | custom-call | flops 1000000000 | bytes 2000000 | tf_op jit(solution)/shard_map/lower1_last/pallas_call | solution.py:226
  89.9 2.4 %collective-permute-start.19 = (s16[528,512]{1,0:T(8,128)(2,1)S(1)}, s16[528,512]{1,0:T(8,128)(2,1)S(1)}, u32[]{:S(2)}, u32[]{:S(2)}) collective-permute-start(s16[528,512]{1,0:T(8,128)(2,1)S(1)} %get-tuple-element.42), channel_id=1, source_target_pairs={{0,1},{16,17},{1,0},{17,16},{2,3},{18,19},{3,2},{19,18},{4,5},{20,... | collective-permute-start | bytes 1622024 | tf_op jit(solution)/shard_map/ppermute | solution.py:309
  92.2 2.0 %collective-permute-start.21 = (s16[528,512]{1,0:T(8,128)(2,1)S(1)}, s16[528,512]{1,0:T(8,128)(2,1)S(1)}, u32[]{:S(2)}, u32[]{:S(2)}) collective-permute-start(s16[528,512]{1,0:T(8,128)(2,1)S(1)} %get-tuple-element.49), channel_id=1, source_target_pairs={{0,17},{16,0},{1,16},{17,1},{2,19},{18,2},{3,18},{19,3},{4,21},{20... | collective-permute-start | bytes 1622024 | tf_op jit(solution)/shard_map/ppermute | solution.py:309
  94.3 12.1 %upper8_last.1 = (f32[1024,512]{1,0:T(8,128)}, s16[528,512]{1,0:T(8,128)(2,1)S(1)}, s16[528,512]{1,0:T(8,128)(2,1)S(1)}, s16[528,512]{1,0:T(8,128)(2,1)S(1)}) custom-call(s32[4]{0:T(128)S(1)} %pad_add_fusion.place, bf16[3152,128]{1,0:T(8,128)(2,1)S(1)} %copy-done.8, bf16[3152,128]{1,0:T(8,128)(2,1)S(1)} %copy-done.4, ...), custom_call_target="tpu_custom_call", output_to_operand_aliasing={{0}: (18, {})} | custom-call | flops 8000000000 | bytes 16000000 | tf_op jit(solution)/shard_map/upper8_last/pallas_call | solution.py:226
  106.4 1.5 %collective-permute-start.16 = (s16[528,512]{1,0:T(8,128)(2,1)S(1)}, s16[528,512]{1,0:T(8,128)(2,1)S(1)}, u32[]{:S(2)}, u32[]{:S(2)}) collective-permute-start(s16[528,512]{1,0:T(8,128)(2,1)S(1)} %get-tuple-element.45), channel_id=1, source_target_pairs={{0,1},{16,17},{1,0},{17,16},{2,3},{18,19},{3,2},{19,18},{4,5},{20,... | collective-permute-start | bytes 1622024 | tf_op jit(solution)/shard_map/ppermute | solution.py:309
  107.9 2.6 %collective-permute-start.17 = (s16[528,512]{1,0:T(8,128)(2,1)S(1)}, s16[528,512]{1,0:T(8,128)(2,1)S(1)}, u32[]{:S(2)}, u32[]{:S(2)}) collective-permute-start(s16[528,512]{1,0:T(8,128)(2,1)S(1)} %get-tuple-element.46), channel_id=1, source_target_pairs={{0,16},{16,1},{1,17},{17,0},{2,18},{18,3},{3,19},{19,2},{4,20},{20... | collective-permute-start | bytes 1622024 | tf_op jit(solution)/shard_map/ppermute | solution.py:309
  110.5 7.9 %collective-permute-done.20.refs_1_ = s16[528,512]{1,0:T(8,128)(2,1)S(1)} collective-permute-done((s16[528,512]{1,0:T(8,128)(2,1)S(1)}, s16[528,512]{1,0:T(8,128)(2,1)S(1)}, u32[]{:S(2)}, u32[]{:S(2)}) %collective-permute-start.20) | collective-permute-done | bytes 540704 | tf_op jit(solution)/shard_map/ppermute | solution.py:309
  118.9 2.2 %add_up.2.refs_3_ = f32[1024,512]{1,0:T(8,128)} custom-call(s16[528,512]{1,0:T(8,128)(2,1)S(1)} %collective-permute-done.19.refs_0_, s16[528,512]{1,0:T(8,128)(2,1)S(1)} %collective-permute-done.20.refs_1_, s16[528,512]{1,0:T(8,128)(2,1)S(1)} %collective-permute-done.21.refs_2_, f32[1024,512]{1,0:T(8,128)} %get-tuple-element.50.refs_3_), custom_call_target="tpu_custom_call", output_to_operand_aliasing={{}: (3, {})} | custom-call | tf_op jit(solution)/shard_map/add_up/pallas_call | solution.py:283
  121.1 8.8 %collective-permute-done.16.refs_0_ = s16[528,512]{1,0:T(8,128)(2,1)S(1)} collective-permute-done((s16[528,512]{1,0:T(8,128)(2,1)S(1)}, s16[528,512]{1,0:T(8,128)(2,1)S(1)}, u32[]{:S(2)}, u32[]{:S(2)}) %collective-permute-start.16) | collective-permute-done | bytes 540704 | tf_op jit(solution)/shard_map/ppermute | solution.py:309
  129.9 8.6 %collective-permute-done.17.refs_1_ = s16[528,512]{1,0:T(8,128)(2,1)S(1)} collective-permute-done((s16[528,512]{1,0:T(8,128)(2,1)S(1)}, s16[528,512]{1,0:T(8,128)(2,1)S(1)}, u32[]{:S(2)}, u32[]{:S(2)}) %collective-permute-start.17) | collective-permute-done | bytes 540704 | tf_op jit(solution)/shard_map/ppermute | solution.py:309
  138.5 2.2 %add_up.3 = f32[1024,512]{1,0:T(8,128)} custom-call(s16[528,512]{1,0:T(8,128)(2,1)S(1)} %collective-permute-done.16.refs_0_, s16[528,512]{1,0:T(8,128)(2,1)S(1)} %collective-permute-done.17.refs_1_, s16[528,512]{1,0:T(8,128)(2,1)S(1)} %collective-permute-done.18.refs_2_, f32[1024,512]{1,0:T(8,128)} %add_up.2.refs_3_), custom_call_target="tpu_custom_call", output_to_operand_aliasing={{}: (3, {})} | custom-call | tf_op jit(solution)/shard_map/add_up/pallas_call | solution.py:283
  (43 shorter events, 7.2 us)
Async XLA Ops:
  3.5 23.4 %collective-permute-start.1 = (bf16[3152,128]{1,0:T(8,128)(2,1)}, bf16[3152,128]{1,0:T(8,128)(2,1)S(1)}, u32[]{:S(2)}, u32[]{:S(2)}) collective-permute-start(bf16[3152,128]{1,0:T(8,128)(2,1)} %get-tuple-element.43.refs_0_), channel_id=1, source_target_pairs={{0,14},{2,0},{4,2},{6,4},{8,6},{10,8},{12,10},{14,12},{1,15},{3,1}... | collective-permute-start | bytes 2420744 | tf_op jit(solution)/shard_map/ppermute | solution.py:301
  9.4 20.9 %collective-permute-start = (bf16[3152,128]{1,0:T(8,128)(2,1)}, bf16[3152,128]{1,0:T(8,128)(2,1)S(1)}, u32[]{:S(2)}, u32[]{:S(2)}) collective-permute-start(bf16[3152,128]{1,0:T(8,128)(2,1)} %get-tuple-element.43.refs_0_), channel_id=1, source_target_pairs={{0,2},{2,4},{4,6},{6,8},{8,10},{10,12},{12,14},{14,0},{1,3},{3,5},... | collective-permute-start | bytes 2420744 | tf_op jit(solution)/shard_map/ppermute | solution.py:301
  9.4 12.6 %collective-permute-start.2 = (bf16[1568,128]{1,0:T(8,128)(2,1)}, bf16[1568,128]{1,0:T(8,128)(2,1)}, u32[]{:S(2)}, u32[]{:S(2)}) collective-permute-start(bf16[1568,128]{1,0:T(8,128)(2,1)} %get-tuple-element.29), channel_id=1, source_target_pairs={{0,128},{32,160},{64,192},{96,224},{128,0},{160,32},{192,64},{224,... | collective-permute-start | bytes 1204232 | tf_op jit(solution)/shard_map/ppermute | solution.py:301
  12.4 21.1 %collective-permute-start.6 = (bf16[1568,128]{1,0:T(8,128)(2,1)}, bf16[1568,128]{1,0:T(8,128)(2,1)S(1)}, u32[]{:S(2)}, u32[]{:S(2)}) collective-permute-start(bf16[1568,128]{1,0:T(8,128)(2,1)} %get-tuple-element.29), channel_id=1, source_target_pairs={{0,16},{16,0},{1,17},{17,1},{2,18},{18,2},{3,19},{19,3},{4,20},{20... | collective-permute-start | bytes 1204232 | tf_op jit(solution)/shard_map/ppermute | solution.py:301
  30.2 19.8 %copy-start.2 = (bf16[3152,128]{1,0:T(8,128)(2,1)}, bf16[3152,128]{1,0:T(8,128)(2,1)S(1)}, u32[]{:S(2)}) copy-start(bf16[3152,128]{1,0:T(8,128)(2,1)S(1)} %collective-permute-done.refs_0_.refs_1_) | copy-start | bytes 2420740
  30.3 19.8 %collective-permute-start.3 = (bf16[3152,128]{1,0:T(8,128)(2,1)S(1)}, bf16[3152,128]{1,0:T(8,128)(2,1)}, u32[]{:S(2)}, u32[]{:S(2)}) collective-permute-start(bf16[3152,128]{1,0:T(8,128)(2,1)S(1)} %collective-permute-done.refs_0_.refs_1_), channel_id=1, source_target_pairs={{0,2},{2,4},{4,6},{6,8},{8,10},{10,12},{12,14},{14,0},{1,3},{3,5},... | collective-permute-start | bytes 2420744 | tf_op jit(solution)/shard_map/ppermute | solution.py:301
  30.3 19.8 %collective-permute-start.4 = (bf16[3152,128]{1,0:T(8,128)(2,1)S(1)}, bf16[3152,128]{1,0:T(8,128)(2,1)S(1)}, u32[]{:S(2)}, u32[]{:S(2)}) collective-permute-start(bf16[3152,128]{1,0:T(8,128)(2,1)S(1)} %collective-permute-done.1.refs_1_.refs_2_), channel_id=1, source_target_pairs={{0,14},{2,0},{4,2},{6,4},{8,6},{10,8},{12,10},{14,12},{1,15},{3,1}... | collective-permute-start | bytes 2420744 | tf_op jit(solution)/shard_map/ppermute | solution.py:301
  33.5 20.7 %collective-permute-start.10 = (bf16[3136,128]{1,0:T(8,128)(2,1)S(1)}, bf16[3136,128]{1,0:T(8,128)(2,1)}, u32[]{:S(2)}, u32[]{:S(2)}) collective-permute-start(bf16[3136,128]{1,0:T(8,128)(2,1)S(1)} %constant_dynamic-update-slice_fusion.refs_1_.refs_8_), channel_id=1, source_target_pairs={{0,224},{32,0},{64,32},{96,64},{128,96},{160,128},{192,160},{224,1... | collective-permute-start | bytes 2408456 | tf_op jit(solution)/shard_map/ppermute | solution.py:301
  34.0 20.2 %collective-permute-start.9 = (bf16[3136,128]{1,0:T(8,128)(2,1)S(1)}, bf16[3136,128]{1,0:T(8,128)(2,1)}, u32[]{:S(2)}, u32[]{:S(2)}) collective-permute-start(bf16[3136,128]{1,0:T(8,128)(2,1)S(1)} %constant_dynamic-update-slice_fusion.refs_1_.refs_8_), channel_id=1, source_target_pairs={{0,32},{32,64},{64,96},{96,128},{128,160},{160,192},{192,224},{224... | collective-permute-start | bytes 2408456 | tf_op jit(solution)/shard_map/ppermute | solution.py:301
  34.1 12.3 %collective-permute-start.5 = (bf16[1568,128]{1,0:T(8,128)(2,1)}, bf16[1568,128]{1,0:T(8,128)(2,1)}, u32[]{:S(2)}, u32[]{:S(2)}) collective-permute-start(bf16[1568,128]{1,0:T(8,128)(2,1)} %collective-permute-done.2.refs_1_.refs_15_), channel_id=1, source_target_pairs={{0,16},{16,0},{1,17},{17,1},{2,18},{18,2},{3,19},{19,3},{4,20},{20... | collective-permute-start | bytes 1204232 | tf_op jit(solution)/shard_map/ppermute | solution.py:301
  34.6 1.1 copy-start.7
  39.1 2.0 %copy-start = (f32[16,512,128]{2,1,0:T(8,128)}, f32[16,512,128]{2,1,0:T(8,128)S(1)}, u32[]{:S(2)}) copy-start(f32[16,512,128]{2,1,0:T(8,128)S(1)} %lower1.1.refs_4_) | copy-start | bytes 12582916
  50.1 0.9 copy-start.5
  51.0 19.0 %collective-permute-start.7 = (bf16[3152,128]{1,0:T(8,128)(2,1)}, bf16[3152,128]{1,0:T(8,128)(2,1)S(1)}, u32[]{:S(2)}, u32[]{:S(2)}) collective-permute-start(bf16[3152,128]{1,0:T(8,128)(2,1)} %collective-permute-done.3.refs_0_.refs_3_), channel_id=1, source_target_pairs={{0,2},{2,4},{4,6},{6,8},{8,10},{10,12},{12,14},{14,0},{1,3},{3,5},... | collective-permute-start | bytes 2420744 | tf_op jit(solution)/shard_map/ppermute | solution.py:301
  51.0 19.0 %collective-permute-start.8 = (bf16[3152,128]{1,0:T(8,128)(2,1)}, bf16[3152,128]{1,0:T(8,128)(2,1)S(1)}, u32[]{:S(2)}, u32[]{:S(2)}) collective-permute-start(bf16[3152,128]{1,0:T(8,128)(2,1)} %copy-done.5), channel_id=1, source_target_pairs={{0,14},{2,0},{4,2},{6,4},{8,6},{10,8},{12,10},{14,12},{1,15},{3,1}... | collective-permute-start | bytes 2420744 | tf_op jit(solution)/shard_map/ppermute | solution.py:301
  54.2 10.0 %collective-permute-start.14 = (bf16[3136,128]{1,0:T(8,128)(2,1)}, bf16[3136,128]{1,0:T(8,128)(2,1)}, u32[]{:S(2)}, u32[]{:S(2)}) collective-permute-start(bf16[3136,128]{1,0:T(8,128)(2,1)} %collective-permute-done.10.refs_3_.refs_10_), channel_id=1, source_target_pairs={{0,224},{32,0},{64,32},{96,64},{128,96},{160,128},{192,160},{224,1... | collective-permute-start | bytes 2408456 | tf_op jit(solution)/shard_map/ppermute | solution.py:301
  54.2 13.3 %collective-permute-start.12 = (bf16[3136,128]{1,0:T(8,128)(2,1)}, bf16[3136,128]{1,0:T(8,128)(2,1)}, u32[]{:S(2)}, u32[]{:S(2)}) collective-permute-start(bf16[3136,128]{1,0:T(8,128)(2,1)} %collective-permute-done.9.refs_2_.refs_9_), channel_id=1, source_target_pairs={{0,32},{32,64},{64,96},{96,128},{128,160},{160,192},{192,224},{224... | collective-permute-start | bytes 2408456 | tf_op jit(solution)/shard_map/ppermute | solution.py:301
  54.7 2.2 %copy-start.1 = (f32[16,512,128]{2,1,0:T(8,128)S(1)}, f32[16,512,128]{2,1,0:T(8,128)}, u32[]{:S(2)}) copy-start(f32[16,512,128]{2,1,0:T(8,128)} %copy-done) | copy-start | bytes 12582916
  56.9 1.1 copy-start.3
  58.1 12.1 %copy-start.6 = (bf16[3152,128]{1,0:T(8,128)(2,1)S(1)}, bf16[3152,128]{1,0:T(8,128)(2,1)}, u32[]{:S(2)}) copy-start(bf16[3152,128]{1,0:T(8,128)(2,1)} %copy-done.5) | copy-start | bytes 2420740
  64.2 13.3 %collective-permute-start.15 = (bf16[3136,128]{1,0:T(8,128)(2,1)}, bf16[3136,128]{1,0:T(8,128)(2,1)S(1)}, u32[]{:S(2)}, u32[]{:S(2)}) collective-permute-start(bf16[3136,128]{1,0:T(8,128)(2,1)} %collective-permute-done.14.refs_3_.refs_12_), channel_id=1, source_target_pairs={{0,224},{32,0},{64,32},{96,64},{128,96},{160,128},{192,160},{224,1... | collective-permute-start | bytes 2408456 | tf_op jit(solution)/shard_map/ppermute | solution.py:301
  67.5 13.0 %collective-permute-start.13 = (bf16[3136,128]{1,0:T(8,128)(2,1)}, bf16[3136,128]{1,0:T(8,128)(2,1)S(1)}, u32[]{:S(2)}, u32[]{:S(2)}) collective-permute-start(bf16[3136,128]{1,0:T(8,128)(2,1)} %collective-permute-done.12.refs_2_.refs_11_), channel_id=1, source_target_pairs={{0,32},{32,64},{64,96},{96,128},{128,160},{160,192},{192,224},{224... | collective-permute-start | bytes 2408456 | tf_op jit(solution)/shard_map/ppermute | solution.py:301
  70.1 15.5 %collective-permute-start.11 = (bf16[3152,128]{1,0:T(8,128)(2,1)S(1)}, bf16[3152,128]{1,0:T(8,128)(2,1)S(1)}, u32[]{:S(2)}, u32[]{:S(2)}) collective-permute-start(bf16[3152,128]{1,0:T(8,128)(2,1)S(1)} %broadcast_select_fusion), channel_id=1, source_target_pairs={{0,2},{2,4},{4,6},{6,8},{8,10},{10,12},{12,14},{14,0},{32,46},{34,... | collective-permute-start | bytes 2420744 | tf_op jit(solution)/shard_map/ppermute | solution.py:342
  85.6 8.7 %copy-start.4 = (bf16[3152,128]{1,0:T(8,128)(2,1)S(1)}, bf16[3152,128]{1,0:T(8,128)(2,1)}, u32[]{:S(2)}) copy-start(bf16[3152,128]{1,0:T(8,128)(2,1)} %copy-done.2) | copy-start | bytes 2420740
  85.6 8.7 %copy-start.8 = (bf16[3152,128]{1,0:T(8,128)(2,1)S(1)}, bf16[3152,128]{1,0:T(8,128)(2,1)}, u32[]{:S(2)}) copy-start(bf16[3152,128]{1,0:T(8,128)(2,1)} %get-tuple-element.43.refs_0_) | copy-start | bytes 2420740
  89.9 29.1 %collective-permute-start.19 = (s16[528,512]{1,0:T(8,128)(2,1)S(1)}, s16[528,512]{1,0:T(8,128)(2,1)S(1)}, u32[]{:S(2)}, u32[]{:S(2)}) collective-permute-start(s16[528,512]{1,0:T(8,128)(2,1)S(1)} %get-tuple-element.42), channel_id=1, source_target_pairs={{0,1},{16,17},{1,0},{17,16},{2,3},{18,19},{3,2},{19,18},{4,5},{20,... | collective-permute-start | bytes 1622024 | tf_op jit(solution)/shard_map/ppermute | solution.py:309
  92.2 26.1 %collective-permute-start.20 = (s16[528,512]{1,0:T(8,128)(2,1)S(1)}, s16[528,512]{1,0:T(8,128)(2,1)S(1)}, u32[]{:S(2)}, u32[]{:S(2)}) collective-permute-start(s16[528,512]{1,0:T(8,128)(2,1)S(1)} %get-tuple-element.48), channel_id=1, source_target_pairs={{0,16},{16,1},{1,17},{17,0},{2,18},{18,3},{3,19},{19,2},{4,20},{20... | collective-permute-start | bytes 1622024 | tf_op jit(solution)/shard_map/ppermute | solution.py:309
  92.2 26.7 %collective-permute-start.21 = (s16[528,512]{1,0:T(8,128)(2,1)S(1)}, s16[528,512]{1,0:T(8,128)(2,1)S(1)}, u32[]{:S(2)}, u32[]{:S(2)}) collective-permute-start(s16[528,512]{1,0:T(8,128)(2,1)S(1)} %get-tuple-element.49), channel_id=1, source_target_pairs={{0,17},{16,0},{1,16},{17,1},{2,19},{18,2},{3,18},{19,3},{4,21},{20... | collective-permute-start | bytes 1622024 | tf_op jit(solution)/shard_map/ppermute | solution.py:309
  106.4 23.5 %collective-permute-start.16 = (s16[528,512]{1,0:T(8,128)(2,1)S(1)}, s16[528,512]{1,0:T(8,128)(2,1)S(1)}, u32[]{:S(2)}, u32[]{:S(2)}) collective-permute-start(s16[528,512]{1,0:T(8,128)(2,1)S(1)} %get-tuple-element.45), channel_id=1, source_target_pairs={{0,1},{16,17},{1,0},{17,16},{2,3},{18,19},{3,2},{19,18},{4,5},{20,... | collective-permute-start | bytes 1622024 | tf_op jit(solution)/shard_map/ppermute | solution.py:309
  107.9 30.7 %collective-permute-start.17 = (s16[528,512]{1,0:T(8,128)(2,1)S(1)}, s16[528,512]{1,0:T(8,128)(2,1)S(1)}, u32[]{:S(2)}, u32[]{:S(2)}) collective-permute-start(s16[528,512]{1,0:T(8,128)(2,1)S(1)} %get-tuple-element.46), channel_id=1, source_target_pairs={{0,16},{16,1},{1,17},{17,0},{2,18},{18,3},{3,19},{19,2},{4,20},{20... | collective-permute-start | bytes 1622024 | tf_op jit(solution)/shard_map/ppermute | solution.py:309
  118.4 20.2 %collective-permute-start.18 = (s16[528,512]{1,0:T(8,128)(2,1)S(1)}, s16[528,512]{1,0:T(8,128)(2,1)S(1)}, u32[]{:S(2)}, u32[]{:S(2)}) collective-permute-start(s16[528,512]{1,0:T(8,128)(2,1)S(1)} %get-tuple-element.47), channel_id=1, source_target_pairs={{0,17},{16,0},{1,16},{17,1},{2,19},{18,2},{3,18},{19,3},{4,21},{20... | collective-permute-start | bytes 1622024 | tf_op jit(solution)/shard_map/ppermute | solution.py:309
